TPU v7x, 128 devices: a whole 4x4x4 slice. The times are simulated.
128 devices in a mesh: corpus: 16 (over z, x_lo, core), group: 8 (over x_hi, y).
Axes of the slice: x: 4 (x_hi: 2, x_lo: 2; x = x_hi * 2 + x_lo), y: 4, z: 4, core: 2. Of those that a mesh axis runs over, the one named last changes fastest.
Arguments:
- queries: bfloat16 [1024, 32768], P('corpus', 'group'), may hold values from -6 to 6
- precond: bfloat16 [8, 4096, 4096], P('group', 'corpus'), may hold values from -0.09375 to 0.09375
- documents: bfloat16 [24576, 32768], P('corpus', 'group'), may hold values from -6 to 6
Outputs:
- scores: float32 [1024, 24576], P('group', 'corpus')
All inputs are finite; a program needn't handle non-finite values.
Results may differ from a plain program's by a relative error of at most 0.0029.
Values may be sent and summed in bfloat16 or wider, within the bound.
No kernel may reach another device: no remote copies, remote signals or barrier semaphores. Data moves between devices by JAX's collectives and lax.ppermute only.
A program may use at most 128 MiB of HBM per device.

v0:
```python
import jax
import jax.numpy as jnp
from jax import lax
from jax.sharding import PartitionSpec as P


def doc_scores(rows, documents):
    return lax.dot_general(
        rows, documents, (((1,), (1,)), ((), ())), preferred_element_type=jnp.float32
    )


def local(queries, precond, documents):
    feat = queries.shape[1]
    n_group = lax.axis_size("group")
    summed = jnp.dot(
        queries,
        lax.all_gather(precond, "corpus", axis=1, tiled=True)[0],
        preferred_element_type=jnp.float32,
    )
    conditioned = summed.astype(jnp.bfloat16)
    block = doc_scores(lax.all_gather(conditioned, "corpus", axis=0, tiled=True), documents)
    summed_scores = lax.psum_scatter(block, "group", scatter_dimension=0, tiled=True)
    return summed_scores / jnp.sqrt(jnp.float32(n_group * feat))


def solution(mesh):
    placed = (P("corpus", "group"), P("group", "corpus", None), P("corpus", "group"))
    return jax.shard_map(
        local, mesh=mesh, in_specs=placed, out_specs=P("group", "corpus"), check_vma=False
    )
```

profile of v0, /device:TPU:0, one launch (start us, length us, event | category | flops | bytes accessed | tf_op | source)
XLA Modules:
  0.0 377.6 jit_solution(5938842677587874399)
XLA Ops:
  6.5 0.0 copy-start
  6.5 0.0 all-gather.3.cloned.1.call-start
  6.5 0.7 all-gather.3.cloned.1.call-update
  7.3 0.0 all-gather.5.cloned.1.call-start
  7.3 174.9 %all-gather.3.cloned.1.call-done = bf16[1,4096,4096]{2,1,0:T(8,128)(2,1)} async-done(((bf16[1,256,4096]{2,1,0:T(8,128)(2,1)}), bf16[1,4096,4096]{2,1,0:T(8,128)(2,1)}) %all-gather.3.cloned.1.call-update) | async-done | bytes 33554448 | tf_op jit(solution)/shard_map/all_gather | solution.py:18
  182.2 0.0 copy-done
  182.2 14.4 %fusion.2 = bf16[64,4096]{1,0:T(8,128)(2,1)} fusion(bf16[64,4096]{1,0:T(8,128)(2,1)S(1)} %copy-done, bf16[1,4096,4096]{2,1,0:T(8,128)(2,1)} %all-gather.3.cloned.1.call-done), kind=kOutput, calls=%fused_computation.2 | convolution fusion | flops 2147745792 | bytes 34603008 | tf_op jit(solution)/shard_map/dot_general | solution.py:16
  196.6 0.0 all-gather.5.cloned.1.call-update
  196.6 0.0 reduce-scatter.2.cloned.1.call-start
  196.7 53.2 %all-gather.5.cloned.1.call-done = bf16[1024,4096]{1,0:T(8,128)(2,1)} async-done(((bf16[64,4096]{1,0:T(8,128)(2,1)}), bf16[1024,4096]{1,0:T(8,128)(2,1)}) %all-gather.5.cloned.1.call-update) | async-done | bytes 8388624 | tf_op jit(solution)/shard_map/all_gather | solution.py:22
  249.9 19.7 %fusion.5 = f32[1024,1536]{1,0:T(8,128)} fusion(bf16[1024,4096]{1,0:T(8,128)(2,1)} %all-gather.5.cloned.1.call-done, bf16[1536,4096]{1,0:T(8,128)(2,1)} %param.5), kind=kOutput, calls=%fused_computation.4 | convolution fusion | flops 12884901888 | bytes 27262976 | tf_op jit(solution)/shard_map/dot_general | solution.py:8
  269.6 0.0 reduce-scatter.2.cloned.1.call-update
  269.7 99.3 %reduce-scatter.2.cloned.1.call-done = f32[128,1536]{1,0:T(8,128)} async-done(((f32[1024,1536]{1,0:T(8,128)}), f32[128,1536]{1,0:T(8,128)}) %reduce-scatter.2.cloned.1.call-update) | async-done | bytes 786448 | tf_op jit(solution)/shard_map/reduce_scatter | solution.py:23
  369.0 2.1 broadcast_multiply_fusion
Async XLA Ops:
  6.5 175.7 %copy-start = (bf16[64,4096]{1,0:T(8,128)(2,1)S(1)}, bf16[64,4096]{1,0:T(8,128)(2,1)}, u32[]{:S(2)}) copy-start(bf16[64,4096]{1,0:T(8,128)(2,1)} %param.3) | copy-start | bytes 1572868
  6.5 175.7 %all-gather.3.cloned.1.call-start = ((), (), s32[]{:S(2)}) async-start(), calls=%async_computation.1 | async-start | bytes 35651584 | tf_op jit(solution)/shard_map/all_gather | solution.py:18
  7.3 242.7 %all-gather.5.cloned.1.call-start = ((), (), s32[]{:S(2)}) async-start(), calls=%async_computation.2 | async-start | bytes 8912896 | tf_op jit(solution)/shard_map/all_gather | solution.py:22
  196.6 172.4 %reduce-scatter.2.cloned.1.call-start = ((), (), s32[]{:S(2)}) async-start(), calls=%async_computation.3 | async-start | bytes 7077888 | tf_op jit(solution)/shard_map/reduce_scatter | solution.py:23
Sparse Core Ops, SparseCore 0:
  9.1 173.0 all-gather.2
  196.8 53.1 all-gather.4
  269.8 99.1 reduce-scatter.1
where the time goes:
time: 378 us
  waiting for transfers between devices  328 us (87%)
  matrix products  34.1 us (9%)
  between operations  13.1 us (3%)
    all_gather x1, waiting for transfers between devices, local(): lax.all_gather(precond, 'corpus', axis=1, tiled=True)[0]  175 us
    reduce_scatter x1, waiting for transfers between devices, local(): lax.psum_scatter(block, 'group', scatter_dimension=0, tiled=True)  99.3 us
    all_gather x1, waiting for transfers between devices, local(): lax.all_gather(conditioned, 'corpus', axis=0, tiled=True)  53.2 us
    dot_general x1, matrix products, doc_scores(): lax.dot_general(rows, documents, (((1,), (1,)), ((), ())), preferred_elem...  19.7 us
    dot_general x1, matrix products, local(): jnp.dot(queries, lax.all_gather(precond, 'corpus', axis=1, tiled=True)[0]...  14.4 us
  transfers between devices with their start and end apart: 3, of which 3 were waited for; matrix products, arithmetic and copies ran while one was open for 0% of the time, Pallas kernels for 0%

commit v1 on v0

v1 whole, which is shorter than its diff:
```python
import functools

import jax
import jax.numpy as jnp
from jax import lax
from jax.experimental import pallas as pl
from jax.experimental.pallas import tpu as pltpu
from jax.sharding import PartitionSpec as P

NZ, NX, NC, NH, NY = 4, 2, 2, 2, 4
CHIPS = NZ * NX
GROUP = NH * NY
ROLES = ((0, 0), (-1, 0), (1, 0), (2, 0), (0, 1), (-1, 1), (1, 1), (2, 1))


def corpus_perm(move):
    pairs = []
    for z in range(NZ):
        for x in range(NX):
            for c in range(NC):
                dz, dx, dc = move(1 - 2 * c)
                to = ((z + dz) % NZ, (x + dx) % NX, (c + dc) % NC)
                pairs.append(((z * NX + x) * NC + c, (to[0] * NX + to[1]) * NC + to[2]))
    return pairs


def group_perm(dh, dy):
    return [(h * NY + y, (h + dh) % NH * NY + (y + dy) % NY) for h in range(NH) for y in range(NY)]


AHEAD = corpus_perm(lambda d: (d, 0, 0))
BACK = corpus_perm(lambda d: (-d, 0, 0))
CROSS = corpus_perm(lambda d: (0, 1, 0))
CORE = corpus_perm(lambda d: (0, 0, 1))
SAME_CORE = [[chip * NC + c for chip in range(CHIPS)] for c in range(NC)]


def gather_pieces(own):
    go = functools.partial(lax.ppermute, axis_name="corpus")
    cross = go(own, perm=CROSS)
    behind = go(own, perm=AHEAD)
    ahead = go(own, perm=BACK)
    cross_behind = go(cross, perm=AHEAD)
    far = go(behind, perm=AHEAD)
    cross_ahead = go(ahead, perm=CROSS)
    cross_far = go(cross_behind, perm=AHEAD)
    return [own, behind, ahead, far, cross, cross_behind, cross_ahead, cross_far]


def chip_of(direction):
    place = lax.axis_index("corpus")
    z, x = place // (NX * NC), place // NC % NX
    return [((z + dz * direction + NZ) % NZ) * NX + (x + dx) % NX for dz, dx in ROLES]


def condition_kernel(place, *refs):
    pieces, weights, own, other, rows = refs[:CHIPS], *refs[CHIPS:]
    half = pieces[0].shape[0] // 2
    total = own.shape[0]
    for i, piece in enumerate(pieces):
        start = pl.multiple_of(place[i] * half, half)
        rows[pl.ds(start, half), :] = piece[:half, :]
        rows[pl.ds(total + start, half), :] = piece[half:, :]
    step = min(256, total)

    @pl.loop(0, total // step)
    def _(i):
        at = pl.ds(pl.multiple_of(i * step, step), step)
        own[at, :] = jnp.dot(rows[at, :], weights[...], preferred_element_type=jnp.float32)

    @pl.loop(0, total // step)
    def _(i):
        at = pl.ds(pl.multiple_of(i * step, step), step)
        off = pl.ds(pl.multiple_of(total + i * step, step), step)
        other[at, :] = jnp.dot(rows[off, :], weights[...], preferred_element_type=jnp.float32)


def condition(place, pieces, weights):
    rows, depth = pieces[0].shape
    wide = weights.shape[1]
    total = rows // 2 * CHIPS
    whole = pl.BlockSpec(memory_space=pltpu.VMEM)
    return pl.pallas_call(
        condition_kernel,
        out_shape=[jax.ShapeDtypeStruct((total, wide), jnp.float32)] * 2,
        in_specs=[pl.BlockSpec(memory_space=pltpu.SMEM)] + [whole] * (CHIPS + 1),
        out_specs=[whole] * 2,
        scratch_shapes=[pltpu.VMEM((2 * total, depth), jnp.bfloat16)],
        compiler_params=pltpu.CompilerParams(vmem_limit_bytes=32 * 2**20),
        cost_estimate=pl.CostEstimate(flops=4 * total * depth * wide, bytes_accessed=2**23, transcendentals=0),
    )(place, *pieces, weights)


def score_kernel(chips, *refs):
    pieces, docs = refs[:CHIPS], refs[CHIPS]
    outs, (acc, piece) = refs[CHIPS + 1 : -2], refs[-2:]
    k = pl.program_id(0)
    for i, ref in enumerate(pieces):

        @pl.when(k == i)
        def _():
            piece[...] = ref[...]

    step = 256
    steps = docs.shape[0] // step

    def add(first):
        @pl.loop(0, steps)
        def _(i):
            at = pl.ds(pl.multiple_of(i * step, step), step)
            part = lax.dot_general(
                piece[...], docs[at, :], (((1,), (1,)), ((), ())), preferred_element_type=jnp.float32
            )
            acc[:, at] = part if first else acc[:, at] + part

    @pl.when(k == 0)
    def _():
        add(True)

    @pl.when(k > 0)
    def _():
        add(False)

    @pl.when(k == CHIPS - 1)
    def _():
        tall = outs[0].shape[0]
        for i, out in enumerate(outs):
            out[...] = acc[i * tall : (i + 1) * tall, :].astype(out.dtype)


def score(chips, pieces, docs):
    rows, wide = pieces[0].shape
    n_docs = docs.shape[0]
    tall = rows // NY
    whole = pl.BlockSpec(pieces[0].shape, lambda k, chips: (0, 0))
    out = pl.BlockSpec((tall, n_docs), lambda k, chips: (0, 0))
    return pl.pallas_call(
        score_kernel,
        out_shape=[
            jax.ShapeDtypeStruct((tall, n_docs), jnp.bfloat16 if i else jnp.float32) for i in range(NY)
        ],
        grid_spec=pltpu.PrefetchScalarGridSpec(
            num_scalar_prefetch=1,
            grid=(CHIPS,),
            in_specs=[whole] * CHIPS + [pl.BlockSpec((n_docs, wide), lambda k, chips: (0, chips[k]))],
            out_specs=[out] * NY,
            scratch_shapes=[
                pltpu.VMEM((rows, n_docs), jnp.float32),
                pltpu.VMEM((rows, wide), jnp.bfloat16),
            ],
        ),
        compiler_params=pltpu.CompilerParams(
            dimension_semantics=("arbitrary",), vmem_limit_bytes=40 * 2**20
        ),
        cost_estimate=pl.CostEstimate(
            flops=2 * rows * n_docs * wide * CHIPS, bytes_accessed=n_docs * wide * CHIPS * 2, transcendentals=0
        ),
    )(chips, *pieces, docs)


def reduce_scores(parts):
    own, ahead, far, back = parts
    go = functools.partial(lax.ppermute, axis_name="group")
    got = [go(ahead, perm=group_perm(0, 1)), go(back, perm=group_perm(0, -1)), go(far, perm=group_perm(0, 2))]
    total = own
    for part in got:
        total = total + part.astype(jnp.float32)
    half = total.shape[0] // NH
    sent = go(total[half:].astype(jnp.bfloat16), perm=group_perm(1, 0))
    return total[:half] + sent.astype(jnp.float32)


def local(queries, precond, documents):
    rows, feat = queries.shape
    core = lax.axis_index("corpus") % NC
    direction = 1 - 2 * core
    h, y = lax.axis_index("group") // NY, lax.axis_index("group") % NY

    split = queries.reshape(rows, CHIPS, NC, feat // (CHIPS * NC))
    mine, theirs = [
        lax.dynamic_index_in_dim(split, i, 2, keepdims=False).reshape(rows, feat // NC)
        for i in (core, 1 - core)
    ]
    query_piece = jnp.concatenate([mine, lax.ppermute(theirs, "corpus", CORE)], axis=0)
    query_pieces = gather_pieces(query_piece)
    weights = lax.all_to_all(precond[0], "corpus", 1, 0, tiled=True, axis_index_groups=SAME_CORE)

    chips = jnp.stack(chip_of(direction))
    chips_other = jnp.stack(chip_of(-direction))
    place = (chips % NY - y + NY) % NY * NH + (chips // NY - h + NH) % NH
    own, other = condition(place, query_pieces, weights)
    conditioned = (own + lax.ppermute(other, "corpus", CORE)).astype(jnp.bfloat16)

    pieces = gather_pieces(conditioned)
    pieces_other = [lax.ppermute(piece, "corpus", CORE) for piece in pieces]
    mine = reduce_scores(score(chips, pieces, documents))
    theirs = reduce_scores(score(chips_other, pieces_other, documents))
    first = core == 0
    scores = jnp.concatenate([jnp.where(first, mine, theirs), jnp.where(first, theirs, mine)], axis=0)
    return scores / jnp.sqrt(jnp.float32(GROUP * feat))


def solution(mesh):
    placed = (P("corpus", "group"), P("group", "corpus", None), P("corpus", "group"))
    return jax.shard_map(
        local, mesh=mesh, in_specs=placed, out_specs=P("group", "corpus"), check_vma=False
    )
```

time: 378 us -> 192 us (0.51)
  waiting for transfers between devices: 328 us -> 103 us
  Pallas kernels: 0 us -> 43.7 us
  starting transfers between devices: 0.08 us -> 35 us
  matrix products: 34.1 us -> 0 us
  between operations: 13.1 us -> 0.23 us
  local copies, waits for them, and re-layouts: 0.01 us -> 7.97 us
    all_gather x2 -> x0, waiting for transfers between devices: 228 us -> none  [the longest x1 175 us: local(): lax.all_gather(precond, 'corpus', axis=1, tiled=True)[0]]
    ppermute x0 -> x32, waiting for transfers between devices: none -> 103 us  [the longest x2 42.9 us: gather_pieces(): cross = go(own, perm=CROSS)]
    reduce_scatter x1 -> x0, waiting for transfers between devices: 99.3 us -> none  [local(): lax.psum_scatter(block, 'group', scatter_dimension=0, tiled=True)]
    pallas_call x0 -> x3, Pallas kernels: none -> 43.7 us  [the longest x2 38.7 us: score(): pl.pallas_call(score_kernel, out_shape=[jax.ShapeDtypeStruct((tall, n_doc...]
    dot_general x2 -> x0, matrix products: 34.1 us -> none  [the longest x1 19.7 us: doc_scores(): lax.dot_general(rows, documents, (((1,), (1,)), ((), ())), preferred_elem...]
    ppermute x0 -> x32, starting transfers between devices: none -> 28.7 us  [the longest x2 5.59 us: reduce_scores(): sent = go(total[half:].astype(jnp.bfloat16), perm=group_perm(1, 0))]
    all_to_all x0 -> x1, starting transfers between devices: none -> 6.32 us  [local(): lax.all_to_all(precond[0], 'corpus', 1, 0, tiled=True, axis_index_groups=...]
  transfers between devices with their start and end apart: 3 -> 33, of which waited for: 3 -> 15; matrix products, arithmetic and copies ran while one was open for 0% -> 2% of each run, Pallas kernels for 0% -> 20%
where the time goes in v1:
time: 192 us
  waiting for transfers between devices  103 us (54%)
  Pallas kernels  43.7 us (23%)
  starting transfers between devices  35 us (18%)
  local copies, waits for them, and re-layouts  7.97 us (4%)
    ppermute x2, waiting for transfers between devices, gather_pieces(): cross = go(own, perm=CROSS)  42.9 us
    pallas_call x2, Pallas kernels, score(): pl.pallas_call(score_kernel, out_shape=[jax.ShapeDtypeStruct((tall, n_doc...  38.7 us
    ppermute x2, waiting for transfers between devices, gather_pieces(): cross_behind = go(cross, perm=AHEAD)  14.5 us
    ppermute x2, waiting for transfers between devices, gather_pieces(): far = go(behind, perm=AHEAD)  11.1 us
    ppermute x2, waiting for transfers between devices, gather_pieces(): cross_far = go(cross_behind, perm=AHEAD)  10.1 us
    ppermute x2, waiting for transfers between devices, reduce_scores(): go(far, perm=group_perm(0, 2))  7.23 us
    ppermute x2, waiting for transfers between devices, reduce_scores(): go(back, perm=group_perm(0, -1))  6.68 us
    all_to_all x1, starting transfers between devices, local(): lax.all_to_all(precond[0], 'corpus', 1, 0, tiled=True, axis_index_groups=...  6.32 us
  transfers between devices with their start and end apart: 33, of which 15 were waited for; matrix products, arithmetic and copies ran while one was open for 2% of the time, Pallas kernels for 20%

profile of v1, /device:TPU:0, one launch (start us, length us, event | category | flops | bytes accessed | tf_op | source)
XLA Modules:
  0.0 191.8 jit_solution(298083782296604005)
XLA Ops:
  0.0 1.6 reshape.15
  1.6 3.1 %dynamic-slice_reduce_fusion = (bf16[64,8,256]{2,1,0:T(8,128)(2,1)S(1)}, bf16[64,8,256]{2,1,0:T(8,128)(2,1)S(1)}) fusion(bf16[64,8,2,256]{3,2,1,0:T(2,128)(2,1)S(1)} %reshape.15, s32[]{:T(128)S(6)} %select_n.167, s32[]{:T(128)S(6)} %select_n.166), kind=kLoop, calls=%fused_computation.4 | loop fusion | bytes 1048584 | tf_op jit(solution)/shard_map/jit(dynamic_index_in_dim)/dynamic_slice | solution.py:181
  5.8 2.0 %copy.6 = bf16[256,8,512]{2,0,1:T(8,128)(2,1)} copy(bf16[256,8,512]{2,1,0:T(8,128)(2,1)S(1)} %bitcast.25) | data formatting | bytes 4194304 | tf_op jit(solution)/shard_map/all_to_all | solution.py:186
  7.8 6.3 %all-to-all-start = ((bf16[256,8,512]{2,0,1:T(8,128)(2,1)}), bf16[256,8,512]{2,0,1:T(8,128)(2,1)S(1)}, u32[]{:S(2)}, u32[]{:S(2)}) async-start(bf16[256,8,512]{2,0,1:T(8,128)(2,1)} %copy.6), calls=%async_computation | async-start | bytes 4194304 | tf_op jit(solution)/shard_map/all_to_all | solution.py:186
  14.2 2.1 %collective-permute-start.4 = (bf16[128,2048]{1,0:T(8,128)(2,1)S(1)}, bf16[128,2048]{1,0:T(8,128)(2,1)S(1)}, u32[]{:S(2)}, u32[]{:S(2)}) collective-permute-start(bf16[128,2048]{1,0:T(8,128)(2,1)S(1)} %constant_dynamic-update-slice_fusion.refs_0_), channel_id=1, source_target_pairs={{0,16},{8,24},{16,0},{24,8},{32,48},{40,56},{48,32},{56,40},{64,80... | collective-permute-start | bytes 1572872 | tf_op jit(solution)/shard_map/ppermute | solution.py:40
  16.3 1.5 collective-permute-start.1
  17.8 1.8 collective-permute-start.2
  19.6 32.3 %collective-permute-done.4.refs_4_ = bf16[128,2048]{1,0:T(8,128)(2,1)S(1)} collective-permute-done((bf16[128,2048]{1,0:T(8,128)(2,1)S(1)}, bf16[128,2048]{1,0:T(8,128)(2,1)S(1)}, u32[]{:S(2)}, u32[]{:S(2)}) %collective-permute-start.4) | collective-permute-done | bytes 524320 | tf_op jit(solution)/shard_map/ppermute | solution.py:40
  52.4 2.2 %collective-permute-start.3 = (bf16[128,2048]{1,0:T(8,128)(2,1)}, bf16[128,2048]{1,0:T(8,128)(2,1)}, u32[]{:S(2)}, u32[]{:S(2)}) collective-permute-start(bf16[128,2048]{1,0:T(8,128)(2,1)} %collective-permute-done.1.refs_1_), channel_id=1, source_target_pairs={{0,32},{8,104},{16,48},{24,120},{32,64},{40,8},{48,80},{56,24},{64... | collective-permute-start | bytes 1572872 | tf_op jit(solution)/shard_map/ppermute | solution.py:44
  54.5 7.9 %collective-permute-done.5.refs_5_ = bf16[128,2048]{1,0:T(8,128)(2,1)} collective-permute-done((bf16[128,2048]{1,0:T(8,128)(2,1)S(1)}, bf16[128,2048]{1,0:T(8,128)(2,1)}, u32[]{:S(2)}, u32[]{:S(2)}) %collective-permute-start.5) | collective-permute-done | bytes 524320 | tf_op jit(solution)/shard_map/ppermute | solution.py:43
  62.5 5.5 %collective-permute-done.3.refs_3_ = bf16[128,2048]{1,0:T(8,128)(2,1)} collective-permute-done((bf16[128,2048]{1,0:T(8,128)(2,1)}, bf16[128,2048]{1,0:T(8,128)(2,1)}, u32[]{:S(2)}, u32[]{:S(2)}) %collective-permute-start.3) | collective-permute-done | bytes 524320 | tf_op jit(solution)/shard_map/ppermute | solution.py:44
  68.1 5.5 %collective-permute-done.7.refs_7_ = bf16[128,2048]{1,0:T(8,128)(2,1)} collective-permute-done((bf16[128,2048]{1,0:T(8,128)(2,1)}, bf16[128,2048]{1,0:T(8,128)(2,1)}, u32[]{:S(2)}, u32[]{:S(2)}) %collective-permute-start.7) | collective-permute-done | bytes 524320 | tf_op jit(solution)/shard_map/ppermute | solution.py:46
  73.6 4.9 %shard_map.37 = (f32[512,512]{1,0:T(8,128)S(1)}, f32[512,512]{1,0:T(8,128)S(1)}) custom-call(s32[8]{0:T(128)S(1)} %fusion.2.place, bf16[128,2048]{1,0:T(8,128)(2,1)S(1)} %constant_dynamic-update-slice_fusion.refs_0_, bf16[128,2048]{1,0:T(8,128)(2,1)} %collective-permute-done.1.refs_1_, bf16[128,2048]{1,0:T(8,128)(2,1)} %collective-permute-done.2.refs_2_, ...), custom_call_target="tpu_custom_call" | custom-call | flops 2147483648 | bytes 8388608 | tf_op jit(solution)/shard_map/pallas_call | solution.py:83
  78.7 2.6 %collective-permute-done.8 = f32[512,512]{1,0:T(8,128)S(1)} collective-permute-done((f32[512,512]{1,0:T(8,128)S(1)}, f32[512,512]{1,0:T(8,128)S(1)}, u32[]{:S(2)}, u32[]{:S(2)}) %collective-permute-start.8) | collective-permute-done | bytes 1048608 | tf_op jit(solution)/shard_map/ppermute | solution.py:192
  81.7 3.2 %collective-permute-start.10 = (bf16[512,512]{1,0:T(8,128)(2,1)S(1)}, bf16[512,512]{1,0:T(8,128)(2,1)}, u32[]{:S(2)}, u32[]{:S(2)}) collective-permute-start(bf16[512,512]{1,0:T(8,128)(2,1)S(1)} %add_convert_fusion.refs_0_), channel_id=1, source_target_pairs={{0,96},{8,40},{16,112},{24,56},{32,0},{40,72},{48,16},{56,88},{64,... | collective-permute-start | bytes 1572872 | tf_op jit(solution)/shard_map/ppermute | solution.py:42
  85.0 10.6 %collective-permute-done.12.refs_4_ = bf16[512,512]{1,0:T(8,128)(2,1)S(1)} collective-permute-done((bf16[512,512]{1,0:T(8,128)(2,1)S(1)}, bf16[512,512]{1,0:T(8,128)(2,1)S(1)}, u32[]{:S(2)}, u32[]{:S(2)}) %collective-permute-start.12) | collective-permute-done | bytes 524320 | tf_op jit(solution)/shard_map/ppermute | solution.py:40
  95.6 1.9 collective-permute-done.9.refs_1_
  97.5 1.3 collective-permute-start.14
  99.4 6.6 %collective-permute-done.13.refs_5_ = bf16[512,512]{1,0:T(8,128)(2,1)S(1)} collective-permute-done((bf16[512,512]{1,0:T(8,128)(2,1)S(1)}, bf16[512,512]{1,0:T(8,128)(2,1)S(1)}, u32[]{:S(2)}, u32[]{:S(2)}) %collective-permute-start.13) | collective-permute-done | bytes 524320 | tf_op jit(solution)/shard_map/ppermute | solution.py:43
  106.1 5.6 %collective-permute-done.11.refs_3_ = bf16[512,512]{1,0:T(8,128)(2,1)} collective-permute-done((bf16[512,512]{1,0:T(8,128)(2,1)}, bf16[512,512]{1,0:T(8,128)(2,1)}, u32[]{:S(2)}, u32[]{:S(2)}) %collective-permute-start.11) | collective-permute-done | bytes 524320 | tf_op jit(solution)/shard_map/ppermute | solution.py:44
  112.7 4.6 %collective-permute-done.15.refs_7_ = bf16[512,512]{1,0:T(8,128)(2,1)} collective-permute-done((bf16[512,512]{1,0:T(8,128)(2,1)S(1)}, bf16[512,512]{1,0:T(8,128)(2,1)}, u32[]{:S(2)}, u32[]{:S(2)}) %collective-permute-start.15) | collective-permute-done | bytes 524320 | tf_op jit(solution)/shard_map/ppermute | solution.py:46
  117.3 19.6 %shard_map.38 = (f32[128,1536]{1,0:T(8,128)S(1)}, bf16[128,1536]{1,0:T(8,128)(2,1)S(1)}, bf16[128,1536]{1,0:T(8,128)(2,1)S(1)}, bf16[128,1536]{1,0:T(8,128)(2,1)S(1)}) custom-call(s32[8]{0:T(128)S(1)} %stack.58.chips, bf16[512,512]{1,0:T(8,128)(2,1)S(1)} %add_convert_fusion.refs_0_, bf16[512,512]{1,0:T(8,128)(2,1)} %collective-permute-done.9.refs_1_, ...), custom_call_target="tpu_custom_call" | custom-call | flops 6442450944 | bytes 12582912 | tf_op jit(solution)/shard_map/pallas_call | solution.py:137
  137.0 3.3 %collective-permute-start.18 = (bf16[128,1536]{1,0:T(8,128)(2,1)S(1)}, bf16[128,1536]{1,0:T(8,128)(2,1)S(1)}, u32[]{:S(2)}, u32[]{:S(2)}) collective-permute-start(bf16[128,1536]{1,0:T(8,128)(2,1)S(1)} %get-tuple-element.20), channel_id=1, source_target_pairs={{0,2},{1,3},{2,0},{3,1},{4,6},{5,7},{6,4},{7,5},{8,10},{9,11},{10,... | collective-permute-start | bytes 1179656 | tf_op jit(solution)/shard_map/ppermute | solution.py:164
  140.2 1.1 collective-permute-start.17
  141.3 1.0 collective-permute-start.16
  142.3 19.1 %shard_map.39 = (f32[128,1536]{1,0:T(8,128)S(1)}, bf16[128,1536]{1,0:T(8,128)(2,1)S(1)}, bf16[128,1536]{1,0:T(8,128)(2,1)S(1)}, bf16[128,1536]{1,0:T(8,128)(2,1)S(1)}) custom-call(s32[8]{0:T(128)S(1)} %stack.65.chips, bf16[512,512]{1,0:T(8,128)(2,1)S(1)} %collective-permute-done.20.refs_0_, bf16[512,512]{1,0:T(8,128)(2,1)S(1)} %collective-permute-done.21.refs_1_, ...), custom_call_target="tpu_custom_call" | custom-call | flops 6442450944 | bytes 12582912 | tf_op jit(solution)/shard_map/pallas_call | solution.py:137
  162.2 2.6 %collective-permute-start.29 = (bf16[128,1536]{1,0:T(8,128)(2,1)S(1)}, bf16[128,1536]{1,0:T(8,128)(2,1)S(1)}, u32[]{:S(2)}, u32[]{:S(2)}) collective-permute-start(bf16[128,1536]{1,0:T(8,128)(2,1)S(1)} %get-tuple-element.23), channel_id=1, source_target_pairs={{0,3},{1,0},{2,1},{3,2},{4,7},{5,4},{6,5},{7,6},{8,11},{9,8},{10,9... | collective-permute-start | bytes 1179656 | tf_op jit(solution)/shard_map/ppermute | solution.py:164
  165.0 2.8 %collective-permute-start.19 = (bf16[64,1536]{1,0:T(8,128)(2,1)S(1)}, bf16[64,1536]{1,0:T(8,128)(2,1)S(1)}, u32[]{:S(2)}, u32[]{:S(2)}) collective-permute-start(bf16[64,1536]{1,0:T(8,128)(2,1)S(1)} %slice.35), channel_id=1, source_target_pairs={{0,4},{1,5},{2,6},{3,7},{4,0},{5,1},{6,2},{7,3},{8,12},{9,13},{10,... | collective-permute-start | bytes 589832 | tf_op jit(solution)/shard_map/ppermute | solution.py:169
  167.8 7.2 %collective-permute-done.30 = bf16[128,1536]{1,0:T(8,128)(2,1)S(1)} collective-permute-done((bf16[128,1536]{1,0:T(8,128)(2,1)S(1)}, bf16[128,1536]{1,0:T(8,128)(2,1)S(1)}, u32[]{:S(2)}, u32[]{:S(2)}) %collective-permute-start.30) | collective-permute-done | bytes 393248 | tf_op jit(solution)/shard_map/ppermute | solution.py:164
  175.0 6.7 %collective-permute-done.29 = bf16[128,1536]{1,0:T(8,128)(2,1)S(1)} collective-permute-done((bf16[128,1536]{1,0:T(8,128)(2,1)S(1)}, bf16[128,1536]{1,0:T(8,128)(2,1)S(1)}, u32[]{:S(2)}, u32[]{:S(2)}) %collective-permute-start.29) | collective-permute-done | bytes 393248 | tf_op jit(solution)/shard_map/ppermute | solution.py:164
  182.3 2.8 %collective-permute-start.31 = (bf16[64,1536]{1,0:T(8,128)(2,1)S(1)}, bf16[64,1536]{1,0:T(8,128)(2,1)S(1)}, u32[]{:S(2)}, u32[]{:S(2)}) collective-permute-start(bf16[64,1536]{1,0:T(8,128)(2,1)S(1)} %slice.34), channel_id=1, source_target_pairs={{0,4},{1,5},{2,6},{3,7},{4,0},{5,1},{6,2},{7,3},{8,12},{9,13},{10,... | collective-permute-start | bytes 589832 | tf_op jit(solution)/shard_map/ppermute | solution.py:169
  185.1 5.6 %collective-permute-done.31 = bf16[64,1536]{1,0:T(8,128)(2,1)S(1)} collective-permute-done((bf16[64,1536]{1,0:T(8,128)(2,1)S(1)}, bf16[64,1536]{1,0:T(8,128)(2,1)S(1)}, u32[]{:S(2)}, u32[]{:S(2)}) %collective-permute-start.31) | collective-permute-done | bytes 196640 | tf_op jit(solution)/shard_map/ppermute | solution.py:169
  (57 shorter events, 6.6 us)
Async XLA Ops:
  4.8 9.5 %collective-permute-start = (bf16[64,2048]{1,0:T(8,128)(2,1)S(1)}, bf16[64,2048]{1,0:T(8,128)(2,1)S(1)}, u32[]{:S(2)}, u32[]{:S(2)}) collective-permute-start(bf16[64,2048]{1,0:T(8,128)(2,1)S(1)} %bitcast.30), channel_id=1, source_target_pairs={{0,8},{8,0},{16,24},{24,16},{32,40},{40,32},{48,56},{56,48},{64,72... | collective-permute-start | bytes 786440 | tf_op jit(solution)/shard_map/ppermute | solution.py:184
  7.8 65.8 %all-to-all-start = ((bf16[256,8,512]{2,0,1:T(8,128)(2,1)}), bf16[256,8,512]{2,0,1:T(8,128)(2,1)S(1)}, u32[]{:S(2)}, u32[]{:S(2)}) async-start(bf16[256,8,512]{2,0,1:T(8,128)(2,1)} %copy.6), calls=%async_computation | async-start | bytes 4194304 | tf_op jit(solution)/shard_map/all_to_all | solution.py:186
  14.2 37.6 %collective-permute-start.4 = (bf16[128,2048]{1,0:T(8,128)(2,1)S(1)}, bf16[128,2048]{1,0:T(8,128)(2,1)S(1)}, u32[]{:S(2)}, u32[]{:S(2)}) collective-permute-start(bf16[128,2048]{1,0:T(8,128)(2,1)S(1)} %constant_dynamic-update-slice_fusion.refs_0_), channel_id=1, source_target_pairs={{0,16},{8,24},{16,0},{24,8},{32,48},{40,56},{48,32},{56,40},{64,80... | collective-permute-start | bytes 1572872 | tf_op jit(solution)/shard_map/ppermute | solution.py:40
  16.3 36.0 %collective-permute-start.1 = (bf16[128,2048]{1,0:T(8,128)(2,1)S(1)}, bf16[128,2048]{1,0:T(8,128)(2,1)}, u32[]{:S(2)}, u32[]{:S(2)}) collective-permute-start(bf16[128,2048]{1,0:T(8,128)(2,1)S(1)} %constant_dynamic-update-slice_fusion.refs_0_), channel_id=1, source_target_pairs={{0,32},{8,104},{16,48},{24,120},{32,64},{40,8},{48,80},{56,24},{64... | collective-permute-start | bytes 1572872 | tf_op jit(solution)/shard_map/ppermute | solution.py:41
  17.8 36.7 %collective-permute-start.2 = (bf16[128,2048]{1,0:T(8,128)(2,1)S(1)}, bf16[128,2048]{1,0:T(8,128)(2,1)}, u32[]{:S(2)}, u32[]{:S(2)}) collective-permute-start(bf16[128,2048]{1,0:T(8,128)(2,1)S(1)} %constant_dynamic-update-slice_fusion.refs_0_), channel_id=1, source_target_pairs={{0,96},{8,40},{16,112},{24,56},{32,0},{40,72},{48,16},{56,88},{64,... | collective-permute-start | bytes 1572872 | tf_op jit(solution)/shard_map/ppermute | solution.py:42
  51.9 10.5 %collective-permute-start.5 = (bf16[128,2048]{1,0:T(8,128)(2,1)S(1)}, bf16[128,2048]{1,0:T(8,128)(2,1)}, u32[]{:S(2)}, u32[]{:S(2)}) collective-permute-start(bf16[128,2048]{1,0:T(8,128)(2,1)S(1)} %collective-permute-done.4.refs_4_), channel_id=1, source_target_pairs={{0,32},{8,104},{16,48},{24,120},{32,64},{40,8},{48,80},{56,24},{64... | collective-permute-start | bytes 1572872 | tf_op jit(solution)/shard_map/ppermute | solution.py:43
  52.4 15.6 %collective-permute-start.3 = (bf16[128,2048]{1,0:T(8,128)(2,1)}, bf16[128,2048]{1,0:T(8,128)(2,1)}, u32[]{:S(2)}, u32[]{:S(2)}) collective-permute-start(bf16[128,2048]{1,0:T(8,128)(2,1)} %collective-permute-done.1.refs_1_), channel_id=1, source_target_pairs={{0,32},{8,104},{16,48},{24,120},{32,64},{40,8},{48,80},{56,24},{64... | collective-permute-start | bytes 1572872 | tf_op jit(solution)/shard_map/ppermute | solution.py:44
  54.5 13.6 %collective-permute-start.6 = (bf16[128,2048]{1,0:T(8,128)(2,1)}, bf16[128,2048]{1,0:T(8,128)(2,1)}, u32[]{:S(2)}, u32[]{:S(2)}) collective-permute-start(bf16[128,2048]{1,0:T(8,128)(2,1)} %collective-permute-done.2.refs_2_), channel_id=1, source_target_pairs={{0,16},{8,24},{16,0},{24,8},{32,48},{40,56},{48,32},{56,40},{64,80... | collective-permute-start | bytes 1572872 | tf_op jit(solution)/shard_map/ppermute | solution.py:45
  62.4 11.2 %collective-permute-start.7 = (bf16[128,2048]{1,0:T(8,128)(2,1)}, bf16[128,2048]{1,0:T(8,128)(2,1)}, u32[]{:S(2)}, u32[]{:S(2)}) collective-permute-start(bf16[128,2048]{1,0:T(8,128)(2,1)} %collective-permute-done.5.refs_5_), channel_id=1, source_target_pairs={{0,32},{8,104},{16,48},{24,120},{32,64},{40,8},{48,80},{56,24},{64... | collective-permute-start | bytes 1572872 | tf_op jit(solution)/shard_map/ppermute | solution.py:46
  81.6 14.0 %collective-permute-start.12 = (bf16[512,512]{1,0:T(8,128)(2,1)S(1)}, bf16[512,512]{1,0:T(8,128)(2,1)S(1)}, u32[]{:S(2)}, u32[]{:S(2)}) collective-permute-start(bf16[512,512]{1,0:T(8,128)(2,1)S(1)} %add_convert_fusion.refs_0_), channel_id=1, source_target_pairs={{0,16},{8,24},{16,0},{24,8},{32,48},{40,56},{48,32},{56,40},{64,80... | collective-permute-start | bytes 1572872 | tf_op jit(solution)/shard_map/ppermute | solution.py:40
  81.6 15.9 %collective-permute-start.9 = (bf16[512,512]{1,0:T(8,128)(2,1)S(1)}, bf16[512,512]{1,0:T(8,128)(2,1)}, u32[]{:S(2)}, u32[]{:S(2)}) collective-permute-start(bf16[512,512]{1,0:T(8,128)(2,1)S(1)} %add_convert_fusion.refs_0_), channel_id=1, source_target_pairs={{0,32},{8,104},{16,48},{24,120},{32,64},{40,8},{48,80},{56,24},{64... | collective-permute-start | bytes 1572872 | tf_op jit(solution)/shard_map/ppermute | solution.py:41
  81.7 15.8 %collective-permute-start.10 = (bf16[512,512]{1,0:T(8,128)(2,1)S(1)}, bf16[512,512]{1,0:T(8,128)(2,1)}, u32[]{:S(2)}, u32[]{:S(2)}) collective-permute-start(bf16[512,512]{1,0:T(8,128)(2,1)S(1)} %add_convert_fusion.refs_0_), channel_id=1, source_target_pairs={{0,96},{8,40},{16,112},{24,56},{32,0},{40,72},{48,16},{56,88},{64,... | collective-permute-start | bytes 1572872 | tf_op jit(solution)/shard_map/ppermute | solution.py:42
  85.0 13.9 %collective-permute-start.20 = (bf16[512,512]{1,0:T(8,128)(2,1)S(1)}, bf16[512,512]{1,0:T(8,128)(2,1)S(1)}, u32[]{:S(2)}, u32[]{:S(2)}) collective-permute-start(bf16[512,512]{1,0:T(8,128)(2,1)S(1)} %add_convert_fusion.refs_0_), channel_id=1, source_target_pairs={{0,8},{8,0},{16,24},{24,16},{32,40},{40,32},{48,56},{56,48},{64,72... | collective-permute-start | bytes 1572872 | tf_op jit(solution)/shard_map/ppermute | solution.py:195
  95.6 10.4 %collective-permute-start.13 = (bf16[512,512]{1,0:T(8,128)(2,1)S(1)}, bf16[512,512]{1,0:T(8,128)(2,1)S(1)}, u32[]{:S(2)}, u32[]{:S(2)}) collective-permute-start(bf16[512,512]{1,0:T(8,128)(2,1)S(1)} %collective-permute-done.12.refs_4_), channel_id=1, source_target_pairs={{0,32},{8,104},{16,48},{24,120},{32,64},{40,8},{48,80},{56,24},{64... | collective-permute-start | bytes 1572872 | tf_op jit(solution)/shard_map/ppermute | solution.py:43
  97.5 14.2 %collective-permute-start.11 = (bf16[512,512]{1,0:T(8,128)(2,1)}, bf16[512,512]{1,0:T(8,128)(2,1)}, u32[]{:S(2)}, u32[]{:S(2)}) collective-permute-start(bf16[512,512]{1,0:T(8,128)(2,1)} %collective-permute-done.9.refs_1_), channel_id=1, source_target_pairs={{0,32},{8,104},{16,48},{24,120},{32,64},{40,8},{48,80},{56,24},{64... | collective-permute-start | bytes 1572872 | tf_op jit(solution)/shard_map/ppermute | solution.py:44
  97.5 14.2 %collective-permute-start.14 = (bf16[512,512]{1,0:T(8,128)(2,1)}, bf16[512,512]{1,0:T(8,128)(2,1)}, u32[]{:S(2)}, u32[]{:S(2)}) collective-permute-start(bf16[512,512]{1,0:T(8,128)(2,1)} %collective-permute-done.10.refs_2_), channel_id=1, source_target_pairs={{0,16},{8,24},{16,0},{24,8},{32,48},{40,56},{48,32},{56,40},{64,80... | collective-permute-start | bytes 1572872 | tf_op jit(solution)/shard_map/ppermute | solution.py:45
  98.9 13.4 %collective-permute-start.21 = (bf16[512,512]{1,0:T(8,128)(2,1)}, bf16[512,512]{1,0:T(8,128)(2,1)S(1)}, u32[]{:S(2)}, u32[]{:S(2)}) collective-permute-start(bf16[512,512]{1,0:T(8,128)(2,1)} %collective-permute-done.9.refs_1_), channel_id=1, source_target_pairs={{0,8},{8,0},{16,24},{24,16},{32,40},{40,32},{48,56},{56,48},{64,72... | collective-permute-start | bytes 1572872 | tf_op jit(solution)/shard_map/ppermute | solution.py:195
  98.9 13.5 %collective-permute-start.22 = (bf16[512,512]{1,0:T(8,128)(2,1)}, bf16[512,512]{1,0:T(8,128)(2,1)}, u32[]{:S(2)}, u32[]{:S(2)}) collective-permute-start(bf16[512,512]{1,0:T(8,128)(2,1)} %collective-permute-done.10.refs_2_), channel_id=1, source_target_pairs={{0,8},{8,0},{16,24},{24,16},{32,40},{40,32},{48,56},{56,48},{64,72... | collective-permute-start | bytes 1572872 | tf_op jit(solution)/shard_map/ppermute | solution.py:195
  106.0 11.3 %collective-permute-start.15 = (bf16[512,512]{1,0:T(8,128)(2,1)S(1)}, bf16[512,512]{1,0:T(8,128)(2,1)}, u32[]{:S(2)}, u32[]{:S(2)}) collective-permute-start(bf16[512,512]{1,0:T(8,128)(2,1)S(1)} %collective-permute-done.13.refs_5_), channel_id=1, source_target_pairs={{0,32},{8,104},{16,48},{24,120},{32,64},{40,8},{48,80},{56,24},{64... | collective-permute-start | bytes 1572872 | tf_op jit(solution)/shard_map/ppermute | solution.py:46
  111.7 25.3 %collective-permute-start.24 = (bf16[512,512]{1,0:T(8,128)(2,1)S(1)}, bf16[512,512]{1,0:T(8,128)(2,1)S(1)}, u32[]{:S(2)}, u32[]{:S(2)}) collective-permute-start(bf16[512,512]{1,0:T(8,128)(2,1)S(1)} %collective-permute-done.12.refs_4_), channel_id=1, source_target_pairs={{0,8},{8,0},{16,24},{24,16},{32,40},{40,32},{48,56},{56,48},{64,72... | collective-permute-start | bytes 1572872 | tf_op jit(solution)/shard_map/ppermute | solution.py:195
  111.7 29.6 %collective-permute-start.25 = (bf16[512,512]{1,0:T(8,128)(2,1)S(1)}, bf16[512,512]{1,0:T(8,128)(2,1)S(1)}, u32[]{:S(2)}, u32[]{:S(2)}) collective-permute-start(bf16[512,512]{1,0:T(8,128)(2,1)S(1)} %collective-permute-done.13.refs_5_), channel_id=1, source_target_pairs={{0,8},{8,0},{16,24},{24,16},{32,40},{40,32},{48,56},{56,48},{64,72... | collective-permute-start | bytes 1572872 | tf_op jit(solution)/shard_map/ppermute | solution.py:195
  112.2 28.0 %collective-permute-start.23 = (bf16[512,512]{1,0:T(8,128)(2,1)}, bf16[512,512]{1,0:T(8,128)(2,1)S(1)}, u32[]{:S(2)}, u32[]{:S(2)}) collective-permute-start(bf16[512,512]{1,0:T(8,128)(2,1)} %collective-permute-done.11.refs_3_), channel_id=1, source_target_pairs={{0,8},{8,0},{16,24},{24,16},{32,40},{40,32},{48,56},{56,48},{64,72... | collective-permute-start | bytes 1572872 | tf_op jit(solution)/shard_map/ppermute | solution.py:195
  112.3 30.0 %collective-permute-start.26 = (bf16[512,512]{1,0:T(8,128)(2,1)}, bf16[512,512]{1,0:T(8,128)(2,1)S(1)}, u32[]{:S(2)}, u32[]{:S(2)}) collective-permute-start(bf16[512,512]{1,0:T(8,128)(2,1)} %collective-permute-done.14.refs_6_), channel_id=1, source_target_pairs={{0,8},{8,0},{16,24},{24,16},{32,40},{40,32},{48,56},{56,48},{64,72... | collective-permute-start | bytes 1572872 | tf_op jit(solution)/shard_map/ppermute | solution.py:195
  117.3 25.0 %collective-permute-start.27 = (bf16[512,512]{1,0:T(8,128)(2,1)}, bf16[512,512]{1,0:T(8,128)(2,1)S(1)}, u32[]{:S(2)}, u32[]{:S(2)}) collective-permute-start(bf16[512,512]{1,0:T(8,128)(2,1)} %collective-permute-done.15.refs_7_), channel_id=1, source_target_pairs={{0,8},{8,0},{16,24},{24,16},{32,40},{40,32},{48,56},{56,48},{64,72... | collective-permute-start | bytes 1572872 | tf_op jit(solution)/shard_map/ppermute | solution.py:195
  137.0 27.8 %collective-permute-start.18 = (bf16[128,1536]{1,0:T(8,128)(2,1)S(1)}, bf16[128,1536]{1,0:T(8,128)(2,1)S(1)}, u32[]{:S(2)}, u32[]{:S(2)}) collective-permute-start(bf16[128,1536]{1,0:T(8,128)(2,1)S(1)} %get-tuple-element.20), channel_id=1, source_target_pairs={{0,2},{1,3},{2,0},{3,1},{4,6},{5,7},{6,4},{7,5},{8,10},{9,11},{10,... | collective-permute-start | bytes 1179656 | tf_op jit(solution)/shard_map/ppermute | solution.py:164
  140.2 24.5 %collective-permute-start.17 = (bf16[128,1536]{1,0:T(8,128)(2,1)S(1)}, bf16[128,1536]{1,0:T(8,128)(2,1)S(1)}, u32[]{:S(2)}, u32[]{:S(2)}) collective-permute-start(bf16[128,1536]{1,0:T(8,128)(2,1)S(1)} %get-tuple-element.19), channel_id=1, source_target_pairs={{0,3},{1,0},{2,1},{3,2},{4,7},{5,4},{6,5},{7,6},{8,11},{9,8},{10,9... | collective-permute-start | bytes 1179656 | tf_op jit(solution)/shard_map/ppermute | solution.py:164
  141.3 23.5 %collective-permute-start.16 = (bf16[128,1536]{1,0:T(8,128)(2,1)S(1)}, bf16[128,1536]{1,0:T(8,128)(2,1)S(1)}, u32[]{:S(2)}, u32[]{:S(2)}) collective-permute-start(bf16[128,1536]{1,0:T(8,128)(2,1)S(1)} %get-tuple-element.18), channel_id=1, source_target_pairs={{0,1},{1,2},{2,3},{3,0},{4,5},{5,6},{6,7},{7,4},{8,9},{9,10},{10,1... | collective-permute-start | bytes 1179656 | tf_op jit(solution)/shard_map/ppermute | solution.py:164
  161.4 13.7 %collective-permute-start.30 = (bf16[128,1536]{1,0:T(8,128)(2,1)S(1)}, bf16[128,1536]{1,0:T(8,128)(2,1)S(1)}, u32[]{:S(2)}, u32[]{:S(2)}) collective-permute-start(bf16[128,1536]{1,0:T(8,128)(2,1)S(1)} %get-tuple-element.24), channel_id=1, source_target_pairs={{0,2},{1,3},{2,0},{3,1},{4,6},{5,7},{6,4},{7,5},{8,10},{9,11},{10,... | collective-permute-start | bytes 1179656 | tf_op jit(solution)/shard_map/ppermute | solution.py:164
  162.2 19.5 %collective-permute-start.29 = (bf16[128,1536]{1,0:T(8,128)(2,1)S(1)}, bf16[128,1536]{1,0:T(8,128)(2,1)S(1)}, u32[]{:S(2)}, u32[]{:S(2)}) collective-permute-start(bf16[128,1536]{1,0:T(8,128)(2,1)S(1)} %get-tuple-element.23), channel_id=1, source_target_pairs={{0,3},{1,0},{2,1},{3,2},{4,7},{5,4},{6,5},{7,6},{8,11},{9,8},{10,9... | collective-permute-start | bytes 1179656 | tf_op jit(solution)/shard_map/ppermute | solution.py:164
  164.8 17.3 %collective-permute-start.28 = (bf16[128,1536]{1,0:T(8,128)(2,1)S(1)}, bf16[128,1536]{1,0:T(8,128)(2,1)S(1)}, u32[]{:S(2)}, u32[]{:S(2)}) collective-permute-start(bf16[128,1536]{1,0:T(8,128)(2,1)S(1)} %get-tuple-element.22), channel_id=1, source_target_pairs={{0,1},{1,2},{2,3},{3,0},{4,5},{5,6},{6,7},{7,4},{8,9},{9,10},{10,1... | collective-permute-start | bytes 1179656 | tf_op jit(solution)/shard_map/ppermute | solution.py:164
  165.0 20.1 %collective-permute-start.19 = (bf16[64,1536]{1,0:T(8,128)(2,1)S(1)}, bf16[64,1536]{1,0:T(8,128)(2,1)S(1)}, u32[]{:S(2)}, u32[]{:S(2)}) collective-permute-start(bf16[64,1536]{1,0:T(8,128)(2,1)S(1)} %slice.35), channel_id=1, source_target_pairs={{0,4},{1,5},{2,6},{3,7},{4,0},{5,1},{6,2},{7,3},{8,12},{9,13},{10,... | collective-permute-start | bytes 589832 | tf_op jit(solution)/shard_map/ppermute | solution.py:169
  182.3 8.4 %collective-permute-start.31 = (bf16[64,1536]{1,0:T(8,128)(2,1)S(1)}, bf16[64,1536]{1,0:T(8,128)(2,1)S(1)}, u32[]{:S(2)}, u32[]{:S(2)}) collective-permute-start(bf16[64,1536]{1,0:T(8,128)(2,1)S(1)} %slice.34), channel_id=1, source_target_pairs={{0,4},{1,5},{2,6},{3,7},{4,0},{5,1},{6,2},{7,3},{8,12},{9,13},{10,... | collective-permute-start | bytes 589832 | tf_op jit(solution)/shard_map/ppermute | solution.py:169
  (2 other events, 7.6 us)

commit v2 on v0

v2 whole, which is shorter than its diff:
```python
import functools

import jax
import jax.numpy as jnp
from jax import lax
from jax.experimental import pallas as pl
from jax.experimental.pallas import tpu as pltpu
from jax.sharding import PartitionSpec as P

NZ, NX, NC, NH, NY = 4, 2, 2, 2, 4
CHIPS = NZ * NX
GROUP = NH * NY
ROLES = ((0, 0), (0, 1), (-1, 0), (1, 0), (-1, 1), (2, 0), (1, 1), (2, 1))
STAGES = ((0, 4), (4, 7), (7, 8))


def corpus_perm(move):
    pairs = []
    for z in range(NZ):
        for x in range(NX):
            for c in range(NC):
                dz, dx, dc = move(1 - 2 * c)
                to = ((z + dz) % NZ, (x + dx) % NX, (c + dc) % NC)
                pairs.append(((z * NX + x) * NC + c, (to[0] * NX + to[1]) * NC + to[2]))
    return pairs


def group_perm(dh, dy):
    return [(h * NY + y, (h + dh) % NH * NY + (y + dy) % NY) for h in range(NH) for y in range(NY)]


AHEAD = corpus_perm(lambda d: (d, 0, 0))
BACK = corpus_perm(lambda d: (-d, 0, 0))
CROSS = corpus_perm(lambda d: (0, 1, 0))
CORE = corpus_perm(lambda d: (0, 0, 1))


CHUNKS = 2
STEP = 512
SCOPED = 16 * 2**20
ANY_SPEC = pl.BlockSpec(memory_space=pl.ANY)
HBM_SPEC = pl.BlockSpec(memory_space=pltpu.HBM)
VMEM_SPEC = pl.BlockSpec(memory_space=pltpu.VMEM)
SMEM_SPEC = pl.BlockSpec(memory_space=pltpu.SMEM)


def move(piece, perm, axis="corpus"):
    return lax.ppermute(piece, axis, perm)


def with_core(pieces):
    return [p for piece in pieces for p in (piece, move(piece, CORE))]


def first_stage(own):
    return [own, move(own, CROSS), move(own, AHEAD), move(own, BACK)]


def second_stage(own, cross, behind, ahead):
    return [move(cross, AHEAD), move(behind, AHEAD), move(ahead, CROSS)]


def third_stage(cross_behind, far, cross_ahead):
    return [move(cross_behind, AHEAD)]


def places():
    place = lax.axis_index("corpus")
    z, x, core = place // (NX * NC), place // NC % NX, place % NC
    chips, cores = [], []
    for dz, dx in ROLES:
        for c in (core, 1 - core):
            chips.append(((z + dz * (1 - 2 * c) + NZ) % NZ) * NX + (x + dx) % NX)
            cores.append(c)
    return jnp.stack(chips), jnp.stack(cores)


def blocks_kernel(weights, out, sems):
    wide = out.shape[2]
    copies = [
        pltpu.make_async_copy(weights.at[0, :, pl.ds(i * wide, wide)], out.at[i], sems.at[i])
        for i in range(out.shape[0])
    ]
    for copy in copies:
        copy.start()
    for copy in copies:
        copy.wait()


def column_blocks(weights, count):
    _, rows, columns = weights.shape
    return pl.pallas_call(
        blocks_kernel,
        out_shape=jax.ShapeDtypeStruct((count, rows, columns // count), weights.dtype),
        in_specs=[HBM_SPEC],
        out_specs=VMEM_SPEC,
        scratch_shapes=[pltpu.SemaphoreType.DMA((count,))],
    )(weights)


def condition_kernel(n, place, *refs):
    pieces, weights, (out, held, rows, sems) = refs[:n], refs[n], refs[n + 1 :]
    tall = pieces[0].shape[0]
    loads = [pltpu.make_async_copy(weights, held, sems.at[n])]
    for i, piece in enumerate(pieces):
        loads.append(pltpu.make_async_copy(piece, rows.at[pl.ds(i * tall, tall), :], sems.at[i]))
    for load in loads:
        load.start()
    for load in loads:
        load.wait()
    done = jnp.dot(rows[...], held[...], preferred_element_type=jnp.float32).astype(jnp.bfloat16)
    to_places(place, n, tall, done, out)


def to_places(place, n, tall, done, out):
    few = tall // CHUNKS
    for i in range(n):
        for k in range(CHUNKS):
            to = pl.multiple_of(place[k, i] * few, few)
            out[pl.ds(to, few), :] = done[i * tall + k * few : i * tall + (k + 1) * few, :]


def condition(place, pieces, weights):
    tall, depth = pieces[0].shape
    wide = weights.shape[1]
    n = len(pieces)
    return pl.pallas_call(
        functools.partial(condition_kernel, n),
        out_shape=[
            jax.ShapeDtypeStruct((CHIPS * NC * tall, wide), jnp.bfloat16),
            jax.ShapeDtypeStruct(weights.shape, weights.dtype),
        ],
        in_specs=[SMEM_SPEC] + [ANY_SPEC] * n + [HBM_SPEC],
        out_specs=[VMEM_SPEC] * 2,
        scratch_shapes=[pltpu.VMEM((n * tall, depth), jnp.bfloat16), pltpu.SemaphoreType.DMA((n + 1,))],
        compiler_params=pltpu.CompilerParams(vmem_limit_bytes=48 * 2**20),
        cost_estimate=pl.CostEstimate(
            flops=2 * n * tall * depth * wide, bytes_accessed=(n * tall + wide) * depth * 2, transcendentals=0
        ),
    )(place, *pieces, weights)


def condition_rest_kernel(n, place, *refs):
    pieces, (weights, into, out) = refs[:n], refs[n:]
    tall = pieces[0].shape[0]
    rows = jnp.concatenate([piece[...] for piece in pieces], axis=0)
    done = jnp.dot(rows, weights[...], preferred_element_type=jnp.float32).astype(jnp.bfloat16)
    out[...] = into[...]
    to_places(place, n, tall, done, out)


def condition_rest(place, pieces, weights, into):
    tall, depth = pieces[0].shape
    n = len(pieces)
    return pl.pallas_call(
        functools.partial(condition_rest_kernel, n),
        out_shape=jax.ShapeDtypeStruct(into.shape, into.dtype),
        in_specs=[SMEM_SPEC] + [VMEM_SPEC] * (n + 2),
        out_specs=VMEM_SPEC,
        compiler_params=pltpu.CompilerParams(vmem_limit_bytes=SCOPED),
        cost_estimate=pl.CostEstimate(
            flops=2 * n * tall * depth * into.shape[1], bytes_accessed=2**22, transcendentals=0
        ),
    )(place, *pieces, weights, into)


def score_kernel(n, adds, last, blocks, *refs):
    pieces, docs = refs[:n], refs[n]
    wide = pieces[0].shape[1]
    if last:
        outs = refs[n + 1 + adds :]
        rows = jnp.concatenate([piece[...] for piece in pieces], axis=1)
    else:
        outs, (packed, sems) = refs[n + 1 + adds : -2], refs[-2:]
        copies = [
            pltpu.make_async_copy(piece, packed.at[:, pl.ds(i * wide, wide)], sems.at[i])
            for i, piece in enumerate(pieces)
        ]
        for copy in copies:
            copy.start()
        for copy in copies:
            copy.wait()
        rows = packed[...]
    for j in range(docs.shape[0] // STEP):
        at = slice(j * STEP, (j + 1) * STEP)
        held = jnp.concatenate(
            [docs[at, pl.ds(pl.multiple_of(blocks[i] * wide, wide), wide)] for i in range(n)], axis=1
        )
        part = lax.dot_general(rows, held, (((1,), (1,)), ((), ())), preferred_element_type=jnp.float32)
        if adds:
            part += refs[n + 1][:, at]
        start = 0
        for out in outs:
            out[:, at] = part[start : start + out.shape[0], :].astype(out.dtype)
            start += out.shape[0]


def score(blocks, pieces, docs, before=None, last=False):
    rows, wide = pieces[0].shape
    n_docs = docs.shape[0]
    n = len(pieces)
    given = [] if before is None else [before]
    if last:
        tall = rows // CHUNKS
        shapes = [
            jax.ShapeDtypeStruct((tall // count, n_docs), jnp.bfloat16 if i else jnp.float32)
            for count in (NH, NY)
            for i in range(count)
        ]
    else:
        shapes = [jax.ShapeDtypeStruct((rows, n_docs), jnp.float32)]
    return pl.pallas_call(
        functools.partial(score_kernel, n, len(given), last),
        out_shape=shapes,
        in_specs=[SMEM_SPEC] + [VMEM_SPEC if last else ANY_SPEC] * n + [VMEM_SPEC] * (1 + len(given)),
        out_specs=[VMEM_SPEC] * len(shapes),
        scratch_shapes=[] if last else [pltpu.VMEM((rows, n * wide), jnp.bfloat16), pltpu.SemaphoreType.DMA((n,))],
        input_output_aliases={n + 2: 0} if given and not last else {},
        compiler_params=pltpu.CompilerParams(vmem_limit_bytes=SCOPED),
        cost_estimate=pl.CostEstimate(
            flops=2 * rows * n_docs * n * wide, bytes_accessed=(rows + n_docs) * n * wide * 2, transcendentals=0
        ),
    )(blocks, *pieces, docs, *given)


def exchange_y(own, ahead, far, back):
    steps = ((ahead, 1), (back, -1), (far, 2))
    return [own] + [move(part, group_perm(0, dy), "group") for part, dy in steps]


def exchange_h(own, other):
    return [own, move(other, group_perm(1, 0), "group")]


def added(parts):
    return sum(part.astype(jnp.float32) for part in parts)


def parts_of(rows, count):
    tall = rows.shape[0] // count
    return [rows[i * tall : (i + 1) * tall].astype(jnp.bfloat16 if i else jnp.float32) for i in range(count)]


def local(queries, precond, documents):
    rows, feat = queries.shape
    h, y = lax.axis_index("group") // NY, lax.axis_index("group") % NY
    chips, cores = places()
    dy, dh = (chips % NY - y + NY) % NY, (chips // NY - h + NH) % NH
    place = jnp.stack([(dh * NY + dy) * NC + cores, GROUP * NC + (dy * NH + dh) * NC + cores])
    blocks = chips * NC + cores
    early = NC * STAGES[1][1]
    half = NC * STAGES[0][1]

    one = lax.optimization_barrier(first_stage(queries))
    weights = lax.all_to_all(column_blocks(precond, CHIPS * NC), "corpus", 0, 0, tiled=True).reshape(feat, -1)
    two = second_stage(*one)
    three = third_stage(*two)
    conditioned, weights = condition(place[:, :early], with_core(one + two), weights)
    three, conditioned = lax.optimization_barrier((three, conditioned))
    conditioned = condition_rest(place[:, early:], with_core(three), weights, conditioned)

    one = first_stage(conditioned)
    two = second_stage(*one)
    (scores,) = score(blocks[:half], with_core(one), documents)
    two, scores = lax.optimization_barrier((two, scores))
    three = third_stage(*two)
    (scores,) = score(blocks[half:early], with_core(two), documents, scores)
    three, scores = lax.optimization_barrier((three, scores))
    parts = score(blocks[early:], with_core(three), documents, scores, last=True)
    first, second = lax.optimization_barrier((exchange_h(*parts[:NH]), exchange_y(*parts[NH:])))
    first = added(exchange_y(*parts_of(added(first), NY)))
    second = added(exchange_h(*parts_of(added(second), NH)))
    totals = [total.reshape(NC, rows // CHUNKS, -1) for total in (first, second)]
    scores = jnp.concatenate(totals, axis=1).reshape(NC * rows, -1)
    return scores / jnp.sqrt(jnp.float32(GROUP * feat))


def solution(mesh):
    placed = (P("corpus", "group"), P("group", "corpus", None), P("corpus", "group"))
    return jax.shard_map(
        local, mesh=mesh, in_specs=placed, out_specs=P("group", "corpus"), check_vma=False
    )
```

time: 378 us -> 162 us (0.43)
  waiting for transfers between devices: 328 us -> 76.6 us
  starting transfers between devices: 0.08 us -> 39 us
  matrix products: 34.1 us -> 0 us
  Pallas kernels: 0 us -> 28.5 us
  local copies, waits for them, and re-layouts: 0.01 us -> 15.2 us
  between operations: 13.1 us -> 0.24 us
    all_gather x2 -> x0, waiting for transfers between devices: 228 us -> none  [the longest x1 175 us: local(): lax.all_gather(precond, 'corpus', axis=1, tiled=True)[0]]
    reduce_scatter x1 -> x0, waiting for transfers between devices: 99.3 us -> none  [local(): lax.psum_scatter(block, 'group', scatter_dimension=0, tiled=True)]
    ppermute x0 -> x38, waiting for transfers between devices: none -> 76.6 us  [move(): return lax.ppermute(piece, axis, perm)]
    ppermute x0 -> x38, starting transfers between devices: none -> 34.4 us  [move(): return lax.ppermute(piece, axis, perm)]
    dot_general x2 -> x0, matrix products: 34.1 us -> none  [the longest x1 19.7 us: doc_scores(): lax.dot_general(rows, documents, (((1,), (1,)), ((), ())), preferred_elem...]
    pallas_call x0 -> x6, Pallas kernels: none -> 28.5 us  [the longest x3 17.4 us: score(): pl.pallas_call(functools.partial(score_kernel, n, len(given), last), out_...]
    unnamed x2 -> x16, local copies, waits for them, and re-layouts: 0.01 us -> 14.5 us
    all_to_all x0 -> x1, starting transfers between devices: none -> 4.58 us  [local(): lax.all_to_all(column_blocks(precond, CHIPS * NC), 'corpus', 0, 0, tiled=...]
  transfers between devices with their start and end apart: 3 -> 39, of which waited for: 3 -> 23; matrix products, arithmetic and copies ran while one was open for 0% -> 1% of each run, Pallas kernels for 0% -> 15%
where the time goes in v2:
time: 162 us; the launch traced here: 161 us
  waiting for transfers between devices  76.6 us (47%)
  starting transfers between devices  39 us (24%)
  Pallas kernels  28.5 us (18%)
  local copies, waits for them, and re-layouts  15.2 us (9%)
    ppermute x38, waiting for transfers between devices, move(): return lax.ppermute(piece, axis, perm)  76.6 us
    ppermute x38, starting transfers between devices, move(): return lax.ppermute(piece, axis, perm)  34.4 us
    pallas_call x3, Pallas kernels, score(): pl.pallas_call(functools.partial(score_kernel, n, len(given), last), out_...  17.4 us
    unnamed x16, local copies, waits for them, and re-layouts  14.5 us
    pallas_call x1, Pallas kernels, condition(): pl.pallas_call(functools.partial(condition_kernel, n), out_shape=[jax.Sha...  6.48 us
    all_to_all x1, starting transfers between devices, local(): lax.all_to_all(column_blocks(precond, CHIPS * NC), 'corpus', 0, 0, tiled=...  4.58 us
  transfers between devices with their start and end apart: 39, of which 23 were waited for; matrix products, arithmetic and copies ran while one was open for 1% of the time, Pallas kernels for 15%

profile of v2, /device:TPU:0, one launch (start us, length us, event | category | flops | bytes accessed | tf_op | source)
XLA Modules:
  0.0 161.0 jit_solution(16629730364908705360)
XLA Ops:
  0.0 2.0 %collective-permute-start.1 = (bf16[64,4096]{1,0:T(8,128)(2,1)}, bf16[64,4096]{1,0:T(8,128)(2,1)S(1)}, u32[]{:S(2)}, u32[]{:S(2)}) collective-permute-start(bf16[64,4096]{1,0:T(8,128)(2,1)} %refs_0_), channel_id=1, source_target_pairs={{0,32},{8,104},{16,48},{24,120},{32,64},{40,8},{48,80},{56,24},{64... | collective-permute-start | bytes 1572872 | tf_op jit(solution)/shard_map/ppermute | solution.py:48
  3.5 2.1 %collective-permute-start.2 = (bf16[64,4096]{1,0:T(8,128)(2,1)}, bf16[64,4096]{1,0:T(8,128)(2,1)S(1)}, u32[]{:S(2)}, u32[]{:S(2)}) collective-permute-start(bf16[64,4096]{1,0:T(8,128)(2,1)} %refs_0_), channel_id=1, source_target_pairs={{0,96},{8,40},{16,112},{24,56},{32,0},{40,72},{48,16},{56,88},{64,... | collective-permute-start | bytes 1572872 | tf_op jit(solution)/shard_map/ppermute | solution.py:48
  5.6 3.1 %shard_map.37 = bf16[16,256,256]{2,1,0:T(8,128)(2,1)} custom-call(bf16[1,256,4096]{2,1,0:T(8,128)(2,1)} %weights.1), custom_call_target="tpu_custom_call" | custom-call | tf_op jit(solution)/shard_map/pallas_call | solution.py:92
  8.7 4.6 %all-to-all-start = ((bf16[16,256,256]{2,1,0:T(8,128)(2,1)}), bf16[16,256,256]{2,1,0:T(8,128)(2,1)}, u32[]{:S(2)}, u32[]{:S(2)}) async-start(bf16[16,256,256]{2,1,0:T(8,128)(2,1)} %shard_map.37), calls=%async_computation | async-start | bytes 4194304 | tf_op jit(solution)/shard_map/all_to_all | solution.py:255
  14.0 2.3 %collective-permute-done.refs_2_ = bf16[64,4096]{1,0:T(8,128)(2,1)S(1)} collective-permute-done((bf16[64,4096]{1,0:T(8,128)(2,1)}, bf16[64,4096]{1,0:T(8,128)(2,1)S(1)}, u32[]{:S(2)}, u32[]{:S(2)}) %collective-permute-start) | collective-permute-done | bytes 524320 | tf_op jit(solution)/shard_map/ppermute | solution.py:48
  16.3 8.9 %collective-permute-done.2.refs_6_ = bf16[64,4096]{1,0:T(8,128)(2,1)S(1)} collective-permute-done((bf16[64,4096]{1,0:T(8,128)(2,1)}, bf16[64,4096]{1,0:T(8,128)(2,1)S(1)}, u32[]{:S(2)}, u32[]{:S(2)}) %collective-permute-start.2) | collective-permute-done | bytes 524320 | tf_op jit(solution)/shard_map/ppermute | solution.py:48
  25.7 3.5 %collective-permute-start.7 = (bf16[64,4096]{1,0:T(8,128)(2,1)S(1)}, bf16[64,4096]{1,0:T(8,128)(2,1)}, u32[]{:S(2)}, u32[]{:S(2)}) collective-permute-start(bf16[64,4096]{1,0:T(8,128)(2,1)S(1)} %collective-permute-done.1.refs_4_), channel_id=1, source_target_pairs={{0,8},{8,0},{16,24},{24,16},{32,40},{40,32},{48,56},{56,48},{64,72... | collective-permute-start | bytes 1572872 | tf_op jit(solution)/shard_map/ppermute | solution.py:48
  30.8 14.9 %collective-permute-done.3.refs_8_ = bf16[64,4096]{1,0:T(8,128)(2,1)S(1)} collective-permute-done((bf16[64,4096]{1,0:T(8,128)(2,1)S(1)}, bf16[64,4096]{1,0:T(8,128)(2,1)S(1)}, u32[]{:S(2)}, u32[]{:S(2)}) %collective-permute-start.3) | collective-permute-done | bytes 524320 | tf_op jit(solution)/shard_map/ppermute | solution.py:48
  45.6 5.7 %collective-permute-done.10.refs_10_ = bf16[64,4096]{1,0:T(8,128)(2,1)} collective-permute-done((bf16[64,4096]{1,0:T(8,128)(2,1)S(1)}, bf16[64,4096]{1,0:T(8,128)(2,1)}, u32[]{:S(2)}, u32[]{:S(2)}) %collective-permute-start.10) | collective-permute-done | bytes 524320 | tf_op jit(solution)/shard_map/ppermute | solution.py:48
  57.3 6.5 %shard_map.38 = (bf16[1024,256]{1,0:T(8,128)(2,1)S(1)}, bf16[4096,256]{1,0:T(8,128)(2,1)}) custom-call(s32[2,14]{1,0:T(2,128)S(1)} %bitcast.38, bf16[64,4096]{1,0:T(8,128)(2,1)S(1)} %copy-done.3, bf16[64,4096]{1,0:T(8,128)(2,1)S(1)} %collective-permute-done.5.refs_1_, bf16[64,4096]{1,0:T(8,128)(2,1)S(1)} %collective-permute-done.refs_2_, ...), custom_call_target="tpu_custom_call" | custom-call | flops 1879048192 | bytes 9437184 | tf_op jit(solution)/shard_map/pallas_call | solution.py:127
  64.3 1.7 %collective-permute-done.14.refs_1_ = bf16[64,4096]{1,0:T(8,128)(2,1)S(1)} collective-permute-done((bf16[64,4096]{1,0:T(8,128)(2,1)}, bf16[64,4096]{1,0:T(8,128)(2,1)S(1)}, u32[]{:S(2)}, u32[]{:S(2)}) %collective-permute-start.14) | collective-permute-done | bytes 524320 | tf_op jit(solution)/shard_map/ppermute | solution.py:48
  66.0 1.6 copy-done.2
  69.1 2.5 %collective-permute-start.19 = (bf16[1024,256]{1,0:T(8,128)(2,1)S(1)}, bf16[1024,256]{1,0:T(8,128)(2,1)S(1)}, u32[]{:S(2)}, u32[]{:S(2)}) collective-permute-start(bf16[1024,256]{1,0:T(8,128)(2,1)S(1)} %shard_map.39.refs_0_), channel_id=1, source_target_pairs={{0,96},{8,40},{16,112},{24,56},{32,0},{40,72},{48,16},{56,88},{64,... | collective-permute-start | bytes 1572872 | tf_op jit(solution)/shard_map/ppermute | solution.py:48
  73.4 10.4 %collective-permute-done.19.refs_6_ = bf16[1024,256]{1,0:T(8,128)(2,1)S(1)} collective-permute-done((bf16[1024,256]{1,0:T(8,128)(2,1)S(1)}, bf16[1024,256]{1,0:T(8,128)(2,1)S(1)}, u32[]{:S(2)}, u32[]{:S(2)}) %collective-permute-start.19) | collective-permute-done | bytes 524320 | tf_op jit(solution)/shard_map/ppermute | solution.py:48
  86.2 1.6 collective-permute-start.20
  88.5 4.6 %copy-done = bf16[1536,4096]{1,0:T(8,128)(2,1)S(1)} copy-done((bf16[1536,4096]{1,0:T(8,128)(2,1)S(1)}, bf16[1536,4096]{1,0:T(8,128)(2,1)}, u32[]{:S(2)}) %copy-start) | copy-done | bytes 12582936
  93.0 8.8 %shard_map.40.refs_7_ = f32[1024,1536]{1,0:T(8,128)S(1)} custom-call(s32[8]{0:T(128)S(1)} %bitcast.39, bf16[1024,256]{1,0:T(8,128)(2,1)S(1)} %shard_map.39.refs_0_, bf16[1024,256]{1,0:T(8,128)(2,1)S(1)} %collective-permute-done.21.refs_1_, bf16[1024,256]{1,0:T(8,128)(2,1)S(1)} %collective-permute-done.15.refs_2_, ...), custom_call_target="tpu_custom_call" | custom-call | flops 6442450944 | bytes 10485760 | tf_op jit(solution)/shard_map/pallas_call | solution.py:212
  101.8 2.0 %collective-permute-done.16.refs_0_ = bf16[1024,256]{1,0:T(8,128)(2,1)S(1)} collective-permute-done((bf16[1024,256]{1,0:T(8,128)(2,1)S(1)}, bf16[1024,256]{1,0:T(8,128)(2,1)S(1)}, u32[]{:S(2)}, u32[]{:S(2)}) %collective-permute-start.16) | collective-permute-done | bytes 524320 | tf_op jit(solution)/shard_map/ppermute | solution.py:48
  107.2 4.6 %copy-done.1 = bf16[1536,4096]{1,0:T(8,128)(2,1)S(1)} copy-done((bf16[1536,4096]{1,0:T(8,128)(2,1)S(1)}, bf16[1536,4096]{1,0:T(8,128)(2,1)}, u32[]{:S(2)}) %copy-start.1) | copy-done | bytes 12582936
  111.8 6.2 %shard_map.41.refs_3_ = f32[1024,1536]{1,0:T(8,128)S(1)} custom-call(s32[6]{0:T(128)S(1)} %slice.41.blocks, bf16[1024,256]{1,0:T(8,128)(2,1)S(1)} %collective-permute-done.16.refs_0_, bf16[1024,256]{1,0:T(8,128)(2,1)S(1)} %collective-permute-done.26.refs_1_, bf16[1024,256]{1,0:T(8,128)(2,1)S(1)} %collective-permute-done.18.refs_2_, ...), custom_call_target="tpu_custom_call", output_to_operand_aliasing={{}: (8, {})} | custom-call | flops 4831838208 | bytes 7864320 | tf_op jit(solution)/shard_map/pallas_call | solution.py:212
  118.3 1.7 %collective-permute-done.29.refs_1_ = bf16[1024,256]{1,0:T(8,128)(2,1)S(1)} collective-permute-done((bf16[1024,256]{1,0:T(8,128)(2,1)S(1)}, bf16[1024,256]{1,0:T(8,128)(2,1)S(1)}, u32[]{:S(2)}, u32[]{:S(2)}) %collective-permute-start.29) | collective-permute-done | bytes 524320 | tf_op jit(solution)/shard_map/ppermute | solution.py:48
  120.0 2.4 %shard_map.42 = (f32[256,1536]{1,0:T(8,128)S(1)}, bf16[256,1536]{1,0:T(8,128)(2,1)S(1)}, f32[128,1536]{1,0:T(8,128)S(1)}, bf16[128,1536]{1,0:T(8,128)(2,1)S(1)},...) custom-call(s32[2]{0:T(128)S(1)} %slice.37.blocks, bf16[1024,256]{1,0:T(8,128)(2,1)S(1)} %collective-permute-done.25.refs_0_, ...), custom_call_target="tpu_custom_call" | custom-call | flops 1610612736 | bytes 2621440 | tf_op jit(solution)/shard_map/pallas_call | solution.py:212
  122.5 2.8 %collective-permute-start.30 = (bf16[256,1536]{1,0:T(8,128)(2,1)S(1)}, bf16[256,1536]{1,0:T(8,128)(2,1)S(1)}, u32[]{:S(2)}, u32[]{:S(2)}) collective-permute-start(bf16[256,1536]{1,0:T(8,128)(2,1)S(1)} %get-tuple-element.46), channel_id=1, source_target_pairs={{0,4},{1,5},{2,6},{3,7},{4,0},{5,1},{6,2},{7,3},{8,12},{9,13},{10,... | collective-permute-start | bytes 2359304 | tf_op jit(solution)/shard_map/ppermute | solution.py:48
  125.3 1.6 collective-permute-start.31
  126.8 1.7 %collective-permute-start.32 = (bf16[128,1536]{1,0:T(8,128)(2,1)S(1)}, bf16[128,1536]{1,0:T(8,128)(2,1)S(1)}, u32[]{:S(2)}, u32[]{:S(2)}) collective-permute-start(bf16[128,1536]{1,0:T(8,128)(2,1)S(1)} %get-tuple-element.49), channel_id=1, source_target_pairs={{0,3},{1,0},{2,1},{3,2},{4,7},{5,4},{6,5},{7,6},{8,11},{9,8},{10,9... | collective-permute-start | bytes 1179656 | tf_op jit(solution)/shard_map/ppermute | solution.py:48
  128.5 2.0 %collective-permute-start.33 = (bf16[128,1536]{1,0:T(8,128)(2,1)S(1)}, bf16[128,1536]{1,0:T(8,128)(2,1)S(1)}, u32[]{:S(2)}, u32[]{:S(2)}) collective-permute-start(bf16[128,1536]{1,0:T(8,128)(2,1)S(1)} %get-tuple-element.50), channel_id=1, source_target_pairs={{0,2},{1,3},{2,0},{3,1},{4,6},{5,7},{6,4},{7,5},{8,10},{9,11},{10,... | collective-permute-start | bytes 1179656 | tf_op jit(solution)/shard_map/ppermute | solution.py:48
  130.5 6.9 %collective-permute-done.31 = bf16[128,1536]{1,0:T(8,128)(2,1)S(1)} collective-permute-done((bf16[128,1536]{1,0:T(8,128)(2,1)S(1)}, bf16[128,1536]{1,0:T(8,128)(2,1)S(1)}, u32[]{:S(2)}, u32[]{:S(2)}) %collective-permute-start.31) | collective-permute-done | bytes 393248 | tf_op jit(solution)/shard_map/ppermute | solution.py:48
  138.9 8.1 %collective-permute-done.33 = bf16[128,1536]{1,0:T(8,128)(2,1)S(1)} collective-permute-done((bf16[128,1536]{1,0:T(8,128)(2,1)S(1)}, bf16[128,1536]{1,0:T(8,128)(2,1)S(1)}, u32[]{:S(2)}, u32[]{:S(2)}) %collective-permute-start.33) | collective-permute-done | bytes 393248 | tf_op jit(solution)/shard_map/ppermute | solution.py:48
  149.6 2.1 %collective-permute-start.36 = (bf16[64,1536]{1,0:T(8,128)(2,1)S(1)}, bf16[64,1536]{1,0:T(8,128)(2,1)S(1)}, u32[]{:S(2)}, u32[]{:S(2)}) collective-permute-start(bf16[64,1536]{1,0:T(8,128)(2,1)S(1)} %get-tuple-element.63), channel_id=1, source_target_pairs={{0,2},{1,3},{2,0},{3,1},{4,6},{5,7},{6,4},{7,5},{8,10},{9,11},{10,... | collective-permute-start | bytes 589832 | tf_op jit(solution)/shard_map/ppermute | solution.py:48
  152.8 1.7 %collective-permute-done.37 = bf16[64,1536]{1,0:T(8,128)(2,1)S(1)} collective-permute-done((bf16[64,1536]{1,0:T(8,128)(2,1)S(1)}, bf16[64,1536]{1,0:T(8,128)(2,1)S(1)}, u32[]{:S(2)}, u32[]{:S(2)}) %collective-permute-start.37) | collective-permute-done | bytes 196640 | tf_op jit(solution)/shard_map/ppermute | solution.py:48
  154.6 2.8 %collective-permute-done.34 = bf16[64,1536]{1,0:T(8,128)(2,1)S(1)} collective-permute-done((bf16[64,1536]{1,0:T(8,128)(2,1)S(1)}, bf16[64,1536]{1,0:T(8,128)(2,1)S(1)}, u32[]{:S(2)}, u32[]{:S(2)}) %collective-permute-start.34) | collective-permute-done | bytes 196640 | tf_op jit(solution)/shard_map/ppermute | solution.py:48
  157.4 2.1 %collective-permute-done.36 = bf16[64,1536]{1,0:T(8,128)(2,1)S(1)} collective-permute-done((bf16[64,1536]{1,0:T(8,128)(2,1)S(1)}, bf16[64,1536]{1,0:T(8,128)(2,1)S(1)}, u32[]{:S(2)}, u32[]{:S(2)}) %collective-permute-start.36) | collective-permute-done | bytes 196640 | tf_op jit(solution)/shard_map/ppermute | solution.py:48
  (86 shorter events, 27.4 us)
Async XLA Ops:
  0.0 14.0 %collective-permute-start.1 = (bf16[64,4096]{1,0:T(8,128)(2,1)}, bf16[64,4096]{1,0:T(8,128)(2,1)S(1)}, u32[]{:S(2)}, u32[]{:S(2)}) collective-permute-start(bf16[64,4096]{1,0:T(8,128)(2,1)} %refs_0_), channel_id=1, source_target_pairs={{0,32},{8,104},{16,48},{24,120},{32,64},{40,8},{48,80},{56,24},{64... | collective-permute-start | bytes 1572872 | tf_op jit(solution)/shard_map/ppermute | solution.py:48
  2.0 14.3 %collective-permute-start = (bf16[64,4096]{1,0:T(8,128)(2,1)}, bf16[64,4096]{1,0:T(8,128)(2,1)S(1)}, u32[]{:S(2)}, u32[]{:S(2)}) collective-permute-start(bf16[64,4096]{1,0:T(8,128)(2,1)} %refs_0_), channel_id=1, source_target_pairs={{0,16},{8,24},{16,0},{24,8},{32,48},{40,56},{48,32},{56,40},{64,80... | collective-permute-start | bytes 1572872 | tf_op jit(solution)/shard_map/ppermute | solution.py:48
  3.5 21.7 %collective-permute-start.2 = (bf16[64,4096]{1,0:T(8,128)(2,1)}, bf16[64,4096]{1,0:T(8,128)(2,1)S(1)}, u32[]{:S(2)}, u32[]{:S(2)}) collective-permute-start(bf16[64,4096]{1,0:T(8,128)(2,1)} %refs_0_), channel_id=1, source_target_pairs={{0,96},{8,40},{16,112},{24,56},{32,0},{40,72},{48,16},{56,88},{64,... | collective-permute-start | bytes 1572872 | tf_op jit(solution)/shard_map/ppermute | solution.py:48
  8.7 46.5 %all-to-all-start = ((bf16[16,256,256]{2,1,0:T(8,128)(2,1)}), bf16[16,256,256]{2,1,0:T(8,128)(2,1)}, u32[]{:S(2)}, u32[]{:S(2)}) async-start(bf16[16,256,256]{2,1,0:T(8,128)(2,1)} %shard_map.37), calls=%async_computation | async-start | bytes 4194304 | tf_op jit(solution)/shard_map/all_to_all | solution.py:255
  25.2 4.0 %collective-permute-start.5 = (bf16[64,4096]{1,0:T(8,128)(2,1)S(1)}, bf16[64,4096]{1,0:T(8,128)(2,1)S(1)}, u32[]{:S(2)}, u32[]{:S(2)}) collective-permute-start(bf16[64,4096]{1,0:T(8,128)(2,1)S(1)} %copy-done.3), channel_id=1, source_target_pairs={{0,8},{8,0},{16,24},{24,16},{32,40},{40,32},{48,56},{56,48},{64,72... | collective-permute-start | bytes 1572872 | tf_op jit(solution)/shard_map/ppermute | solution.py:48
  25.2 5.5 %collective-permute-start.6 = (bf16[64,4096]{1,0:T(8,128)(2,1)S(1)}, bf16[64,4096]{1,0:T(8,128)(2,1)}, u32[]{:S(2)}, u32[]{:S(2)}) collective-permute-start(bf16[64,4096]{1,0:T(8,128)(2,1)S(1)} %collective-permute-done.refs_2_), channel_id=1, source_target_pairs={{0,8},{8,0},{16,24},{24,16},{32,40},{40,32},{48,56},{56,48},{64,72... | collective-permute-start | bytes 1572872 | tf_op jit(solution)/shard_map/ppermute | solution.py:48
  25.7 19.9 %collective-permute-start.3 = (bf16[64,4096]{1,0:T(8,128)(2,1)S(1)}, bf16[64,4096]{1,0:T(8,128)(2,1)S(1)}, u32[]{:S(2)}, u32[]{:S(2)}) collective-permute-start(bf16[64,4096]{1,0:T(8,128)(2,1)S(1)} %collective-permute-done.refs_2_), channel_id=1, source_target_pairs={{0,32},{8,104},{16,48},{24,120},{32,64},{40,8},{48,80},{56,24},{64... | collective-permute-start | bytes 1572872 | tf_op jit(solution)/shard_map/ppermute | solution.py:48
  25.7 25.6 %collective-permute-start.10 = (bf16[64,4096]{1,0:T(8,128)(2,1)S(1)}, bf16[64,4096]{1,0:T(8,128)(2,1)}, u32[]{:S(2)}, u32[]{:S(2)}) collective-permute-start(bf16[64,4096]{1,0:T(8,128)(2,1)S(1)} %collective-permute-done.1.refs_4_), channel_id=1, source_target_pairs={{0,32},{8,104},{16,48},{24,120},{32,64},{40,8},{48,80},{56,24},{64... | collective-permute-start | bytes 1572872 | tf_op jit(solution)/shard_map/ppermute | solution.py:48
  25.7 25.7 %collective-permute-start.7 = (bf16[64,4096]{1,0:T(8,128)(2,1)S(1)}, bf16[64,4096]{1,0:T(8,128)(2,1)}, u32[]{:S(2)}, u32[]{:S(2)}) collective-permute-start(bf16[64,4096]{1,0:T(8,128)(2,1)S(1)} %collective-permute-done.1.refs_4_), channel_id=1, source_target_pairs={{0,8},{8,0},{16,24},{24,16},{32,40},{40,32},{48,56},{56,48},{64,72... | collective-permute-start | bytes 1572872 | tf_op jit(solution)/shard_map/ppermute | solution.py:48
  29.2 23.4 %collective-permute-start.12 = (bf16[64,4096]{1,0:T(8,128)(2,1)S(1)}, bf16[64,4096]{1,0:T(8,128)(2,1)}, u32[]{:S(2)}, u32[]{:S(2)}) collective-permute-start(bf16[64,4096]{1,0:T(8,128)(2,1)S(1)} %collective-permute-done.2.refs_6_), channel_id=1, source_target_pairs={{0,16},{8,24},{16,0},{24,8},{32,48},{40,56},{48,32},{56,40},{64,80... | collective-permute-start | bytes 1572872 | tf_op jit(solution)/shard_map/ppermute | solution.py:48
  30.7 22.0 %collective-permute-start.8 = (bf16[64,4096]{1,0:T(8,128)(2,1)S(1)}, bf16[64,4096]{1,0:T(8,128)(2,1)S(1)}, u32[]{:S(2)}, u32[]{:S(2)}) collective-permute-start(bf16[64,4096]{1,0:T(8,128)(2,1)S(1)} %collective-permute-done.2.refs_6_), channel_id=1, source_target_pairs={{0,8},{8,0},{16,24},{24,16},{32,40},{40,32},{48,56},{56,48},{64,72... | collective-permute-start | bytes 1572872 | tf_op jit(solution)/shard_map/ppermute | solution.py:48
  45.6 7.9 %collective-permute-start.9 = (bf16[64,4096]{1,0:T(8,128)(2,1)S(1)}, bf16[64,4096]{1,0:T(8,128)(2,1)S(1)}, u32[]{:S(2)}, u32[]{:S(2)}) collective-permute-start(bf16[64,4096]{1,0:T(8,128)(2,1)S(1)} %collective-permute-done.3.refs_8_), channel_id=1, source_target_pairs={{0,8},{8,0},{16,24},{24,16},{32,40},{40,32},{48,56},{56,48},{64,72... | collective-permute-start | bytes 1572872 | tf_op jit(solution)/shard_map/ppermute | solution.py:48
  51.4 12.4 %collective-permute-start.4 = (bf16[64,4096]{1,0:T(8,128)(2,1)S(1)}, bf16[64,4096]{1,0:T(8,128)(2,1)}, u32[]{:S(2)}, u32[]{:S(2)}) collective-permute-start(bf16[64,4096]{1,0:T(8,128)(2,1)S(1)} %collective-permute-done.3.refs_8_), channel_id=1, source_target_pairs={{0,32},{8,104},{16,48},{24,120},{32,64},{40,8},{48,80},{56,24},{64... | collective-permute-start | bytes 1572872 | tf_op jit(solution)/shard_map/ppermute | solution.py:48
  51.4 3.1 %collective-permute-start.11 = (bf16[64,4096]{1,0:T(8,128)(2,1)}, bf16[64,4096]{1,0:T(8,128)(2,1)}, u32[]{:S(2)}, u32[]{:S(2)}) collective-permute-start(bf16[64,4096]{1,0:T(8,128)(2,1)} %collective-permute-done.10.refs_10_), channel_id=1, source_target_pairs={{0,8},{8,0},{16,24},{24,16},{32,40},{40,32},{48,56},{56,48},{64,72... | collective-permute-start | bytes 1572872 | tf_op jit(solution)/shard_map/ppermute | solution.py:48
  69.1 14.8 %collective-permute-start.19 = (bf16[1024,256]{1,0:T(8,128)(2,1)S(1)}, bf16[1024,256]{1,0:T(8,128)(2,1)S(1)}, u32[]{:S(2)}, u32[]{:S(2)}) collective-permute-start(bf16[1024,256]{1,0:T(8,128)(2,1)S(1)} %shard_map.39.refs_0_), channel_id=1, source_target_pairs={{0,96},{8,40},{16,112},{24,56},{32,0},{40,72},{48,16},{56,88},{64,... | collective-permute-start | bytes 1572872 | tf_op jit(solution)/shard_map/ppermute | solution.py:48
  71.6 13.0 %collective-permute-start.17 = (bf16[1024,256]{1,0:T(8,128)(2,1)S(1)}, bf16[1024,256]{1,0:T(8,128)(2,1)S(1)}, u32[]{:S(2)}, u32[]{:S(2)}) collective-permute-start(bf16[1024,256]{1,0:T(8,128)(2,1)S(1)} %shard_map.39.refs_0_), channel_id=1, source_target_pairs={{0,32},{8,104},{16,48},{24,120},{32,64},{40,8},{48,80},{56,24},{64... | collective-permute-start | bytes 1572872 | tf_op jit(solution)/shard_map/ppermute | solution.py:48
  71.6 14.5 %collective-permute-start.15 = (bf16[1024,256]{1,0:T(8,128)(2,1)S(1)}, bf16[1024,256]{1,0:T(8,128)(2,1)S(1)}, u32[]{:S(2)}, u32[]{:S(2)}) collective-permute-start(bf16[1024,256]{1,0:T(8,128)(2,1)S(1)} %shard_map.39.refs_0_), channel_id=1, source_target_pairs={{0,16},{8,24},{16,0},{24,8},{32,48},{40,56},{48,32},{56,40},{64,80... | collective-permute-start | bytes 1572872 | tf_op jit(solution)/shard_map/ppermute | solution.py:48
  73.0 14.8 %collective-permute-start.21 = (bf16[1024,256]{1,0:T(8,128)(2,1)S(1)}, bf16[1024,256]{1,0:T(8,128)(2,1)S(1)}, u32[]{:S(2)}, u32[]{:S(2)}) collective-permute-start(bf16[1024,256]{1,0:T(8,128)(2,1)S(1)} %shard_map.39.refs_0_), channel_id=1, source_target_pairs={{0,8},{8,0},{16,24},{24,16},{32,40},{40,32},{48,56},{56,48},{64,72... | collective-permute-start | bytes 1572872 | tf_op jit(solution)/shard_map/ppermute | solution.py:48
  83.8 4.0 %collective-permute-start.24 = (bf16[1024,256]{1,0:T(8,128)(2,1)S(1)}, bf16[1024,256]{1,0:T(8,128)(2,1)S(1)}, u32[]{:S(2)}, u32[]{:S(2)}) collective-permute-start(bf16[1024,256]{1,0:T(8,128)(2,1)S(1)} %collective-permute-done.19.refs_6_), channel_id=1, source_target_pairs={{0,8},{8,0},{16,24},{24,16},{32,40},{40,32},{48,56},{56,48},{64,72... | collective-permute-start | bytes 1572872 | tf_op jit(solution)/shard_map/ppermute | solution.py:48
  84.6 3.9 %collective-permute-start.23 = (bf16[1024,256]{1,0:T(8,128)(2,1)S(1)}, bf16[1024,256]{1,0:T(8,128)(2,1)}, u32[]{:S(2)}, u32[]{:S(2)}) collective-permute-start(bf16[1024,256]{1,0:T(8,128)(2,1)S(1)} %collective-permute-done.17.refs_4_), channel_id=1, source_target_pairs={{0,8},{8,0},{16,24},{24,16},{32,40},{40,32},{48,56},{56,48},{64,72... | collective-permute-start | bytes 1572872 | tf_op jit(solution)/shard_map/ppermute | solution.py:48
  86.2 15.6 %collective-permute-start.20 = (bf16[1024,256]{1,0:T(8,128)(2,1)S(1)}, bf16[1024,256]{1,0:T(8,128)(2,1)S(1)}, u32[]{:S(2)}, u32[]{:S(2)}) collective-permute-start(bf16[1024,256]{1,0:T(8,128)(2,1)S(1)} %collective-permute-done.19.refs_6_), channel_id=1, source_target_pairs={{0,16},{8,24},{16,0},{24,8},{32,48},{40,56},{48,32},{56,40},{64,80... | collective-permute-start | bytes 1572872 | tf_op jit(solution)/shard_map/ppermute | solution.py:48
  87.8 14.0 %collective-permute-start.18 = (bf16[1024,256]{1,0:T(8,128)(2,1)S(1)}, bf16[1024,256]{1,0:T(8,128)(2,1)S(1)}, u32[]{:S(2)}, u32[]{:S(2)}) collective-permute-start(bf16[1024,256]{1,0:T(8,128)(2,1)S(1)} %collective-permute-done.17.refs_4_), channel_id=1, source_target_pairs={{0,32},{8,104},{16,48},{24,120},{32,64},{40,8},{48,80},{56,24},{64... | collective-permute-start | bytes 1572872 | tf_op jit(solution)/shard_map/ppermute | solution.py:48
  87.8 16.0 %collective-permute-start.16 = (bf16[1024,256]{1,0:T(8,128)(2,1)S(1)}, bf16[1024,256]{1,0:T(8,128)(2,1)S(1)}, u32[]{:S(2)}, u32[]{:S(2)}) collective-permute-start(bf16[1024,256]{1,0:T(8,128)(2,1)S(1)} %collective-permute-done.15.refs_2_), channel_id=1, source_target_pairs={{0,32},{8,104},{16,48},{24,120},{32,64},{40,8},{48,80},{56,24},{64... | collective-permute-start | bytes 1572872 | tf_op jit(solution)/shard_map/ppermute | solution.py:48
  104.3 13.7 %collective-permute-start.25 = (bf16[1024,256]{1,0:T(8,128)(2,1)S(1)}, bf16[1024,256]{1,0:T(8,128)(2,1)S(1)}, u32[]{:S(2)}, u32[]{:S(2)}) collective-permute-start(bf16[1024,256]{1,0:T(8,128)(2,1)S(1)} %collective-permute-done.16.refs_0_), channel_id=1, source_target_pairs={{0,32},{8,104},{16,48},{24,120},{32,64},{40,8},{48,80},{56,24},{64... | collective-permute-start | bytes 1572872 | tf_op jit(solution)/shard_map/ppermute | solution.py:48
  122.5 24.6 %collective-permute-start.30 = (bf16[256,1536]{1,0:T(8,128)(2,1)S(1)}, bf16[256,1536]{1,0:T(8,128)(2,1)S(1)}, u32[]{:S(2)}, u32[]{:S(2)}) collective-permute-start(bf16[256,1536]{1,0:T(8,128)(2,1)S(1)} %get-tuple-element.46), channel_id=1, source_target_pairs={{0,4},{1,5},{2,6},{3,7},{4,0},{5,1},{6,2},{7,3},{8,12},{9,13},{10,... | collective-permute-start | bytes 2359304 | tf_op jit(solution)/shard_map/ppermute | solution.py:48
  125.3 12.1 %collective-permute-start.31 = (bf16[128,1536]{1,0:T(8,128)(2,1)S(1)}, bf16[128,1536]{1,0:T(8,128)(2,1)S(1)}, u32[]{:S(2)}, u32[]{:S(2)}) collective-permute-start(bf16[128,1536]{1,0:T(8,128)(2,1)S(1)} %get-tuple-element.48), channel_id=1, source_target_pairs={{0,1},{1,2},{2,3},{3,0},{4,5},{5,6},{6,7},{7,4},{8,9},{9,10},{10,1... | collective-permute-start | bytes 1179656 | tf_op jit(solution)/shard_map/ppermute | solution.py:48
  126.8 12.0 %collective-permute-start.32 = (bf16[128,1536]{1,0:T(8,128)(2,1)S(1)}, bf16[128,1536]{1,0:T(8,128)(2,1)S(1)}, u32[]{:S(2)}, u32[]{:S(2)}) collective-permute-start(bf16[128,1536]{1,0:T(8,128)(2,1)S(1)} %get-tuple-element.49), channel_id=1, source_target_pairs={{0,3},{1,0},{2,1},{3,2},{4,7},{5,4},{6,5},{7,6},{8,11},{9,8},{10,9... | collective-permute-start | bytes 1179656 | tf_op jit(solution)/shard_map/ppermute | solution.py:48
  128.5 18.5 %collective-permute-start.33 = (bf16[128,1536]{1,0:T(8,128)(2,1)S(1)}, bf16[128,1536]{1,0:T(8,128)(2,1)S(1)}, u32[]{:S(2)}, u32[]{:S(2)}) collective-permute-start(bf16[128,1536]{1,0:T(8,128)(2,1)S(1)} %get-tuple-element.50), channel_id=1, source_target_pairs={{0,2},{1,3},{2,0},{3,1},{4,6},{5,7},{6,4},{7,5},{8,10},{9,11},{10,... | collective-permute-start | bytes 1179656 | tf_op jit(solution)/shard_map/ppermute | solution.py:48
  147.2 7.4 %collective-permute-start.37 = (bf16[64,1536]{1,0:T(8,128)(2,1)S(1)}, bf16[64,1536]{1,0:T(8,128)(2,1)S(1)}, u32[]{:S(2)}, u32[]{:S(2)}) collective-permute-start(bf16[64,1536]{1,0:T(8,128)(2,1)S(1)} %slice.61), channel_id=1, source_target_pairs={{0,4},{1,5},{2,6},{3,7},{4,0},{5,1},{6,2},{7,3},{8,12},{9,13},{10,... | collective-permute-start | bytes 589832 | tf_op jit(solution)/shard_map/ppermute | solution.py:48
  148.4 9.0 %collective-permute-start.34 = (bf16[64,1536]{1,0:T(8,128)(2,1)S(1)}, bf16[64,1536]{1,0:T(8,128)(2,1)S(1)}, u32[]{:S(2)}, u32[]{:S(2)}) collective-permute-start(bf16[64,1536]{1,0:T(8,128)(2,1)S(1)} %get-tuple-element.62), channel_id=1, source_target_pairs={{0,1},{1,2},{2,3},{3,0},{4,5},{5,6},{6,7},{7,4},{8,9},{9,10},{10,1... | collective-permute-start | bytes 589832 | tf_op jit(solution)/shard_map/ppermute | solution.py:48
  149.6 9.9 %collective-permute-start.36 = (bf16[64,1536]{1,0:T(8,128)(2,1)S(1)}, bf16[64,1536]{1,0:T(8,128)(2,1)S(1)}, u32[]{:S(2)}, u32[]{:S(2)}) collective-permute-start(bf16[64,1536]{1,0:T(8,128)(2,1)S(1)} %get-tuple-element.63), channel_id=1, source_target_pairs={{0,2},{1,3},{2,0},{3,1},{4,6},{5,7},{6,4},{7,5},{8,10},{9,11},{10,... | collective-permute-start | bytes 589832 | tf_op jit(solution)/shard_map/ppermute | solution.py:48
  151.7 8.3 %collective-permute-start.35 = (bf16[64,1536]{1,0:T(8,128)(2,1)S(1)}, bf16[64,1536]{1,0:T(8,128)(2,1)S(1)}, u32[]{:S(2)}, u32[]{:S(2)}) collective-permute-start(bf16[64,1536]{1,0:T(8,128)(2,1)S(1)} %get-tuple-element.64), channel_id=1, source_target_pairs={{0,3},{1,0},{2,1},{3,2},{4,7},{5,4},{6,5},{7,6},{8,11},{9,8},{10,9... | collective-permute-start | bytes 589832 | tf_op jit(solution)/shard_map/ppermute | solution.py:48
  (15 other events, 47.7 us)

commit v3 on v2

--- a/solution.py
+++ b/solution.py
@@ -37,7 +37,7 @@
 
 CHUNKS = 2
 STEP = 512
-SCOPED = 16 * 2**20
+SCOPED = 12 * 2**20
 ANY_SPEC = pl.BlockSpec(memory_space=pl.ANY)
 HBM_SPEC = pl.BlockSpec(memory_space=pltpu.HBM)
 VMEM_SPEC = pl.BlockSpec(memory_space=pltpu.VMEM)
@@ -133,7 +133,7 @@
         in_specs=[SMEM_SPEC] + [ANY_SPEC] * n + [HBM_SPEC],
         out_specs=[VMEM_SPEC] * 2,
         scratch_shapes=[pltpu.VMEM((n * tall, depth), jnp.bfloat16), pltpu.SemaphoreType.DMA((n + 1,))],
-        compiler_params=pltpu.CompilerParams(vmem_limit_bytes=48 * 2**20),
+        compiler_params=pltpu.CompilerParams(vmem_limit_bytes=52 * 2**20),
         cost_estimate=pl.CostEstimate(
             flops=2 * n * tall * depth * wide, bytes_accessed=(n * tall + wide) * depth * 2, transcendentals=0
         ),
@@ -157,70 +157,120 @@
         out_shape=jax.ShapeDtypeStruct(into.shape, into.dtype),
         in_specs=[SMEM_SPEC] + [VMEM_SPEC] * (n + 2),
         out_specs=VMEM_SPEC,
-        compiler_params=pltpu.CompilerParams(vmem_limit_bytes=SCOPED),
+        compiler_params=pltpu.CompilerParams(vmem_limit_bytes=24 * 2**20),
         cost_estimate=pl.CostEstimate(
             flops=2 * n * tall * depth * into.shape[1], bytes_accessed=2**22, transcendentals=0
         ),
     )(place, *pieces, weights, into)
 
 
-def score_kernel(n, adds, last, blocks, *refs):
-    pieces, docs = refs[:n], refs[n]
+def packed_rows(pieces, packed, sems):
     wide = pieces[0].shape[1]
-    if last:
-        outs = refs[n + 1 + adds :]
-        rows = jnp.concatenate([piece[...] for piece in pieces], axis=1)
-    else:
-        outs, (packed, sems) = refs[n + 1 + adds : -2], refs[-2:]
-        copies = [
-            pltpu.make_async_copy(piece, packed.at[:, pl.ds(i * wide, wide)], sems.at[i])
-            for i, piece in enumerate(pieces)
-        ]
-        for copy in copies:
-            copy.start()
-        for copy in copies:
-            copy.wait()
-        rows = packed[...]
+    copies = [
+        pltpu.make_async_copy(piece, packed.at[:, pl.ds(i * wide, wide)], sems.at[i])
+        for i, piece in enumerate(pieces)
+    ]
+    for copy in copies:
+        copy.start()
+    for copy in copies:
+        copy.wait()
+    return packed[...]
+
+
+def product(rows, columns):
+    return lax.dot_general(rows, columns, (((1,), (1,)), ((), ())), preferred_element_type=jnp.float32)
+
+
+def score_first_kernel(n, blocks, *refs):
+    pieces, (docs, out, rest, packed, sems) = refs[:n], refs[n:]
+    wide = pieces[0].shape[1]
+    rows = packed_rows(pieces, packed, sems)
     for j in range(docs.shape[0] // STEP):
         at = slice(j * STEP, (j + 1) * STEP)
-        held = jnp.concatenate(
-            [docs[at, pl.ds(pl.multiple_of(blocks[i] * wide, wide), wide)] for i in range(n)], axis=1
-        )
-        part = lax.dot_general(rows, held, (((1,), (1,)), ((), ())), preferred_element_type=jnp.float32)
-        if adds:
-            part += refs[n + 1][:, at]
-        start = 0
+        columns = [
+            docs[at, pl.ds(pl.multiple_of(blocks[i] * wide, wide), wide)] for i in range(docs.shape[1] // wide)
+        ]
+        out[:, at] = product(rows, jnp.concatenate(columns[:n], axis=1))
+        rest[at, :] = jnp.concatenate(columns[n:], axis=1)
+
+
+def score_first(blocks, pieces, docs):
+    rows, wide = pieces[0].shape
+    n_docs, depth = docs.shape
+    n = len(pieces)
+    return pl.pallas_call(
+        functools.partial(score_first_kernel, n),
+        out_shape=[
+            jax.ShapeDtypeStruct((rows, n_docs), jnp.float32),
+            jax.ShapeDtypeStruct((n_docs, depth - n * wide), docs.dtype),
+        ],
+        in_specs=[SMEM_SPEC] + [ANY_SPEC] * n + [VMEM_SPEC],
+        out_specs=[VMEM_SPEC] * 2,
+        scratch_shapes=[pltpu.VMEM((rows, n * wide), jnp.bfloat16), pltpu.SemaphoreType.DMA((n,))],
+        compiler_params=pltpu.CompilerParams(vmem_limit_bytes=SCOPED),
+        cost_estimate=pl.CostEstimate(
+            flops=2 * rows * n_docs * n * wide, bytes_accessed=(rows + n_docs) * n * wide * 2, transcendentals=0
+        ),
+    )(blocks, *pieces, docs)
+
+
+def score_next_kernel(n, start, *refs):
+    pieces, (columns, before, out, packed, sems) = refs[:n], refs[n:]
+    rows = packed_rows(pieces, packed, sems)
+    for j in range(columns.shape[0] // STEP):
+        at = slice(j * STEP, (j + 1) * STEP)
+        out[:, at] = before[:, at] + product(rows, columns[at, start : start + rows.shape[1]])
+
+
+def score_next(start, pieces, columns, before):
+    rows, wide = pieces[0].shape
+    n_docs = columns.shape[0]
+    n = len(pieces)
+    return pl.pallas_call(
+        functools.partial(score_next_kernel, n, start),
+        out_shape=jax.ShapeDtypeStruct((rows, n_docs), jnp.float32),
+        in_specs=[ANY_SPEC] * n + [VMEM_SPEC] * 2,
+        out_specs=VMEM_SPEC,
+        scratch_shapes=[pltpu.VMEM((rows, n * wide), jnp.bfloat16), pltpu.SemaphoreType.DMA((n,))],
+        input_output_aliases={n + 1: 0},
+        compiler_params=pltpu.CompilerParams(vmem_limit_bytes=SCOPED),
+        cost_estimate=pl.CostEstimate(
+            flops=2 * rows * n_docs * n * wide, bytes_accessed=(rows + n_docs) * n * wide * 2, transcendentals=0
+        ),
+    )(*pieces, columns, before)
+
+
+def score_last_kernel(n, start, *refs):
+    pieces, columns, before, outs = refs[:n], refs[n], refs[n + 1], refs[n + 2 :]
+    rows = jnp.concatenate([piece[...] for piece in pieces], axis=1)
+    for j in range(columns.shape[0] // STEP):
+        at = slice(j * STEP, (j + 1) * STEP)
+        part = before[:, at] + product(rows, columns[at, start:])
+        top = 0
         for out in outs:
-            out[:, at] = part[start : start + out.shape[0], :].astype(out.dtype)
-            start += out.shape[0]
-
-
-def score(blocks, pieces, docs, before=None, last=False):
+            out[:, at] = part[top : top + out.shape[0], :].astype(out.dtype)
+            top += out.shape[0]
+
+
+def score_last(start, pieces, columns, before):
     rows, wide = pieces[0].shape
-    n_docs = docs.shape[0]
-    n = len(pieces)
-    given = [] if before is None else [before]
-    if last:
-        tall = rows // CHUNKS
-        shapes = [
-            jax.ShapeDtypeStruct((tall // count, n_docs), jnp.bfloat16 if i else jnp.float32)
-            for count in (NH, NY)
-            for i in range(count)
-        ]
-    else:
-        shapes = [jax.ShapeDtypeStruct((rows, n_docs), jnp.float32)]
-    return pl.pallas_call(
-        functools.partial(score_kernel, n, len(given), last),
+    n_docs = columns.shape[0]
+    n = len(pieces)
+    shapes = [
+        jax.ShapeDtypeStruct((rows // CHUNKS // count, n_docs), jnp.bfloat16 if i else jnp.float32)
+        for count in (NH, NY)
+        for i in range(count)
+    ]
+    return pl.pallas_call(
+        functools.partial(score_last_kernel, n, start),
         out_shape=shapes,
-        in_specs=[SMEM_SPEC] + [VMEM_SPEC if last else ANY_SPEC] * n + [VMEM_SPEC] * (1 + len(given)),
+        in_specs=[VMEM_SPEC] * (n + 2),
         out_specs=[VMEM_SPEC] * len(shapes),
-        scratch_shapes=[] if last else [pltpu.VMEM((rows, n * wide), jnp.bfloat16), pltpu.SemaphoreType.DMA((n,))],
-        input_output_aliases={n + 2: 0} if given and not last else {},
         compiler_params=pltpu.CompilerParams(vmem_limit_bytes=SCOPED),
         cost_estimate=pl.CostEstimate(
-            flops=2 * rows * n_docs * n * wide, bytes_accessed=(rows + n_docs) * n * wide * 2, transcendentals=0
-        ),
-    )(blocks, *pieces, docs, *given)
+            flops=2 * rows * n_docs * n * wide, bytes_accessed=2**24, transcendentals=0
+        ),
+    )(*pieces, columns, before)
 
 
 def exchange_y(own, ahead, far, back):
@@ -259,16 +309,21 @@
     three, conditioned = lax.optimization_barrier((three, conditioned))
     conditioned = condition_rest(place[:, early:], with_core(three), weights, conditioned)
 
+    wide = conditioned.shape[1]
     one = first_stage(conditioned)
+    scores, columns = score_first(blocks, with_core(one[:1]), documents)
+    one, scores = lax.optimization_barrier((one, scores))
     two = second_stage(*one)
-    (scores,) = score(blocks[:half], with_core(one), documents)
-    two, scores = lax.optimization_barrier((two, scores))
+    scores = score_next(0, with_core(one[1:]), columns, scores)
+    two[0], scores = lax.optimization_barrier((two[0], scores))
     three = third_stage(*two)
-    (scores,) = score(blocks[half:early], with_core(two), documents, scores)
-    three, scores = lax.optimization_barrier((three, scores))
-    parts = score(blocks[early:], with_core(three), documents, scores, last=True)
-    first, second = lax.optimization_barrier((exchange_h(*parts[:NH]), exchange_y(*parts[NH:])))
-    first = added(exchange_y(*parts_of(added(first), NY)))
+    scores, *_ = lax.optimization_barrier((scores, three[0]))
+    scores = score_next((half - NC) * wide, with_core(two), columns, scores)
+    parts = score_last((early - NC) * wide, with_core(three), columns, scores)
+    first, second = exchange_h(*parts[:NH]), exchange_y(*parts[NH:])
+    second, first = lax.optimization_barrier((second, first))
+    first = parts_of(added(first), NY)
+    first = added(exchange_y(*first))
     second = added(exchange_h(*parts_of(added(second), NH)))
     totals = [total.reshape(NC, rows // CHUNKS, -1) for total in (first, second)]
     scores = jnp.concatenate(totals, axis=1).reshape(NC * rows, -1)

time: 162 us -> 155 us (0.957)
  local copies, waits for them, and re-layouts: 15.2 us -> 7.03 us
  waiting for transfers between devices: 76.6 us -> 83.4 us
  starting transfers between devices: 39 us -> 34.3 us
    unnamed x16 -> x14, local copies, waits for them, and re-layouts: 14.5 us -> 6.48 us
    ppermute x38, waiting for transfers between devices: 76.6 us -> 83.4 us  [move(): return lax.ppermute(piece, axis, perm)]
    ppermute x38, starting transfers between devices: 34.4 us -> 29.7 us  [move(): return lax.ppermute(piece, axis, perm)]
    pallas_call x3 -> x4, Pallas kernels: 17.4 us -> 16.5 us  [the longest x2 10.8 us: score_next(): pl.pallas_call(functools.partial(score_next_kernel, n, start), out_shape=...]
  transfers between devices with their start and end apart: 39 -> 39, of which waited for: 23 -> 22; matrix products, arithmetic and copies ran while one was open for 1% -> 1% of each run, Pallas kernels for 15% -> 16%
where the time goes in v3:
time: 155 us
  waiting for transfers between devices  83.4 us (54%)
  starting transfers between devices  34.3 us (22%)
  Pallas kernels  28 us (18%)
  local copies, waits for them, and re-layouts  7.03 us (5%)
  other arithmetic  1.55 us (1%)
    ppermute x38, waiting for transfers between devices, move(): return lax.ppermute(piece, axis, perm)  83.4 us
    ppermute x38, starting transfers between devices, move(): return lax.ppermute(piece, axis, perm)  29.7 us
    pallas_call x2, Pallas kernels, score_next(): pl.pallas_call(functools.partial(score_next_kernel, n, start), out_shape=...  10.8 us
    pallas_call x1, Pallas kernels, condition(): pl.pallas_call(functools.partial(condition_kernel, n), out_shape=[jax.Sha...  7.34 us
    unnamed x14, local copies, waits for them, and re-layouts  6.48 us
    all_to_all x1, starting transfers between devices, local(): lax.all_to_all(column_blocks(precond, CHIPS * NC), 'corpus', 0, 0, tiled=...  4.58 us
    pallas_call x1, Pallas kernels, score_first(): pl.pallas_call(functools.partial(score_first_kernel, n), out_shape=[jax.S...  3.9 us
  transfers between devices with their start and end apart: 39, of which 22 were waited for; matrix products, arithmetic and copies ran while one was open for 1% of the time, Pallas kernels for 16%

profile of v3, /device:TPU:0, one launch (start us, length us, event | category | flops | bytes accessed | tf_op | source)
XLA Modules:
  0.0 154.5 jit_solution(18061799920488501257)
XLA Ops:
  0.0 1.6 %collective-permute-start = (bf16[64,4096]{1,0:T(8,128)(2,1)}, bf16[64,4096]{1,0:T(8,128)(2,1)S(1)}, u32[]{:S(2)}, u32[]{:S(2)}) collective-permute-start(bf16[64,4096]{1,0:T(8,128)(2,1)} %refs_0_), channel_id=1, source_target_pairs={{0,16},{8,24},{16,0},{24,8},{32,48},{40,56},{48,32},{56,40},{64,80... | collective-permute-start | bytes 1572872 | tf_op jit(solution)/shard_map/ppermute | solution.py:48
  1.6 1.9 %collective-permute-start.1 = (bf16[64,4096]{1,0:T(8,128)(2,1)}, bf16[64,4096]{1,0:T(8,128)(2,1)S(1)}, u32[]{:S(2)}, u32[]{:S(2)}) collective-permute-start(bf16[64,4096]{1,0:T(8,128)(2,1)} %refs_0_), channel_id=1, source_target_pairs={{0,32},{8,104},{16,48},{24,120},{32,64},{40,8},{48,80},{56,24},{64... | collective-permute-start | bytes 1572872 | tf_op jit(solution)/shard_map/ppermute | solution.py:48
  3.5 2.1 %collective-permute-start.2 = (bf16[64,4096]{1,0:T(8,128)(2,1)}, bf16[64,4096]{1,0:T(8,128)(2,1)S(1)}, u32[]{:S(2)}, u32[]{:S(2)}) collective-permute-start(bf16[64,4096]{1,0:T(8,128)(2,1)} %refs_0_), channel_id=1, source_target_pairs={{0,96},{8,40},{16,112},{24,56},{32,0},{40,72},{48,16},{56,88},{64,... | collective-permute-start | bytes 1572872 | tf_op jit(solution)/shard_map/ppermute | solution.py:48
  5.6 3.1 %shard_map.37 = bf16[16,256,256]{2,1,0:T(8,128)(2,1)} custom-call(bf16[1,256,4096]{2,1,0:T(8,128)(2,1)} %weights.1), custom_call_target="tpu_custom_call" | custom-call | tf_op jit(solution)/shard_map/pallas_call | solution.py:92
  8.7 4.6 %all-to-all-start = ((bf16[16,256,256]{2,1,0:T(8,128)(2,1)}), bf16[16,256,256]{2,1,0:T(8,128)(2,1)}, u32[]{:S(2)}, u32[]{:S(2)}) async-start(bf16[16,256,256]{2,1,0:T(8,128)(2,1)} %shard_map.37), calls=%async_computation | async-start | bytes 4194304 | tf_op jit(solution)/shard_map/all_to_all | solution.py:305
  13.7 3.3 %collective-permute-done.1.refs_4_ = bf16[64,4096]{1,0:T(8,128)(2,1)S(1)} collective-permute-done((bf16[64,4096]{1,0:T(8,128)(2,1)}, bf16[64,4096]{1,0:T(8,128)(2,1)S(1)}, u32[]{:S(2)}, u32[]{:S(2)}) %collective-permute-start.1) | collective-permute-done | bytes 524320 | tf_op jit(solution)/shard_map/ppermute | solution.py:48
  17.1 9.7 %collective-permute-done.2.refs_6_ = bf16[64,4096]{1,0:T(8,128)(2,1)S(1)} collective-permute-done((bf16[64,4096]{1,0:T(8,128)(2,1)}, bf16[64,4096]{1,0:T(8,128)(2,1)S(1)}, u32[]{:S(2)}, u32[]{:S(2)}) %collective-permute-start.2) | collective-permute-done | bytes 524320 | tf_op jit(solution)/shard_map/ppermute | solution.py:48
  27.6 19.2 %collective-permute-done.3.refs_8_ = bf16[64,4096]{1,0:T(8,128)(2,1)} collective-permute-done((bf16[64,4096]{1,0:T(8,128)(2,1)S(1)}, bf16[64,4096]{1,0:T(8,128)(2,1)}, u32[]{:S(2)}, u32[]{:S(2)}) %collective-permute-start.3) | collective-permute-done | bytes 524320 | tf_op jit(solution)/shard_map/ppermute | solution.py:48
  47.1 5.3 %collective-permute-done.10.refs_10_ = bf16[64,4096]{1,0:T(8,128)(2,1)S(1)} collective-permute-done((bf16[64,4096]{1,0:T(8,128)(2,1)S(1)}, bf16[64,4096]{1,0:T(8,128)(2,1)S(1)}, u32[]{:S(2)}, u32[]{:S(2)}) %collective-permute-start.10) | collective-permute-done | bytes 524320 | tf_op jit(solution)/shard_map/ppermute | solution.py:48
  57.1 7.3 %shard_map.38 = (bf16[1024,256]{1,0:T(8,128)(2,1)S(1)}, bf16[4096,256]{1,0:T(8,128)(2,1)}) custom-call(s32[2,14]{1,0:T(2,128)S(1)} %bitcast.37, bf16[64,4096]{1,0:T(8,128)(2,1)S(1)} %copy-done.2, bf16[64,4096]{1,0:T(8,128)(2,1)S(1)} %collective-permute-done.5.refs_1_, bf16[64,4096]{1,0:T(8,128)(2,1)} %copy-done.3, ...), custom_call_target="tpu_custom_call" | custom-call | flops 1879048192 | bytes 9437184 | tf_op jit(solution)/shard_map/pallas_call | solution.py:127
  66.5 1.6 %copy-done.1 = bf16[4096,256]{1,0:T(8,128)(2,1)S(1)} copy-done((bf16[4096,256]{1,0:T(8,128)(2,1)S(1)}, bf16[4096,256]{1,0:T(8,128)(2,1)}, u32[]{:S(2)}) %copy-start.1) | copy-done | bytes 2097176
  70.3 3.0 %collective-permute-start.17 = (bf16[1024,256]{1,0:T(8,128)(2,1)S(1)}, bf16[1024,256]{1,0:T(8,128)(2,1)S(1)}, u32[]{:S(2)}, u32[]{:S(2)}) collective-permute-start(bf16[1024,256]{1,0:T(8,128)(2,1)S(1)} %shard_map.39.refs_0_), channel_id=1, source_target_pairs={{0,96},{8,40},{16,112},{24,56},{32,0},{40,72},{48,16},{56,88},{64,... | collective-permute-start | bytes 1572872 | tf_op jit(solution)/shard_map/ppermute | solution.py:48
  73.5 4.6 %copy-done = bf16[1536,4096]{1,0:T(8,128)(2,1)S(1)} copy-done((bf16[1536,4096]{1,0:T(8,128)(2,1)S(1)}, bf16[1536,4096]{1,0:T(8,128)(2,1)}, u32[]{:S(2)}) %copy-start) | copy-done | bytes 12582936
  78.1 3.9 %shard_map.40 = (f32[1024,1536]{1,0:T(8,128)S(1)}, bf16[1536,3584]{1,0:T(8,128)(2,1)S(1)}) custom-call(s32[16]{0:T(128)S(1)} %multiply_add_fusion.blocks, bf16[1024,256]{1,0:T(8,128)(2,1)S(1)} %shard_map.39.refs_0_, bf16[1024,256]{1,0:T(8,128)(2,1)S(1)} %collective-permute-done.18.refs_1_, bf16[1536,4096]{1,0:T(8,128)(2,1)S(1)} %copy-done), custom_call_target="tpu_custom_call" | custom-call | flops 1610612736 | bytes 2621440 | tf_op jit(solution)/shard_map/pallas_call | solution.py:201
  82.0 1.5 collective-permute-done.15.refs_0_
  83.5 1.7 %collective-permute-done.16.refs_2_ = bf16[1024,256]{1,0:T(8,128)(2,1)S(1)} collective-permute-done((bf16[1024,256]{1,0:T(8,128)(2,1)S(1)}, bf16[1024,256]{1,0:T(8,128)(2,1)S(1)}, u32[]{:S(2)}, u32[]{:S(2)}) %collective-permute-start.16) | collective-permute-done | bytes 524320 | tf_op jit(solution)/shard_map/ppermute | solution.py:48
  87.4 1.5 collective-permute-start.28
  88.9 5.4 %shard_map.41.refs_7_ = f32[1024,1536]{1,0:T(8,128)S(1)} custom-call(bf16[1024,256]{1,0:T(8,128)(2,1)S(1)} %collective-permute-done.15.refs_0_, bf16[1024,256]{1,0:T(8,128)(2,1)S(1)} %collective-permute-done.20.refs_1_, bf16[1024,256]{1,0:T(8,128)(2,1)S(1)} %collective-permute-done.16.refs_2_, ...), custom_call_target="tpu_custom_call", output_to_operand_aliasing={{}: (7, {})} | custom-call | flops 4831838208 | bytes 7864320 | tf_op jit(solution)/shard_map/pallas_call | solution.py:229
  94.4 2.5 %collective-permute-done.19.refs_0_ = bf16[1024,256]{1,0:T(8,128)(2,1)S(1)} collective-permute-done((bf16[1024,256]{1,0:T(8,128)(2,1)S(1)}, bf16[1024,256]{1,0:T(8,128)(2,1)S(1)}, u32[]{:S(2)}, u32[]{:S(2)}) %collective-permute-start.19) | collective-permute-done | bytes 524320 | tf_op jit(solution)/shard_map/ppermute | solution.py:48
  97.2 5.2 %collective-permute-done.26.refs_2_ = bf16[1024,256]{1,0:T(8,128)(2,1)S(1)} collective-permute-done((bf16[1024,256]{1,0:T(8,128)(2,1)S(1)}, bf16[1024,256]{1,0:T(8,128)(2,1)S(1)}, u32[]{:S(2)}, u32[]{:S(2)}) %collective-permute-start.26) | collective-permute-done | bytes 524320 | tf_op jit(solution)/shard_map/ppermute | solution.py:48
  102.9 5.1 %collective-permute-done.23.refs_0_ = bf16[1024,256]{1,0:T(8,128)(2,1)S(1)} collective-permute-done((bf16[1024,256]{1,0:T(8,128)(2,1)S(1)}, bf16[1024,256]{1,0:T(8,128)(2,1)S(1)}, u32[]{:S(2)}, u32[]{:S(2)}) %collective-permute-start.23) | collective-permute-done | bytes 524320 | tf_op jit(solution)/shard_map/ppermute | solution.py:48
  108.1 5.4 %shard_map.42.refs_3_ = f32[1024,1536]{1,0:T(8,128)S(1)} custom-call(bf16[1024,256]{1,0:T(8,128)(2,1)S(1)} %collective-permute-done.19.refs_0_, bf16[1024,256]{1,0:T(8,128)(2,1)S(1)} %collective-permute-done.25.refs_1_, bf16[1024,256]{1,0:T(8,128)(2,1)S(1)} %collective-permute-done.26.refs_2_, ...), custom_call_target="tpu_custom_call", output_to_operand_aliasing={{}: (7, {})} | custom-call | flops 4831838208 | bytes 7864320 | tf_op jit(solution)/shard_map/pallas_call | solution.py:229
  113.5 1.8 %shard_map.43 = (f32[256,1536]{1,0:T(8,128)S(1)}, bf16[256,1536]{1,0:T(8,128)(2,1)S(1)}, f32[128,1536]{1,0:T(8,128)S(1)}, bf16[128,1536]{1,0:T(8,128)(2,1)S(1)},...) custom-call(bf16[1024,256]{1,0:T(8,128)(2,1)S(1)} %collective-permute-done.23.refs_0_, ...), custom_call_target="tpu_custom_call" | custom-call | flops 1610612736 | bytes 16777216 | tf_op jit(solution)/shard_map/pallas_call | solution.py:264
  115.3 3.1 %collective-permute-start.33 = (bf16[256,1536]{1,0:T(8,128)(2,1)S(1)}, bf16[256,1536]{1,0:T(8,128)(2,1)S(1)}, u32[]{:S(2)}, u32[]{:S(2)}) collective-permute-start(bf16[256,1536]{1,0:T(8,128)(2,1)S(1)} %get-tuple-element.56), channel_id=1, source_target_pairs={{0,4},{1,5},{2,6},{3,7},{4,0},{5,1},{6,2},{7,3},{8,12},{9,13},{10,... | collective-permute-start | bytes 2359304 | tf_op jit(solution)/shard_map/ppermute | solution.py:48
  118.4 1.6 %collective-permute-start.30 = (bf16[128,1536]{1,0:T(8,128)(2,1)S(1)}, bf16[128,1536]{1,0:T(8,128)(2,1)S(1)}, u32[]{:S(2)}, u32[]{:S(2)}) collective-permute-start(bf16[128,1536]{1,0:T(8,128)(2,1)S(1)} %get-tuple-element.52), channel_id=1, source_target_pairs={{0,1},{1,2},{2,3},{3,0},{4,5},{5,6},{6,7},{7,4},{8,9},{9,10},{10,1... | collective-permute-start | bytes 1179656 | tf_op jit(solution)/shard_map/ppermute | solution.py:48
  120.0 1.7 %collective-permute-start.31 = (bf16[128,1536]{1,0:T(8,128)(2,1)S(1)}, bf16[128,1536]{1,0:T(8,128)(2,1)S(1)}, u32[]{:S(2)}, u32[]{:S(2)}) collective-permute-start(bf16[128,1536]{1,0:T(8,128)(2,1)S(1)} %get-tuple-element.53), channel_id=1, source_target_pairs={{0,3},{1,0},{2,1},{3,2},{4,7},{5,4},{6,5},{7,6},{8,11},{9,8},{10,9... | collective-permute-start | bytes 1179656 | tf_op jit(solution)/shard_map/ppermute | solution.py:48
  121.7 2.0 %collective-permute-start.32 = (bf16[128,1536]{1,0:T(8,128)(2,1)S(1)}, bf16[128,1536]{1,0:T(8,128)(2,1)S(1)}, u32[]{:S(2)}, u32[]{:S(2)}) collective-permute-start(bf16[128,1536]{1,0:T(8,128)(2,1)S(1)} %get-tuple-element.54), channel_id=1, source_target_pairs={{0,2},{1,3},{2,0},{3,1},{4,6},{5,7},{6,4},{7,5},{8,10},{9,11},{10,... | collective-permute-start | bytes 1179656 | tf_op jit(solution)/shard_map/ppermute | solution.py:48
  123.7 7.3 %collective-permute-done.30 = bf16[128,1536]{1,0:T(8,128)(2,1)S(1)} collective-permute-done((bf16[128,1536]{1,0:T(8,128)(2,1)S(1)}, bf16[128,1536]{1,0:T(8,128)(2,1)S(1)}, u32[]{:S(2)}, u32[]{:S(2)}) %collective-permute-start.30) | collective-permute-done | bytes 393248 | tf_op jit(solution)/shard_map/ppermute | solution.py:48
  132.0 8.6 %collective-permute-done.32 = bf16[128,1536]{1,0:T(8,128)(2,1)S(1)} collective-permute-done((bf16[128,1536]{1,0:T(8,128)(2,1)S(1)}, bf16[128,1536]{1,0:T(8,128)(2,1)S(1)}, u32[]{:S(2)}, u32[]{:S(2)}) %collective-permute-start.32) | collective-permute-done | bytes 393248 | tf_op jit(solution)/shard_map/ppermute | solution.py:48
  142.9 2.1 %collective-permute-start.35 = (bf16[64,1536]{1,0:T(8,128)(2,1)S(1)}, bf16[64,1536]{1,0:T(8,128)(2,1)S(1)}, u32[]{:S(2)}, u32[]{:S(2)}) collective-permute-start(bf16[64,1536]{1,0:T(8,128)(2,1)S(1)} %get-tuple-element.70), channel_id=1, source_target_pairs={{0,3},{1,0},{2,1},{3,2},{4,7},{5,4},{6,5},{7,6},{8,11},{9,8},{10,9... | collective-permute-start | bytes 589832 | tf_op jit(solution)/shard_map/ppermute | solution.py:48
  145.8 2.8 %collective-permute-done.37 = bf16[64,1536]{1,0:T(8,128)(2,1)S(1)} collective-permute-done((bf16[64,1536]{1,0:T(8,128)(2,1)S(1)}, bf16[64,1536]{1,0:T(8,128)(2,1)S(1)}, u32[]{:S(2)}, u32[]{:S(2)}) %collective-permute-start.37) | collective-permute-done | bytes 196640 | tf_op jit(solution)/shard_map/ppermute | solution.py:48
  150.1 2.3 %collective-permute-done.35 = bf16[64,1536]{1,0:T(8,128)(2,1)S(1)} collective-permute-done((bf16[64,1536]{1,0:T(8,128)(2,1)S(1)}, bf16[64,1536]{1,0:T(8,128)(2,1)S(1)}, u32[]{:S(2)}, u32[]{:S(2)}) %collective-permute-start.35) | collective-permute-done | bytes 196640 | tf_op jit(solution)/shard_map/ppermute | solution.py:48
  (83 shorter events, 21.6 us)
Async XLA Ops:
  0.0 13.7 %collective-permute-start = (bf16[64,4096]{1,0:T(8,128)(2,1)}, bf16[64,4096]{1,0:T(8,128)(2,1)S(1)}, u32[]{:S(2)}, u32[]{:S(2)}) collective-permute-start(bf16[64,4096]{1,0:T(8,128)(2,1)} %refs_0_), channel_id=1, source_target_pairs={{0,16},{8,24},{16,0},{24,8},{32,48},{40,56},{48,32},{56,40},{64,80... | collective-permute-start | bytes 1572872 | tf_op jit(solution)/shard_map/ppermute | solution.py:48
  1.6 15.5 %collective-permute-start.1 = (bf16[64,4096]{1,0:T(8,128)(2,1)}, bf16[64,4096]{1,0:T(8,128)(2,1)S(1)}, u32[]{:S(2)}, u32[]{:S(2)}) collective-permute-start(bf16[64,4096]{1,0:T(8,128)(2,1)} %refs_0_), channel_id=1, source_target_pairs={{0,32},{8,104},{16,48},{24,120},{32,64},{40,8},{48,80},{56,24},{64... | collective-permute-start | bytes 1572872 | tf_op jit(solution)/shard_map/ppermute | solution.py:48
  3.5 23.3 %collective-permute-start.2 = (bf16[64,4096]{1,0:T(8,128)(2,1)}, bf16[64,4096]{1,0:T(8,128)(2,1)S(1)}, u32[]{:S(2)}, u32[]{:S(2)}) collective-permute-start(bf16[64,4096]{1,0:T(8,128)(2,1)} %refs_0_), channel_id=1, source_target_pairs={{0,96},{8,40},{16,112},{24,56},{32,0},{40,72},{48,16},{56,88},{64,... | collective-permute-start | bytes 1572872 | tf_op jit(solution)/shard_map/ppermute | solution.py:48
  8.7 48.4 %all-to-all-start = ((bf16[16,256,256]{2,1,0:T(8,128)(2,1)}), bf16[16,256,256]{2,1,0:T(8,128)(2,1)}, u32[]{:S(2)}, u32[]{:S(2)}) async-start(bf16[16,256,256]{2,1,0:T(8,128)(2,1)} %shard_map.37), calls=%async_computation | async-start | bytes 4194304 | tf_op jit(solution)/shard_map/all_to_all | solution.py:305
  26.8 20.1 %collective-permute-start.3 = (bf16[64,4096]{1,0:T(8,128)(2,1)S(1)}, bf16[64,4096]{1,0:T(8,128)(2,1)}, u32[]{:S(2)}, u32[]{:S(2)}) collective-permute-start(bf16[64,4096]{1,0:T(8,128)(2,1)S(1)} %collective-permute-done.refs_2_), channel_id=1, source_target_pairs={{0,32},{8,104},{16,48},{24,120},{32,64},{40,8},{48,80},{56,24},{64... | collective-permute-start | bytes 1572872 | tf_op jit(solution)/shard_map/ppermute | solution.py:48
  26.8 25.6 %collective-permute-start.10 = (bf16[64,4096]{1,0:T(8,128)(2,1)S(1)}, bf16[64,4096]{1,0:T(8,128)(2,1)S(1)}, u32[]{:S(2)}, u32[]{:S(2)}) collective-permute-start(bf16[64,4096]{1,0:T(8,128)(2,1)S(1)} %collective-permute-done.1.refs_4_), channel_id=1, source_target_pairs={{0,32},{8,104},{16,48},{24,120},{32,64},{40,8},{48,80},{56,24},{64... | collective-permute-start | bytes 1572872 | tf_op jit(solution)/shard_map/ppermute | solution.py:48
  26.8 25.6 %collective-permute-start.12 = (bf16[64,4096]{1,0:T(8,128)(2,1)S(1)}, bf16[64,4096]{1,0:T(8,128)(2,1)}, u32[]{:S(2)}, u32[]{:S(2)}) collective-permute-start(bf16[64,4096]{1,0:T(8,128)(2,1)S(1)} %collective-permute-done.2.refs_6_), channel_id=1, source_target_pairs={{0,16},{8,24},{16,0},{24,8},{32,48},{40,56},{48,32},{56,40},{64,80... | collective-permute-start | bytes 1572872 | tf_op jit(solution)/shard_map/ppermute | solution.py:48
  27.1 26.1 %collective-permute-start.6 = (bf16[64,4096]{1,0:T(8,128)(2,1)S(1)}, bf16[64,4096]{1,0:T(8,128)(2,1)}, u32[]{:S(2)}, u32[]{:S(2)}) collective-permute-start(bf16[64,4096]{1,0:T(8,128)(2,1)S(1)} %collective-permute-done.refs_2_), channel_id=1, source_target_pairs={{0,8},{8,0},{16,24},{24,16},{32,40},{40,32},{48,56},{56,48},{64,72... | collective-permute-start | bytes 1572872 | tf_op jit(solution)/shard_map/ppermute | solution.py:48
  27.1 26.1 %collective-permute-start.7 = (bf16[64,4096]{1,0:T(8,128)(2,1)S(1)}, bf16[64,4096]{1,0:T(8,128)(2,1)}, u32[]{:S(2)}, u32[]{:S(2)}) collective-permute-start(bf16[64,4096]{1,0:T(8,128)(2,1)S(1)} %collective-permute-done.1.refs_4_), channel_id=1, source_target_pairs={{0,8},{8,0},{16,24},{24,16},{32,40},{40,32},{48,56},{56,48},{64,72... | collective-permute-start | bytes 1572872 | tf_op jit(solution)/shard_map/ppermute | solution.py:48
  46.8 7.7 %collective-permute-start.8 = (bf16[64,4096]{1,0:T(8,128)(2,1)S(1)}, bf16[64,4096]{1,0:T(8,128)(2,1)}, u32[]{:S(2)}, u32[]{:S(2)}) collective-permute-start(bf16[64,4096]{1,0:T(8,128)(2,1)S(1)} %collective-permute-done.2.refs_6_), channel_id=1, source_target_pairs={{0,8},{8,0},{16,24},{24,16},{32,40},{40,32},{48,56},{56,48},{64,72... | collective-permute-start | bytes 1572872 | tf_op jit(solution)/shard_map/ppermute | solution.py:48
  53.2 11.3 %collective-permute-start.4 = (bf16[64,4096]{1,0:T(8,128)(2,1)}, bf16[64,4096]{1,0:T(8,128)(2,1)S(1)}, u32[]{:S(2)}, u32[]{:S(2)}) collective-permute-start(bf16[64,4096]{1,0:T(8,128)(2,1)} %collective-permute-done.3.refs_8_), channel_id=1, source_target_pairs={{0,32},{8,104},{16,48},{24,120},{32,64},{40,8},{48,80},{56,24},{64... | collective-permute-start | bytes 1572872 | tf_op jit(solution)/shard_map/ppermute | solution.py:48
  53.2 3.2 %collective-permute-start.11 = (bf16[64,4096]{1,0:T(8,128)(2,1)}, bf16[64,4096]{1,0:T(8,128)(2,1)}, u32[]{:S(2)}, u32[]{:S(2)}) collective-permute-start(bf16[64,4096]{1,0:T(8,128)(2,1)} %copy-done.6), channel_id=1, source_target_pairs={{0,8},{8,0},{16,24},{24,16},{32,40},{40,32},{48,56},{56,48},{64,72... | collective-permute-start | bytes 1572872 | tf_op jit(solution)/shard_map/ppermute | solution.py:48
  69.1 4.4 %collective-permute-start.18 = (bf16[1024,256]{1,0:T(8,128)(2,1)S(1)}, bf16[1024,256]{1,0:T(8,128)(2,1)S(1)}, u32[]{:S(2)}, u32[]{:S(2)}) collective-permute-start(bf16[1024,256]{1,0:T(8,128)(2,1)S(1)} %shard_map.39.refs_0_), channel_id=1, source_target_pairs={{0,8},{8,0},{16,24},{24,16},{32,40},{40,32},{48,56},{56,48},{64,72... | collective-permute-start | bytes 1572872 | tf_op jit(solution)/shard_map/ppermute | solution.py:48
  69.5 14.0 %collective-permute-start.15 = (bf16[1024,256]{1,0:T(8,128)(2,1)S(1)}, bf16[1024,256]{1,0:T(8,128)(2,1)S(1)}, u32[]{:S(2)}, u32[]{:S(2)}) collective-permute-start(bf16[1024,256]{1,0:T(8,128)(2,1)S(1)} %shard_map.39.refs_0_), channel_id=1, source_target_pairs={{0,16},{8,24},{16,0},{24,8},{32,48},{40,56},{48,32},{56,40},{64,80... | collective-permute-start | bytes 1572872 | tf_op jit(solution)/shard_map/ppermute | solution.py:48
  70.1 15.1 %collective-permute-start.16 = (bf16[1024,256]{1,0:T(8,128)(2,1)S(1)}, bf16[1024,256]{1,0:T(8,128)(2,1)S(1)}, u32[]{:S(2)}, u32[]{:S(2)}) collective-permute-start(bf16[1024,256]{1,0:T(8,128)(2,1)S(1)} %shard_map.39.refs_0_), channel_id=1, source_target_pairs={{0,32},{8,104},{16,48},{24,120},{32,64},{40,8},{48,80},{56,24},{64... | collective-permute-start | bytes 1572872 | tf_op jit(solution)/shard_map/ppermute | solution.py:48
  70.3 14.9 %collective-permute-start.17 = (bf16[1024,256]{1,0:T(8,128)(2,1)S(1)}, bf16[1024,256]{1,0:T(8,128)(2,1)S(1)}, u32[]{:S(2)}, u32[]{:S(2)}) collective-permute-start(bf16[1024,256]{1,0:T(8,128)(2,1)S(1)} %shard_map.39.refs_0_), channel_id=1, source_target_pairs={{0,96},{8,40},{16,112},{24,56},{32,0},{40,72},{48,16},{56,88},{64,... | collective-permute-start | bytes 1572872 | tf_op jit(solution)/shard_map/ppermute | solution.py:48
  86.4 10.4 %collective-permute-start.19 = (bf16[1024,256]{1,0:T(8,128)(2,1)S(1)}, bf16[1024,256]{1,0:T(8,128)(2,1)S(1)}, u32[]{:S(2)}, u32[]{:S(2)}) collective-permute-start(bf16[1024,256]{1,0:T(8,128)(2,1)S(1)} %collective-permute-done.15.refs_0_), channel_id=1, source_target_pairs={{0,32},{8,104},{16,48},{24,120},{32,64},{40,8},{48,80},{56,24},{64... | collective-permute-start | bytes 1572872 | tf_op jit(solution)/shard_map/ppermute | solution.py:48
  86.4 16.0 %collective-permute-start.26 = (bf16[1024,256]{1,0:T(8,128)(2,1)S(1)}, bf16[1024,256]{1,0:T(8,128)(2,1)S(1)}, u32[]{:S(2)}, u32[]{:S(2)}) collective-permute-start(bf16[1024,256]{1,0:T(8,128)(2,1)S(1)} %collective-permute-done.16.refs_2_), channel_id=1, source_target_pairs={{0,32},{8,104},{16,48},{24,120},{32,64},{40,8},{48,80},{56,24},{64... | collective-permute-start | bytes 1572872 | tf_op jit(solution)/shard_map/ppermute | solution.py:48
  87.4 15.0 %collective-permute-start.28 = (bf16[1024,256]{1,0:T(8,128)(2,1)S(1)}, bf16[1024,256]{1,0:T(8,128)(2,1)S(1)}, u32[]{:S(2)}, u32[]{:S(2)}) collective-permute-start(bf16[1024,256]{1,0:T(8,128)(2,1)S(1)} %collective-permute-done.17.refs_4_), channel_id=1, source_target_pairs={{0,16},{8,24},{16,0},{24,8},{32,48},{40,56},{48,32},{56,40},{64,80... | collective-permute-start | bytes 1572872 | tf_op jit(solution)/shard_map/ppermute | solution.py:48
  96.8 11.2 %collective-permute-start.23 = (bf16[1024,256]{1,0:T(8,128)(2,1)S(1)}, bf16[1024,256]{1,0:T(8,128)(2,1)S(1)}, u32[]{:S(2)}, u32[]{:S(2)}) collective-permute-start(bf16[1024,256]{1,0:T(8,128)(2,1)S(1)} %collective-permute-done.19.refs_0_), channel_id=1, source_target_pairs={{0,32},{8,104},{16,48},{24,120},{32,64},{40,8},{48,80},{56,24},{64... | collective-permute-start | bytes 1572872 | tf_op jit(solution)/shard_map/ppermute | solution.py:48
  96.8 11.2 %collective-permute-start.25 = (bf16[1024,256]{1,0:T(8,128)(2,1)S(1)}, bf16[1024,256]{1,0:T(8,128)(2,1)S(1)}, u32[]{:S(2)}, u32[]{:S(2)}) collective-permute-start(bf16[1024,256]{1,0:T(8,128)(2,1)S(1)} %collective-permute-done.19.refs_0_), channel_id=1, source_target_pairs={{0,8},{8,0},{16,24},{24,16},{32,40},{40,32},{48,56},{56,48},{64,72... | collective-permute-start | bytes 1572872 | tf_op jit(solution)/shard_map/ppermute | solution.py:48
  102.4 5.6 %collective-permute-start.27 = (bf16[1024,256]{1,0:T(8,128)(2,1)S(1)}, bf16[1024,256]{1,0:T(8,128)(2,1)S(1)}, u32[]{:S(2)}, u32[]{:S(2)}) collective-permute-start(bf16[1024,256]{1,0:T(8,128)(2,1)S(1)} %collective-permute-done.26.refs_2_), channel_id=1, source_target_pairs={{0,8},{8,0},{16,24},{24,16},{32,40},{40,32},{48,56},{56,48},{64,72... | collective-permute-start | bytes 1572872 | tf_op jit(solution)/shard_map/ppermute | solution.py:48
  102.4 5.6 %collective-permute-start.29 = (bf16[1024,256]{1,0:T(8,128)(2,1)S(1)}, bf16[1024,256]{1,0:T(8,128)(2,1)S(1)}, u32[]{:S(2)}, u32[]{:S(2)}) collective-permute-start(bf16[1024,256]{1,0:T(8,128)(2,1)S(1)} %collective-permute-done.28.refs_4_), channel_id=1, source_target_pairs={{0,8},{8,0},{16,24},{24,16},{32,40},{40,32},{48,56},{56,48},{64,72... | collective-permute-start | bytes 1572872 | tf_op jit(solution)/shard_map/ppermute | solution.py:48
  108.0 5.4 %collective-permute-start.24 = (bf16[1024,256]{1,0:T(8,128)(2,1)S(1)}, bf16[1024,256]{1,0:T(8,128)(2,1)S(1)}, u32[]{:S(2)}, u32[]{:S(2)}) collective-permute-start(bf16[1024,256]{1,0:T(8,128)(2,1)S(1)} %collective-permute-done.23.refs_0_), channel_id=1, source_target_pairs={{0,8},{8,0},{16,24},{24,16},{32,40},{40,32},{48,56},{56,48},{64,72... | collective-permute-start | bytes 1572872 | tf_op jit(solution)/shard_map/ppermute | solution.py:48
  115.3 25.2 %collective-permute-start.33 = (bf16[256,1536]{1,0:T(8,128)(2,1)S(1)}, bf16[256,1536]{1,0:T(8,128)(2,1)S(1)}, u32[]{:S(2)}, u32[]{:S(2)}) collective-permute-start(bf16[256,1536]{1,0:T(8,128)(2,1)S(1)} %get-tuple-element.56), channel_id=1, source_target_pairs={{0,4},{1,5},{2,6},{3,7},{4,0},{5,1},{6,2},{7,3},{8,12},{9,13},{10,... | collective-permute-start | bytes 2359304 | tf_op jit(solution)/shard_map/ppermute | solution.py:48
  118.4 12.5 %collective-permute-start.30 = (bf16[128,1536]{1,0:T(8,128)(2,1)S(1)}, bf16[128,1536]{1,0:T(8,128)(2,1)S(1)}, u32[]{:S(2)}, u32[]{:S(2)}) collective-permute-start(bf16[128,1536]{1,0:T(8,128)(2,1)S(1)} %get-tuple-element.52), channel_id=1, source_target_pairs={{0,1},{1,2},{2,3},{3,0},{4,5},{5,6},{6,7},{7,4},{8,9},{9,10},{10,1... | collective-permute-start | bytes 1179656 | tf_op jit(solution)/shard_map/ppermute | solution.py:48
  120.0 12.0 %collective-permute-start.31 = (bf16[128,1536]{1,0:T(8,128)(2,1)S(1)}, bf16[128,1536]{1,0:T(8,128)(2,1)S(1)}, u32[]{:S(2)}, u32[]{:S(2)}) collective-permute-start(bf16[128,1536]{1,0:T(8,128)(2,1)S(1)} %get-tuple-element.53), channel_id=1, source_target_pairs={{0,3},{1,0},{2,1},{3,2},{4,7},{5,4},{6,5},{7,6},{8,11},{9,8},{10,9... | collective-permute-start | bytes 1179656 | tf_op jit(solution)/shard_map/ppermute | solution.py:48
  121.7 18.9 %collective-permute-start.32 = (bf16[128,1536]{1,0:T(8,128)(2,1)S(1)}, bf16[128,1536]{1,0:T(8,128)(2,1)S(1)}, u32[]{:S(2)}, u32[]{:S(2)}) collective-permute-start(bf16[128,1536]{1,0:T(8,128)(2,1)S(1)} %get-tuple-element.54), channel_id=1, source_target_pairs={{0,2},{1,3},{2,0},{3,1},{4,6},{5,7},{6,4},{7,5},{8,10},{9,11},{10,... | collective-permute-start | bytes 1179656 | tf_op jit(solution)/shard_map/ppermute | solution.py:48
  140.8 7.8 %collective-permute-start.37 = (bf16[64,1536]{1,0:T(8,128)(2,1)S(1)}, bf16[64,1536]{1,0:T(8,128)(2,1)S(1)}, u32[]{:S(2)}, u32[]{:S(2)}) collective-permute-start(bf16[64,1536]{1,0:T(8,128)(2,1)S(1)} %slice.49), channel_id=1, source_target_pairs={{0,4},{1,5},{2,6},{3,7},{4,0},{5,1},{6,2},{7,3},{8,12},{9,13},{10,... | collective-permute-start | bytes 589832 | tf_op jit(solution)/shard_map/ppermute | solution.py:48
  141.7 8.4 %collective-permute-start.34 = (bf16[64,1536]{1,0:T(8,128)(2,1)S(1)}, bf16[64,1536]{1,0:T(8,128)(2,1)S(1)}, u32[]{:S(2)}, u32[]{:S(2)}) collective-permute-start(bf16[64,1536]{1,0:T(8,128)(2,1)S(1)} %get-tuple-element.68), channel_id=1, source_target_pairs={{0,1},{1,2},{2,3},{3,0},{4,5},{5,6},{6,7},{7,4},{8,9},{9,10},{10,1... | collective-permute-start | bytes 589832 | tf_op jit(solution)/shard_map/ppermute | solution.py:48
  142.9 9.5 %collective-permute-start.35 = (bf16[64,1536]{1,0:T(8,128)(2,1)S(1)}, bf16[64,1536]{1,0:T(8,128)(2,1)S(1)}, u32[]{:S(2)}, u32[]{:S(2)}) collective-permute-start(bf16[64,1536]{1,0:T(8,128)(2,1)S(1)} %get-tuple-element.70), channel_id=1, source_target_pairs={{0,3},{1,0},{2,1},{3,2},{4,7},{5,4},{6,5},{7,6},{8,11},{9,8},{10,9... | collective-permute-start | bytes 589832 | tf_op jit(solution)/shard_map/ppermute | solution.py:48
  145.0 8.5 %collective-permute-start.36 = (bf16[64,1536]{1,0:T(8,128)(2,1)S(1)}, bf16[64,1536]{1,0:T(8,128)(2,1)S(1)}, u32[]{:S(2)}, u32[]{:S(2)}) collective-permute-start(bf16[64,1536]{1,0:T(8,128)(2,1)S(1)} %get-tuple-element.69), channel_id=1, source_target_pairs={{0,2},{1,3},{2,0},{3,1},{4,6},{5,7},{6,4},{7,5},{8,10},{9,11},{10,... | collective-permute-start | bytes 589832 | tf_op jit(solution)/shard_map/ppermute | solution.py:48
  (14 other events, 182.7 us)

commit v4 on v3

--- a/solution.py
+++ b/solution.py
@@ -240,35 +240,35 @@
     )(*pieces, columns, before)
 
 
-def score_last_kernel(n, start, *refs):
+def score_last_kernel(n, start, chunk, *refs):
     pieces, columns, before, outs = refs[:n], refs[n], refs[n + 1], refs[n + 2 :]
-    rows = jnp.concatenate([piece[...] for piece in pieces], axis=1)
+    tall = before.shape[0] // CHUNKS
+    mine = slice(chunk * tall, (chunk + 1) * tall)
+    rows = jnp.concatenate([piece[mine, :] for piece in pieces], axis=1)
     for j in range(columns.shape[0] // STEP):
         at = slice(j * STEP, (j + 1) * STEP)
-        part = before[:, at] + product(rows, columns[at, start:])
+        part = before[mine, at] + product(rows, columns[at, start:])
         top = 0
         for out in outs:
             out[:, at] = part[top : top + out.shape[0], :].astype(out.dtype)
             top += out.shape[0]
 
 
-def score_last(start, pieces, columns, before):
+def score_last(start, pieces, columns, before, chunk, heights):
     rows, wide = pieces[0].shape
     n_docs = columns.shape[0]
     n = len(pieces)
     shapes = [
-        jax.ShapeDtypeStruct((rows // CHUNKS // count, n_docs), jnp.bfloat16 if i else jnp.float32)
-        for count in (NH, NY)
-        for i in range(count)
+        jax.ShapeDtypeStruct((tall, n_docs), jnp.bfloat16 if i else jnp.float32) for i, tall in enumerate(heights)
     ]
     return pl.pallas_call(
-        functools.partial(score_last_kernel, n, start),
+        functools.partial(score_last_kernel, n, start, chunk),
         out_shape=shapes,
         in_specs=[VMEM_SPEC] * (n + 2),
         out_specs=[VMEM_SPEC] * len(shapes),
         compiler_params=pltpu.CompilerParams(vmem_limit_bytes=SCOPED),
         cost_estimate=pl.CostEstimate(
-            flops=2 * rows * n_docs * n * wide, bytes_accessed=2**24, transcendentals=0
+            flops=2 * rows // CHUNKS * n_docs * n * wide, bytes_accessed=2**23, transcendentals=0
         ),
     )(*pieces, columns, before)
 
@@ -312,19 +312,25 @@
     wide = conditioned.shape[1]
     one = first_stage(conditioned)
     scores, columns = score_first(blocks, with_core(one[:1]), documents)
-    one, scores = lax.optimization_barrier((one, scores))
+    one[1:3], scores = lax.optimization_barrier((one[1:3], scores))
     two = second_stage(*one)
     scores = score_next(0, with_core(one[1:]), columns, scores)
     two[0], scores = lax.optimization_barrier((two[0], scores))
     three = third_stage(*two)
     scores, *_ = lax.optimization_barrier((scores, three[0]))
     scores = score_next((half - NC) * wide, with_core(two), columns, scores)
-    parts = score_last((early - NC) * wide, with_core(three), columns, scores)
-    first, second = exchange_h(*parts[:NH]), exchange_y(*parts[NH:])
-    second, first = lax.optimization_barrier((second, first))
-    first = parts_of(added(first), NY)
-    first = added(exchange_y(*first))
-    second = added(exchange_h(*parts_of(added(second), NH)))
+    start, pieces = (early - NC) * wide, with_core(three)
+    tall = conditioned.shape[0] // CHUNKS
+    first = score_last(start, pieces, columns, scores, 0, [tall // NH] * NH)
+    scores, *_ = lax.optimization_barrier((scores, first[0]))
+    part, less = tall // NY, tall // GROUP
+    own, ahead, far, across, back = score_last(start, pieces, columns, scores, 1, [part, part, less, less, part])
+    go = functools.partial(move, axis="group")
+    near = [own, go(ahead, group_perm(0, 1)), go(back, group_perm(0, -1))]
+    distant = [go(far, group_perm(0, 2)), go(across, group_perm(1, 2))]
+    first, near = lax.optimization_barrier((exchange_h(*first), near))
+    first = added(exchange_y(*parts_of(added(first), NY)))
+    second = added(exchange_h(*parts_of(added(near), NH)) + distant)
     totals = [total.reshape(NC, rows // CHUNKS, -1) for total in (first, second)]
     scores = jnp.concatenate(totals, axis=1).reshape(NC * rows, -1)
     return scores / jnp.sqrt(jnp.float32(GROUP * feat))

time: 155 us -> 153 us (0.987)
  waiting for transfers between devices: 83.4 us -> 76.7 us
  starting transfers between devices: 34.3 us -> 39.4 us
    ppermute x38 -> x39, waiting for transfers between devices: 83.4 us -> 76.7 us  [move(): return lax.ppermute(piece, axis, perm)]
    ppermute x38 -> x39, starting transfers between devices: 29.7 us -> 34.9 us  [move(): return lax.ppermute(piece, axis, perm)]
  transfers between devices with their start and end apart: 39 -> 40, of which waited for: 22 -> 21; matrix products, arithmetic and copies ran while one was open for 1% -> 1% of each run, Pallas kernels for 16% -> 17%
where the time goes in v4:
time: 153 us
  waiting for transfers between devices  76.7 us (50%)
  starting transfers between devices  39.4 us (26%)
  Pallas kernels  28.2 us (18%)
  local copies, waits for them, and re-layouts  7.02 us (5%)
    ppermute x39, waiting for transfers between devices, move(): return lax.ppermute(piece, axis, perm)  76.7 us
    ppermute x39, starting transfers between devices, move(): return lax.ppermute(piece, axis, perm)  34.9 us
    pallas_call x2, Pallas kernels, score_next(): pl.pallas_call(functools.partial(score_next_kernel, n, start), out_shape=...  10.8 us
    pallas_call x1, Pallas kernels, condition(): pl.pallas_call(functools.partial(condition_kernel, n), out_shape=[jax.Sha...  7.37 us
    unnamed x14, local copies, waits for them, and re-layouts  6.47 us
    all_to_all x1, starting transfers between devices, local(): lax.all_to_all(column_blocks(precond, CHIPS * NC), 'corpus', 0, 0, tiled=...  4.59 us
    pallas_call x1, Pallas kernels, score_first(): pl.pallas_call(functools.partial(score_first_kernel, n), out_shape=[jax.S...  3.9 us
    pallas_call x1, Pallas kernels, column_blocks(): pl.pallas_call(blocks_kernel, out_shape=jax.ShapeDtypeStruct((count, rows...  3.12 us
  transfers between devices with their start and end apart: 40, of which 21 were waited for; matrix products, arithmetic and copies ran while one was open for 1% of the time, Pallas kernels for 17%

profile of v4, /device:TPU:0, one launch (start us, length us, event | category | flops | bytes accessed | tf_op | source)
XLA Modules:
  0.0 153.1 jit_solution(10059676423351911551)
XLA Ops:
  1.6 1.9 %collective-permute-start.1 = (bf16[64,4096]{1,0:T(8,128)(2,1)}, bf16[64,4096]{1,0:T(8,128)(2,1)S(1)}, u32[]{:S(2)}, u32[]{:S(2)}) collective-permute-start(bf16[64,4096]{1,0:T(8,128)(2,1)} %refs_0_), channel_id=1, source_target_pairs={{0,32},{8,104},{16,48},{24,120},{32,64},{40,8},{48,80},{56,24},{64... | collective-permute-start | bytes 1572872 | tf_op jit(solution)/shard_map/ppermute | solution.py:48
  3.5 2.1 %collective-permute-start.2 = (bf16[64,4096]{1,0:T(8,128)(2,1)}, bf16[64,4096]{1,0:T(8,128)(2,1)S(1)}, u32[]{:S(2)}, u32[]{:S(2)}) collective-permute-start(bf16[64,4096]{1,0:T(8,128)(2,1)} %refs_0_), channel_id=1, source_target_pairs={{0,96},{8,40},{16,112},{24,56},{32,0},{40,72},{48,16},{56,88},{64,... | collective-permute-start | bytes 1572872 | tf_op jit(solution)/shard_map/ppermute | solution.py:48
  5.6 3.1 %shard_map.37 = bf16[16,256,256]{2,1,0:T(8,128)(2,1)} custom-call(bf16[1,256,4096]{2,1,0:T(8,128)(2,1)} %weights.1), custom_call_target="tpu_custom_call" | custom-call | tf_op jit(solution)/shard_map/pallas_call | solution.py:92
  8.8 4.6 %all-to-all-start = ((bf16[16,256,256]{2,1,0:T(8,128)(2,1)}), bf16[16,256,256]{2,1,0:T(8,128)(2,1)}, u32[]{:S(2)}, u32[]{:S(2)}) async-start(bf16[16,256,256]{2,1,0:T(8,128)(2,1)} %shard_map.37), calls=%async_computation | async-start | bytes 4194304 | tf_op jit(solution)/shard_map/all_to_all | solution.py:305
  13.7 3.3 %collective-permute-done.1.refs_4_ = bf16[64,4096]{1,0:T(8,128)(2,1)S(1)} collective-permute-done((bf16[64,4096]{1,0:T(8,128)(2,1)}, bf16[64,4096]{1,0:T(8,128)(2,1)S(1)}, u32[]{:S(2)}, u32[]{:S(2)}) %collective-permute-start.1) | collective-permute-done | bytes 524320 | tf_op jit(solution)/shard_map/ppermute | solution.py:48
  17.1 9.7 %collective-permute-done.2.refs_6_ = bf16[64,4096]{1,0:T(8,128)(2,1)S(1)} collective-permute-done((bf16[64,4096]{1,0:T(8,128)(2,1)}, bf16[64,4096]{1,0:T(8,128)(2,1)S(1)}, u32[]{:S(2)}, u32[]{:S(2)}) %collective-permute-start.2) | collective-permute-done | bytes 524320 | tf_op jit(solution)/shard_map/ppermute | solution.py:48
  27.6 19.2 %collective-permute-done.3.refs_8_ = bf16[64,4096]{1,0:T(8,128)(2,1)} collective-permute-done((bf16[64,4096]{1,0:T(8,128)(2,1)S(1)}, bf16[64,4096]{1,0:T(8,128)(2,1)}, u32[]{:S(2)}, u32[]{:S(2)}) %collective-permute-start.3) | collective-permute-done | bytes 524320 | tf_op jit(solution)/shard_map/ppermute | solution.py:48
  47.1 5.3 %collective-permute-done.10.refs_10_ = bf16[64,4096]{1,0:T(8,128)(2,1)S(1)} collective-permute-done((bf16[64,4096]{1,0:T(8,128)(2,1)S(1)}, bf16[64,4096]{1,0:T(8,128)(2,1)S(1)}, u32[]{:S(2)}, u32[]{:S(2)}) %collective-permute-start.10) | collective-permute-done | bytes 524320 | tf_op jit(solution)/shard_map/ppermute | solution.py:48
  57.1 7.4 %shard_map.38 = (bf16[1024,256]{1,0:T(8,128)(2,1)S(1)}, bf16[4096,256]{1,0:T(8,128)(2,1)}) custom-call(s32[2,14]{1,0:T(2,128)S(1)} %bitcast.37, bf16[64,4096]{1,0:T(8,128)(2,1)S(1)} %copy-done.2, bf16[64,4096]{1,0:T(8,128)(2,1)S(1)} %collective-permute-done.5.refs_1_, bf16[64,4096]{1,0:T(8,128)(2,1)} %copy-done.3, ...), custom_call_target="tpu_custom_call" | custom-call | flops 1879048192 | bytes 9437184 | tf_op jit(solution)/shard_map/pallas_call | solution.py:127
  70.3 3.0 %collective-permute-start.21 = (bf16[1024,256]{1,0:T(8,128)(2,1)S(1)}, bf16[1024,256]{1,0:T(8,128)(2,1)S(1)}, u32[]{:S(2)}, u32[]{:S(2)}) collective-permute-start(bf16[1024,256]{1,0:T(8,128)(2,1)S(1)} %shard_map.39.refs_0_), channel_id=1, source_target_pairs={{0,96},{8,40},{16,112},{24,56},{32,0},{40,72},{48,16},{56,88},{64,... | collective-permute-start | bytes 1572872 | tf_op jit(solution)/shard_map/ppermute | solution.py:48
  73.6 4.6 %copy-done = bf16[1536,4096]{1,0:T(8,128)(2,1)S(1)} copy-done((bf16[1536,4096]{1,0:T(8,128)(2,1)S(1)}, bf16[1536,4096]{1,0:T(8,128)(2,1)}, u32[]{:S(2)}) %copy-start) | copy-done | bytes 12582936
  78.1 3.9 %shard_map.40 = (f32[1024,1536]{1,0:T(8,128)S(1)}, bf16[1536,3584]{1,0:T(8,128)(2,1)S(1)}) custom-call(s32[16]{0:T(128)S(1)} %multiply_add_fusion.blocks, bf16[1024,256]{1,0:T(8,128)(2,1)S(1)} %shard_map.39.refs_0_, bf16[1024,256]{1,0:T(8,128)(2,1)S(1)} %collective-permute-done.17.refs_1_, bf16[1536,4096]{1,0:T(8,128)(2,1)S(1)} %copy-done), custom_call_target="tpu_custom_call" | custom-call | flops 1610612736 | bytes 2621440 | tf_op jit(solution)/shard_map/pallas_call | solution.py:201
  83.5 1.7 %collective-permute-done.16.refs_2_ = bf16[1024,256]{1,0:T(8,128)(2,1)S(1)} collective-permute-done((bf16[1024,256]{1,0:T(8,128)(2,1)S(1)}, bf16[1024,256]{1,0:T(8,128)(2,1)S(1)}, u32[]{:S(2)}, u32[]{:S(2)}) %collective-permute-start.16) | collective-permute-done | bytes 524320 | tf_op jit(solution)/shard_map/ppermute | solution.py:48
  88.6 5.4 %shard_map.41.refs_7_ = f32[1024,1536]{1,0:T(8,128)S(1)} custom-call(bf16[1024,256]{1,0:T(8,128)(2,1)S(1)} %collective-permute-done.15.refs_0_, bf16[1024,256]{1,0:T(8,128)(2,1)S(1)} %collective-permute-done.19.refs_1_, bf16[1024,256]{1,0:T(8,128)(2,1)S(1)} %collective-permute-done.16.refs_2_, ...), custom_call_target="tpu_custom_call", output_to_operand_aliasing={{}: (7, {})} | custom-call | flops 4831838208 | bytes 7864320 | tf_op jit(solution)/shard_map/pallas_call | solution.py:229
  94.0 2.3 %collective-permute-done.18.refs_0_ = bf16[1024,256]{1,0:T(8,128)(2,1)S(1)} collective-permute-done((bf16[1024,256]{1,0:T(8,128)(2,1)S(1)}, bf16[1024,256]{1,0:T(8,128)(2,1)S(1)}, u32[]{:S(2)}, u32[]{:S(2)}) %collective-permute-start.18) | collective-permute-done | bytes 524320 | tf_op jit(solution)/shard_map/ppermute | solution.py:48
  96.7 5.2 %collective-permute-done.26.refs_2_ = bf16[1024,256]{1,0:T(8,128)(2,1)S(1)} collective-permute-done((bf16[1024,256]{1,0:T(8,128)(2,1)S(1)}, bf16[1024,256]{1,0:T(8,128)(2,1)S(1)}, u32[]{:S(2)}, u32[]{:S(2)}) %collective-permute-start.26) | collective-permute-done | bytes 524320 | tf_op jit(solution)/shard_map/ppermute | solution.py:48
  102.4 5.1 %collective-permute-done.23.refs_0_ = bf16[1024,256]{1,0:T(8,128)(2,1)S(1)} collective-permute-done((bf16[1024,256]{1,0:T(8,128)(2,1)S(1)}, bf16[1024,256]{1,0:T(8,128)(2,1)S(1)}, u32[]{:S(2)}, u32[]{:S(2)}) %collective-permute-start.23) | collective-permute-done | bytes 524320 | tf_op jit(solution)/shard_map/ppermute | solution.py:48
  107.6 5.4 %shard_map.42.refs_3_ = f32[1024,1536]{1,0:T(8,128)S(1)} custom-call(bf16[1024,256]{1,0:T(8,128)(2,1)S(1)} %collective-permute-done.18.refs_0_, bf16[1024,256]{1,0:T(8,128)(2,1)S(1)} %collective-permute-done.25.refs_1_, bf16[1024,256]{1,0:T(8,128)(2,1)S(1)} %collective-permute-done.26.refs_2_, ...), custom_call_target="tpu_custom_call", output_to_operand_aliasing={{}: (7, {})} | custom-call | flops 4831838208 | bytes 7864320 | tf_op jit(solution)/shard_map/pallas_call | solution.py:229
  114.0 3.1 %collective-permute-start.30 = (bf16[256,1536]{1,0:T(8,128)(2,1)S(1)}, bf16[256,1536]{1,0:T(8,128)(2,1)S(1)}, u32[]{:S(2)}, u32[]{:S(2)}) collective-permute-start(bf16[256,1536]{1,0:T(8,128)(2,1)S(1)} %get-tuple-element.51), channel_id=1, source_target_pairs={{0,4},{1,5},{2,6},{3,7},{4,0},{5,1},{6,2},{7,3},{8,12},{9,13},{10,... | collective-permute-start | bytes 2359304 | tf_op jit(solution)/shard_map/ppermute | solution.py:48
  118.1 1.6 %collective-permute-start.31 = (bf16[128,1536]{1,0:T(8,128)(2,1)S(1)}, bf16[128,1536]{1,0:T(8,128)(2,1)S(1)}, u32[]{:S(2)}, u32[]{:S(2)}) collective-permute-start(bf16[128,1536]{1,0:T(8,128)(2,1)S(1)} %get-tuple-element.54), channel_id=1, source_target_pairs={{0,1},{1,2},{2,3},{3,0},{4,5},{5,6},{6,7},{7,4},{8,9},{9,10},{10,1... | collective-permute-start | bytes 1179656 | tf_op jit(solution)/shard_map/ppermute | solution.py:48
  119.8 1.7 %collective-permute-start.32 = (bf16[128,1536]{1,0:T(8,128)(2,1)S(1)}, bf16[128,1536]{1,0:T(8,128)(2,1)S(1)}, u32[]{:S(2)}, u32[]{:S(2)}) collective-permute-start(bf16[128,1536]{1,0:T(8,128)(2,1)S(1)} %get-tuple-element.55), channel_id=1, source_target_pairs={{0,3},{1,0},{2,1},{3,2},{4,7},{5,4},{6,5},{7,6},{8,11},{9,8},{10,9... | collective-permute-start | bytes 1179656 | tf_op jit(solution)/shard_map/ppermute | solution.py:48
  121.4 2.0 %collective-permute-start.37 = (bf16[64,1536]{1,0:T(8,128)(2,1)S(1)}, bf16[64,1536]{1,0:T(8,128)(2,1)S(1)}, u32[]{:S(2)}, u32[]{:S(2)}) collective-permute-start(bf16[64,1536]{1,0:T(8,128)(2,1)S(1)} %get-tuple-element.61), channel_id=1, source_target_pairs={{0,2},{1,3},{2,0},{3,1},{4,6},{5,7},{6,4},{7,5},{8,10},{9,11},{10,... | collective-permute-start | bytes 589832 | tf_op jit(solution)/shard_map/ppermute | solution.py:48
  124.9 5.8 %collective-permute-done.31 = bf16[128,1536]{1,0:T(8,128)(2,1)S(1)} collective-permute-done((bf16[128,1536]{1,0:T(8,128)(2,1)S(1)}, bf16[128,1536]{1,0:T(8,128)(2,1)S(1)}, u32[]{:S(2)}, u32[]{:S(2)}) %collective-permute-start.31) | collective-permute-done | bytes 393248 | tf_op jit(solution)/shard_map/ppermute | solution.py:48
  130.7 3.6 %collective-permute-done.32 = bf16[128,1536]{1,0:T(8,128)(2,1)S(1)} collective-permute-done((bf16[128,1536]{1,0:T(8,128)(2,1)S(1)}, bf16[128,1536]{1,0:T(8,128)(2,1)S(1)}, u32[]{:S(2)}, u32[]{:S(2)}) %collective-permute-start.32) | collective-permute-done | bytes 393248 | tf_op jit(solution)/shard_map/ppermute | solution.py:48
  134.3 1.6 %collective-permute-done.30 = bf16[256,1536]{1,0:T(8,128)(2,1)S(1)} collective-permute-done((bf16[256,1536]{1,0:T(8,128)(2,1)S(1)}, bf16[256,1536]{1,0:T(8,128)(2,1)S(1)}, u32[]{:S(2)}, u32[]{:S(2)}) %collective-permute-start.30) | collective-permute-done | bytes 786464 | tf_op jit(solution)/shard_map/ppermute | solution.py:48
  136.1 3.1 %collective-permute-start.36 = (bf16[64,1536]{1,0:T(8,128)(2,1)S(1)}, bf16[64,1536]{1,0:T(8,128)(2,1)S(1)}, u32[]{:S(2)}, u32[]{:S(2)}) collective-permute-start(bf16[64,1536]{1,0:T(8,128)(2,1)S(1)} %slice.53), channel_id=1, source_target_pairs={{0,4},{1,5},{2,6},{3,7},{4,0},{5,1},{6,2},{7,3},{8,12},{9,13},{10,... | collective-permute-start | bytes 589832 | tf_op jit(solution)/shard_map/ppermute | solution.py:48
  139.5 1.6 %collective-permute-start.33 = (bf16[64,1536]{1,0:T(8,128)(2,1)S(1)}, bf16[64,1536]{1,0:T(8,128)(2,1)S(1)}, u32[]{:S(2)}, u32[]{:S(2)}) collective-permute-start(bf16[64,1536]{1,0:T(8,128)(2,1)S(1)} %get-tuple-element.68), channel_id=1, source_target_pairs={{0,1},{1,2},{2,3},{3,0},{4,5},{5,6},{6,7},{7,4},{8,9},{9,10},{10,1... | collective-permute-start | bytes 589832 | tf_op jit(solution)/shard_map/ppermute | solution.py:48
  141.1 1.7 %collective-permute-start.34 = (bf16[64,1536]{1,0:T(8,128)(2,1)S(1)}, bf16[64,1536]{1,0:T(8,128)(2,1)S(1)}, u32[]{:S(2)}, u32[]{:S(2)}) collective-permute-start(bf16[64,1536]{1,0:T(8,128)(2,1)S(1)} %get-tuple-element.70), channel_id=1, source_target_pairs={{0,3},{1,0},{2,1},{3,2},{4,7},{5,4},{6,5},{7,6},{8,11},{9,8},{10,9... | collective-permute-start | bytes 589832 | tf_op jit(solution)/shard_map/ppermute | solution.py:48
  142.8 2.0 %collective-permute-start.35 = (bf16[64,1536]{1,0:T(8,128)(2,1)S(1)}, bf16[64,1536]{1,0:T(8,128)(2,1)S(1)}, u32[]{:S(2)}, u32[]{:S(2)}) collective-permute-start(bf16[64,1536]{1,0:T(8,128)(2,1)S(1)} %get-tuple-element.69), channel_id=1, source_target_pairs={{0,2},{1,3},{2,0},{3,1},{4,6},{5,7},{6,4},{7,5},{8,10},{9,11},{10,... | collective-permute-start | bytes 589832 | tf_op jit(solution)/shard_map/ppermute | solution.py:48
  144.9 2.6 %collective-permute-done.33 = bf16[64,1536]{1,0:T(8,128)(2,1)S(1)} collective-permute-done((bf16[64,1536]{1,0:T(8,128)(2,1)S(1)}, bf16[64,1536]{1,0:T(8,128)(2,1)S(1)}, u32[]{:S(2)}, u32[]{:S(2)}) %collective-permute-start.33) | collective-permute-done | bytes 196640 | tf_op jit(solution)/shard_map/ppermute | solution.py:48
  147.5 2.8 %collective-permute-done.34 = bf16[64,1536]{1,0:T(8,128)(2,1)S(1)} collective-permute-done((bf16[64,1536]{1,0:T(8,128)(2,1)S(1)}, bf16[64,1536]{1,0:T(8,128)(2,1)S(1)}, u32[]{:S(2)}, u32[]{:S(2)}) %collective-permute-start.34) | collective-permute-done | bytes 196640 | tf_op jit(solution)/shard_map/ppermute | solution.py:48
  150.3 1.8 %collective-permute-done.35 = bf16[64,1536]{1,0:T(8,128)(2,1)S(1)} collective-permute-done((bf16[64,1536]{1,0:T(8,128)(2,1)S(1)}, bf16[64,1536]{1,0:T(8,128)(2,1)S(1)}, u32[]{:S(2)}, u32[]{:S(2)}) %collective-permute-start.35) | collective-permute-done | bytes 196640 | tf_op jit(solution)/shard_map/ppermute | solution.py:48
  (86 shorter events, 24.7 us)
Async XLA Ops:
  0.0 13.7 %collective-permute-start = (bf16[64,4096]{1,0:T(8,128)(2,1)}, bf16[64,4096]{1,0:T(8,128)(2,1)S(1)}, u32[]{:S(2)}, u32[]{:S(2)}) collective-permute-start(bf16[64,4096]{1,0:T(8,128)(2,1)} %refs_0_), channel_id=1, source_target_pairs={{0,16},{8,24},{16,0},{24,8},{32,48},{40,56},{48,32},{56,40},{64,80... | collective-permute-start | bytes 1572872 | tf_op jit(solution)/shard_map/ppermute | solution.py:48
  1.6 15.5 %collective-permute-start.1 = (bf16[64,4096]{1,0:T(8,128)(2,1)}, bf16[64,4096]{1,0:T(8,128)(2,1)S(1)}, u32[]{:S(2)}, u32[]{:S(2)}) collective-permute-start(bf16[64,4096]{1,0:T(8,128)(2,1)} %refs_0_), channel_id=1, source_target_pairs={{0,32},{8,104},{16,48},{24,120},{32,64},{40,8},{48,80},{56,24},{64... | collective-permute-start | bytes 1572872 | tf_op jit(solution)/shard_map/ppermute | solution.py:48
  3.5 23.2 %collective-permute-start.2 = (bf16[64,4096]{1,0:T(8,128)(2,1)}, bf16[64,4096]{1,0:T(8,128)(2,1)S(1)}, u32[]{:S(2)}, u32[]{:S(2)}) collective-permute-start(bf16[64,4096]{1,0:T(8,128)(2,1)} %refs_0_), channel_id=1, source_target_pairs={{0,96},{8,40},{16,112},{24,56},{32,0},{40,72},{48,16},{56,88},{64,... | collective-permute-start | bytes 1572872 | tf_op jit(solution)/shard_map/ppermute | solution.py:48
  8.8 48.3 %all-to-all-start = ((bf16[16,256,256]{2,1,0:T(8,128)(2,1)}), bf16[16,256,256]{2,1,0:T(8,128)(2,1)}, u32[]{:S(2)}, u32[]{:S(2)}) async-start(bf16[16,256,256]{2,1,0:T(8,128)(2,1)} %shard_map.37), calls=%async_computation | async-start | bytes 4194304 | tf_op jit(solution)/shard_map/all_to_all | solution.py:305
  26.7 20.1 %collective-permute-start.3 = (bf16[64,4096]{1,0:T(8,128)(2,1)S(1)}, bf16[64,4096]{1,0:T(8,128)(2,1)}, u32[]{:S(2)}, u32[]{:S(2)}) collective-permute-start(bf16[64,4096]{1,0:T(8,128)(2,1)S(1)} %collective-permute-done.refs_2_), channel_id=1, source_target_pairs={{0,32},{8,104},{16,48},{24,120},{32,64},{40,8},{48,80},{56,24},{64... | collective-permute-start | bytes 1572872 | tf_op jit(solution)/shard_map/ppermute | solution.py:48
  26.7 25.6 %collective-permute-start.10 = (bf16[64,4096]{1,0:T(8,128)(2,1)S(1)}, bf16[64,4096]{1,0:T(8,128)(2,1)S(1)}, u32[]{:S(2)}, u32[]{:S(2)}) collective-permute-start(bf16[64,4096]{1,0:T(8,128)(2,1)S(1)} %collective-permute-done.1.refs_4_), channel_id=1, source_target_pairs={{0,32},{8,104},{16,48},{24,120},{32,64},{40,8},{48,80},{56,24},{64... | collective-permute-start | bytes 1572872 | tf_op jit(solution)/shard_map/ppermute | solution.py:48
  26.7 25.6 %collective-permute-start.12 = (bf16[64,4096]{1,0:T(8,128)(2,1)S(1)}, bf16[64,4096]{1,0:T(8,128)(2,1)}, u32[]{:S(2)}, u32[]{:S(2)}) collective-permute-start(bf16[64,4096]{1,0:T(8,128)(2,1)S(1)} %collective-permute-done.2.refs_6_), channel_id=1, source_target_pairs={{0,16},{8,24},{16,0},{24,8},{32,48},{40,56},{48,32},{56,40},{64,80... | collective-permute-start | bytes 1572872 | tf_op jit(solution)/shard_map/ppermute | solution.py:48
  27.1 26.1 %collective-permute-start.6 = (bf16[64,4096]{1,0:T(8,128)(2,1)S(1)}, bf16[64,4096]{1,0:T(8,128)(2,1)}, u32[]{:S(2)}, u32[]{:S(2)}) collective-permute-start(bf16[64,4096]{1,0:T(8,128)(2,1)S(1)} %collective-permute-done.refs_2_), channel_id=1, source_target_pairs={{0,8},{8,0},{16,24},{24,16},{32,40},{40,32},{48,56},{56,48},{64,72... | collective-permute-start | bytes 1572872 | tf_op jit(solution)/shard_map/ppermute | solution.py:48
  27.1 26.1 %collective-permute-start.7 = (bf16[64,4096]{1,0:T(8,128)(2,1)S(1)}, bf16[64,4096]{1,0:T(8,128)(2,1)}, u32[]{:S(2)}, u32[]{:S(2)}) collective-permute-start(bf16[64,4096]{1,0:T(8,128)(2,1)S(1)} %collective-permute-done.1.refs_4_), channel_id=1, source_target_pairs={{0,8},{8,0},{16,24},{24,16},{32,40},{40,32},{48,56},{56,48},{64,72... | collective-permute-start | bytes 1572872 | tf_op jit(solution)/shard_map/ppermute | solution.py:48
  46.8 7.7 %collective-permute-start.8 = (bf16[64,4096]{1,0:T(8,128)(2,1)S(1)}, bf16[64,4096]{1,0:T(8,128)(2,1)}, u32[]{:S(2)}, u32[]{:S(2)}) collective-permute-start(bf16[64,4096]{1,0:T(8,128)(2,1)S(1)} %collective-permute-done.2.refs_6_), channel_id=1, source_target_pairs={{0,8},{8,0},{16,24},{24,16},{32,40},{40,32},{48,56},{56,48},{64,72... | collective-permute-start | bytes 1572872 | tf_op jit(solution)/shard_map/ppermute | solution.py:48
  53.1 11.4 %collective-permute-start.4 = (bf16[64,4096]{1,0:T(8,128)(2,1)}, bf16[64,4096]{1,0:T(8,128)(2,1)S(1)}, u32[]{:S(2)}, u32[]{:S(2)}) collective-permute-start(bf16[64,4096]{1,0:T(8,128)(2,1)} %collective-permute-done.3.refs_8_), channel_id=1, source_target_pairs={{0,32},{8,104},{16,48},{24,120},{32,64},{40,8},{48,80},{56,24},{64... | collective-permute-start | bytes 1572872 | tf_op jit(solution)/shard_map/ppermute | solution.py:48
  69.1 4.4 %collective-permute-start.17 = (bf16[1024,256]{1,0:T(8,128)(2,1)S(1)}, bf16[1024,256]{1,0:T(8,128)(2,1)S(1)}, u32[]{:S(2)}, u32[]{:S(2)}) collective-permute-start(bf16[1024,256]{1,0:T(8,128)(2,1)S(1)} %shard_map.39.refs_0_), channel_id=1, source_target_pairs={{0,8},{8,0},{16,24},{24,16},{32,40},{40,32},{48,56},{56,48},{64,72... | collective-permute-start | bytes 1572872 | tf_op jit(solution)/shard_map/ppermute | solution.py:48
  69.5 14.0 %collective-permute-start.15 = (bf16[1024,256]{1,0:T(8,128)(2,1)S(1)}, bf16[1024,256]{1,0:T(8,128)(2,1)S(1)}, u32[]{:S(2)}, u32[]{:S(2)}) collective-permute-start(bf16[1024,256]{1,0:T(8,128)(2,1)S(1)} %shard_map.39.refs_0_), channel_id=1, source_target_pairs={{0,16},{8,24},{16,0},{24,8},{32,48},{40,56},{48,32},{56,40},{64,80... | collective-permute-start | bytes 1572872 | tf_op jit(solution)/shard_map/ppermute | solution.py:48
  70.1 15.1 %collective-permute-start.16 = (bf16[1024,256]{1,0:T(8,128)(2,1)S(1)}, bf16[1024,256]{1,0:T(8,128)(2,1)S(1)}, u32[]{:S(2)}, u32[]{:S(2)}) collective-permute-start(bf16[1024,256]{1,0:T(8,128)(2,1)S(1)} %shard_map.39.refs_0_), channel_id=1, source_target_pairs={{0,32},{8,104},{16,48},{24,120},{32,64},{40,8},{48,80},{56,24},{64... | collective-permute-start | bytes 1572872 | tf_op jit(solution)/shard_map/ppermute | solution.py:48
  70.3 15.4 %collective-permute-start.21 = (bf16[1024,256]{1,0:T(8,128)(2,1)S(1)}, bf16[1024,256]{1,0:T(8,128)(2,1)S(1)}, u32[]{:S(2)}, u32[]{:S(2)}) collective-permute-start(bf16[1024,256]{1,0:T(8,128)(2,1)S(1)} %shard_map.39.refs_0_), channel_id=1, source_target_pairs={{0,96},{8,40},{16,112},{24,56},{32,0},{40,72},{48,16},{56,88},{64,... | collective-permute-start | bytes 1572872 | tf_op jit(solution)/shard_map/ppermute | solution.py:48
  85.9 10.4 %collective-permute-start.18 = (bf16[1024,256]{1,0:T(8,128)(2,1)S(1)}, bf16[1024,256]{1,0:T(8,128)(2,1)S(1)}, u32[]{:S(2)}, u32[]{:S(2)}) collective-permute-start(bf16[1024,256]{1,0:T(8,128)(2,1)S(1)} %collective-permute-done.15.refs_0_), channel_id=1, source_target_pairs={{0,32},{8,104},{16,48},{24,120},{32,64},{40,8},{48,80},{56,24},{64... | collective-permute-start | bytes 1572872 | tf_op jit(solution)/shard_map/ppermute | solution.py:48
  85.9 16.0 %collective-permute-start.26 = (bf16[1024,256]{1,0:T(8,128)(2,1)S(1)}, bf16[1024,256]{1,0:T(8,128)(2,1)S(1)}, u32[]{:S(2)}, u32[]{:S(2)}) collective-permute-start(bf16[1024,256]{1,0:T(8,128)(2,1)S(1)} %collective-permute-done.16.refs_2_), channel_id=1, source_target_pairs={{0,32},{8,104},{16,48},{24,120},{32,64},{40,8},{48,80},{56,24},{64... | collective-permute-start | bytes 1572872 | tf_op jit(solution)/shard_map/ppermute | solution.py:48
  87.1 14.8 %collective-permute-start.28 = (bf16[1024,256]{1,0:T(8,128)(2,1)S(1)}, bf16[1024,256]{1,0:T(8,128)(2,1)S(1)}, u32[]{:S(2)}, u32[]{:S(2)}) collective-permute-start(bf16[1024,256]{1,0:T(8,128)(2,1)S(1)} %collective-permute-done.21.refs_4_), channel_id=1, source_target_pairs={{0,16},{8,24},{16,0},{24,8},{32,48},{40,56},{48,32},{56,40},{64,80... | collective-permute-start | bytes 1572872 | tf_op jit(solution)/shard_map/ppermute | solution.py:48
  96.3 11.2 %collective-permute-start.23 = (bf16[1024,256]{1,0:T(8,128)(2,1)S(1)}, bf16[1024,256]{1,0:T(8,128)(2,1)S(1)}, u32[]{:S(2)}, u32[]{:S(2)}) collective-permute-start(bf16[1024,256]{1,0:T(8,128)(2,1)S(1)} %collective-permute-done.18.refs_0_), channel_id=1, source_target_pairs={{0,32},{8,104},{16,48},{24,120},{32,64},{40,8},{48,80},{56,24},{64... | collective-permute-start | bytes 1572872 | tf_op jit(solution)/shard_map/ppermute | solution.py:48
  96.3 11.2 %collective-permute-start.25 = (bf16[1024,256]{1,0:T(8,128)(2,1)S(1)}, bf16[1024,256]{1,0:T(8,128)(2,1)S(1)}, u32[]{:S(2)}, u32[]{:S(2)}) collective-permute-start(bf16[1024,256]{1,0:T(8,128)(2,1)S(1)} %collective-permute-done.18.refs_0_), channel_id=1, source_target_pairs={{0,8},{8,0},{16,24},{24,16},{32,40},{40,32},{48,56},{56,48},{64,72... | collective-permute-start | bytes 1572872 | tf_op jit(solution)/shard_map/ppermute | solution.py:48
  101.9 5.6 %collective-permute-start.27 = (bf16[1024,256]{1,0:T(8,128)(2,1)S(1)}, bf16[1024,256]{1,0:T(8,128)(2,1)S(1)}, u32[]{:S(2)}, u32[]{:S(2)}) collective-permute-start(bf16[1024,256]{1,0:T(8,128)(2,1)S(1)} %collective-permute-done.26.refs_2_), channel_id=1, source_target_pairs={{0,8},{8,0},{16,24},{24,16},{32,40},{40,32},{48,56},{56,48},{64,72... | collective-permute-start | bytes 1572872 | tf_op jit(solution)/shard_map/ppermute | solution.py:48
  101.9 5.6 %collective-permute-start.29 = (bf16[1024,256]{1,0:T(8,128)(2,1)S(1)}, bf16[1024,256]{1,0:T(8,128)(2,1)S(1)}, u32[]{:S(2)}, u32[]{:S(2)}) collective-permute-start(bf16[1024,256]{1,0:T(8,128)(2,1)S(1)} %collective-permute-done.28.refs_4_), channel_id=1, source_target_pairs={{0,8},{8,0},{16,24},{24,16},{32,40},{40,32},{48,56},{56,48},{64,72... | collective-permute-start | bytes 1572872 | tf_op jit(solution)/shard_map/ppermute | solution.py:48
  107.5 5.4 %collective-permute-start.24 = (bf16[1024,256]{1,0:T(8,128)(2,1)S(1)}, bf16[1024,256]{1,0:T(8,128)(2,1)S(1)}, u32[]{:S(2)}, u32[]{:S(2)}) collective-permute-start(bf16[1024,256]{1,0:T(8,128)(2,1)S(1)} %collective-permute-done.23.refs_0_), channel_id=1, source_target_pairs={{0,8},{8,0},{16,24},{24,16},{32,40},{40,32},{48,56},{56,48},{64,72... | collective-permute-start | bytes 1572872 | tf_op jit(solution)/shard_map/ppermute | solution.py:48
  114.0 21.9 %collective-permute-start.30 = (bf16[256,1536]{1,0:T(8,128)(2,1)S(1)}, bf16[256,1536]{1,0:T(8,128)(2,1)S(1)}, u32[]{:S(2)}, u32[]{:S(2)}) collective-permute-start(bf16[256,1536]{1,0:T(8,128)(2,1)S(1)} %get-tuple-element.51), channel_id=1, source_target_pairs={{0,4},{1,5},{2,6},{3,7},{4,0},{5,1},{6,2},{7,3},{8,12},{9,13},{10,... | collective-permute-start | bytes 2359304 | tf_op jit(solution)/shard_map/ppermute | solution.py:48
  118.1 12.6 %collective-permute-start.31 = (bf16[128,1536]{1,0:T(8,128)(2,1)S(1)}, bf16[128,1536]{1,0:T(8,128)(2,1)S(1)}, u32[]{:S(2)}, u32[]{:S(2)}) collective-permute-start(bf16[128,1536]{1,0:T(8,128)(2,1)S(1)} %get-tuple-element.54), channel_id=1, source_target_pairs={{0,1},{1,2},{2,3},{3,0},{4,5},{5,6},{6,7},{7,4},{8,9},{9,10},{10,1... | collective-permute-start | bytes 1179656 | tf_op jit(solution)/shard_map/ppermute | solution.py:48
  119.8 14.5 %collective-permute-start.32 = (bf16[128,1536]{1,0:T(8,128)(2,1)S(1)}, bf16[128,1536]{1,0:T(8,128)(2,1)S(1)}, u32[]{:S(2)}, u32[]{:S(2)}) collective-permute-start(bf16[128,1536]{1,0:T(8,128)(2,1)S(1)} %get-tuple-element.55), channel_id=1, source_target_pairs={{0,3},{1,0},{2,1},{3,2},{4,7},{5,4},{6,5},{7,6},{8,11},{9,8},{10,9... | collective-permute-start | bytes 1179656 | tf_op jit(solution)/shard_map/ppermute | solution.py:48
  121.4 21.4 %collective-permute-start.37 = (bf16[64,1536]{1,0:T(8,128)(2,1)S(1)}, bf16[64,1536]{1,0:T(8,128)(2,1)S(1)}, u32[]{:S(2)}, u32[]{:S(2)}) collective-permute-start(bf16[64,1536]{1,0:T(8,128)(2,1)S(1)} %get-tuple-element.61), channel_id=1, source_target_pairs={{0,2},{1,3},{2,0},{3,1},{4,6},{5,7},{6,4},{7,5},{8,10},{9,11},{10,... | collective-permute-start | bytes 589832 | tf_op jit(solution)/shard_map/ppermute | solution.py:48
  123.4 21.4 %collective-permute-start.38 = (bf16[64,1536]{1,0:T(8,128)(2,1)S(1)}, bf16[64,1536]{1,0:T(8,128)(2,1)S(1)}, u32[]{:S(2)}, u32[]{:S(2)}) collective-permute-start(bf16[64,1536]{1,0:T(8,128)(2,1)S(1)} %get-tuple-element.62), channel_id=1, source_target_pairs={{0,6},{1,7},{2,4},{3,5},{4,2},{5,3},{6,0},{7,1},{8,14},{9,15},{10,... | collective-permute-start | bytes 589832 | tf_op jit(solution)/shard_map/ppermute | solution.py:48
  136.1 8.7 %collective-permute-start.36 = (bf16[64,1536]{1,0:T(8,128)(2,1)S(1)}, bf16[64,1536]{1,0:T(8,128)(2,1)S(1)}, u32[]{:S(2)}, u32[]{:S(2)}) collective-permute-start(bf16[64,1536]{1,0:T(8,128)(2,1)S(1)} %slice.53), channel_id=1, source_target_pairs={{0,4},{1,5},{2,6},{3,7},{4,0},{5,1},{6,2},{7,3},{8,12},{9,13},{10,... | collective-permute-start | bytes 589832 | tf_op jit(solution)/shard_map/ppermute | solution.py:48
  139.5 8.0 %collective-permute-start.33 = (bf16[64,1536]{1,0:T(8,128)(2,1)S(1)}, bf16[64,1536]{1,0:T(8,128)(2,1)S(1)}, u32[]{:S(2)}, u32[]{:S(2)}) collective-permute-start(bf16[64,1536]{1,0:T(8,128)(2,1)S(1)} %get-tuple-element.68), channel_id=1, source_target_pairs={{0,1},{1,2},{2,3},{3,0},{4,5},{5,6},{6,7},{7,4},{8,9},{9,10},{10,1... | collective-permute-start | bytes 589832 | tf_op jit(solution)/shard_map/ppermute | solution.py:48
  141.1 9.1 %collective-permute-start.34 = (bf16[64,1536]{1,0:T(8,128)(2,1)S(1)}, bf16[64,1536]{1,0:T(8,128)(2,1)S(1)}, u32[]{:S(2)}, u32[]{:S(2)}) collective-permute-start(bf16[64,1536]{1,0:T(8,128)(2,1)S(1)} %get-tuple-element.70), channel_id=1, source_target_pairs={{0,3},{1,0},{2,1},{3,2},{4,7},{5,4},{6,5},{7,6},{8,11},{9,8},{10,9... | collective-permute-start | bytes 589832 | tf_op jit(solution)/shard_map/ppermute | solution.py:48
  142.8 9.3 %collective-permute-start.35 = (bf16[64,1536]{1,0:T(8,128)(2,1)S(1)}, bf16[64,1536]{1,0:T(8,128)(2,1)S(1)}, u32[]{:S(2)}, u32[]{:S(2)}) collective-permute-start(bf16[64,1536]{1,0:T(8,128)(2,1)S(1)} %get-tuple-element.69), channel_id=1, source_target_pairs={{0,2},{1,3},{2,0},{3,1},{4,6},{5,7},{6,4},{7,5},{8,10},{9,11},{10,... | collective-permute-start | bytes 589832 | tf_op jit(solution)/shard_map/ppermute | solution.py:48
  (15 other events, 185.7 us)

commit v5 on v4

--- a/solution.py
+++ b/solution.py
@@ -240,14 +240,41 @@
     )(*pieces, columns, before)
 
 
+def score_chunk_kernel(n, start, chunk, *refs):
+    pieces, (columns, before, out, packed, sems) = refs[:n], refs[n:]
+    tall = out.shape[0]
+    mine = pl.ds(chunk * tall, tall)
+    rows = packed_rows([piece.at[mine, :] for piece in pieces], packed, sems)
+    for j in range(columns.shape[0] // STEP):
+        at = slice(j * STEP, (j + 1) * STEP)
+        out[:, at] = before[mine, at] + product(rows, columns[at, start : start + rows.shape[1]])
+
+
+def score_chunk(start, pieces, columns, before, chunk):
+    rows, wide = pieces[0].shape[0] // CHUNKS, pieces[0].shape[1]
+    n_docs = columns.shape[0]
+    n = len(pieces)
+    return pl.pallas_call(
+        functools.partial(score_chunk_kernel, n, start, chunk),
+        out_shape=jax.ShapeDtypeStruct((rows, n_docs), jnp.float32),
+        in_specs=[ANY_SPEC] * n + [VMEM_SPEC] * 2,
+        out_specs=VMEM_SPEC,
+        scratch_shapes=[pltpu.VMEM((rows, n * wide), jnp.bfloat16), pltpu.SemaphoreType.DMA((n,))],
+        compiler_params=pltpu.CompilerParams(vmem_limit_bytes=SCOPED),
+        cost_estimate=pl.CostEstimate(
+            flops=2 * rows * n_docs * n * wide, bytes_accessed=(rows + n_docs) * n * wide * 2, transcendentals=0
+        ),
+    )(*pieces, columns, before)
+
+
 def score_last_kernel(n, start, chunk, *refs):
     pieces, columns, before, outs = refs[:n], refs[n], refs[n + 1], refs[n + 2 :]
-    tall = before.shape[0] // CHUNKS
+    tall = before.shape[0]
     mine = slice(chunk * tall, (chunk + 1) * tall)
     rows = jnp.concatenate([piece[mine, :] for piece in pieces], axis=1)
     for j in range(columns.shape[0] // STEP):
         at = slice(j * STEP, (j + 1) * STEP)
-        part = before[mine, at] + product(rows, columns[at, start:])
+        part = before[:, at] + product(rows, columns[at, start:])
         top = 0
         for out in outs:
             out[:, at] = part[top : top + out.shape[0], :].astype(out.dtype)
@@ -318,13 +345,15 @@
     two[0], scores = lax.optimization_barrier((two[0], scores))
     three = third_stage(*two)
     scores, *_ = lax.optimization_barrier((scores, three[0]))
-    scores = score_next((half - NC) * wide, with_core(two), columns, scores)
-    start, pieces = (early - NC) * wide, with_core(three)
+    after, start = (half - NC) * wide, (early - NC) * wide
+    middle, pieces = with_core(two), with_core(three)
     tall = conditioned.shape[0] // CHUNKS
-    first = score_last(start, pieces, columns, scores, 0, [tall // NH] * NH)
+    first = score_chunk(after, middle, columns, scores, 0)
+    first = score_last(start, pieces, columns, first, 0, [tall // NH] * NH)
     scores, *_ = lax.optimization_barrier((scores, first[0]))
     part, less = tall // NY, tall // GROUP
-    own, ahead, far, across, back = score_last(start, pieces, columns, scores, 1, [part, part, less, less, part])
+    second = score_chunk(after, middle, columns, scores, 1)
+    own, ahead, far, across, back = score_last(start, pieces, columns, second, 1, [part, part, less, less, part])
     go = functools.partial(move, axis="group")
     near = [own, go(ahead, group_perm(0, 1)), go(back, group_perm(0, -1))]
     distant = [go(far, group_perm(0, 2)), go(across, group_perm(1, 2))]

time: 153 us -> 152 us (level)
  starting transfers between devices: 39.4 us -> 36.3 us
    pallas_call x0 -> x2, Pallas kernels: none -> 5.63 us  [score_chunk(): pl.pallas_call(functools.partial(score_chunk_kernel, n, start, chunk), ou...]
    pallas_call x2 -> x1, Pallas kernels: 10.8 us -> 5.4 us  [score_next(): pl.pallas_call(functools.partial(score_next_kernel, n, start), out_shape=...]
    ppermute x39, starting transfers between devices: 34.9 us -> 31.7 us  [move(): return lax.ppermute(piece, axis, perm)]
  transfers between devices with their start and end apart: 40 -> 40, of which waited for: 21 -> 20; matrix products, arithmetic and copies ran while one was open for 1% -> 1% of each run, Pallas kernels for 17% -> 17%
where the time goes in v5:
time: 152 us; the launch traced here: 151 us
  waiting for transfers between devices  77.7 us (51%)
  starting transfers between devices  36.3 us (24%)
  Pallas kernels  28.4 us (19%)
  local copies, waits for them, and re-layouts  7.02 us (5%)
  other arithmetic  1.53 us (1%)
    ppermute x39, waiting for transfers between devices, move(): return lax.ppermute(piece, axis, perm)  77.7 us
    ppermute x39, starting transfers between devices, move(): return lax.ppermute(piece, axis, perm)  31.7 us
    pallas_call x1, Pallas kernels, condition(): pl.pallas_call(functools.partial(condition_kernel, n), out_shape=[jax.Sha...  7.37 us
    unnamed x14, local copies, waits for them, and re-layouts  6.47 us
    pallas_call x2, Pallas kernels, score_chunk(): pl.pallas_call(functools.partial(score_chunk_kernel, n, start, chunk), ou...  5.63 us
    pallas_call x1, Pallas kernels, score_next(): pl.pallas_call(functools.partial(score_next_kernel, n, start), out_shape=...  5.4 us
    all_to_all x1, starting transfers between devices, local(): lax.all_to_all(column_blocks(precond, CHIPS * NC), 'corpus', 0, 0, tiled=...  4.59 us
    pallas_call x1, Pallas kernels, score_first(): pl.pallas_call(functools.partial(score_first_kernel, n), out_shape=[jax.S...  3.9 us
  transfers between devices with their start and end apart: 40, of which 20 were waited for; matrix products, arithmetic and copies ran while one was open for 1% of the time, Pallas kernels for 17%

profile of v5, /device:TPU:0, one launch (start us, length us, event | category | flops | bytes accessed | tf_op | source)
XLA Modules:
  0.0 151.3 jit_solution(2058818311938834700)
XLA Ops:
  0.0 1.6 %collective-permute-start = (bf16[64,4096]{1,0:T(8,128)(2,1)}, bf16[64,4096]{1,0:T(8,128)(2,1)S(1)}, u32[]{:S(2)}, u32[]{:S(2)}) collective-permute-start(bf16[64,4096]{1,0:T(8,128)(2,1)} %refs_0_), channel_id=1, source_target_pairs={{0,16},{8,24},{16,0},{24,8},{32,48},{40,56},{48,32},{56,40},{64,80... | collective-permute-start | bytes 1572872 | tf_op jit(solution)/shard_map/ppermute | solution.py:48
  1.6 1.9 %collective-permute-start.1 = (bf16[64,4096]{1,0:T(8,128)(2,1)}, bf16[64,4096]{1,0:T(8,128)(2,1)S(1)}, u32[]{:S(2)}, u32[]{:S(2)}) collective-permute-start(bf16[64,4096]{1,0:T(8,128)(2,1)} %refs_0_), channel_id=1, source_target_pairs={{0,32},{8,104},{16,48},{24,120},{32,64},{40,8},{48,80},{56,24},{64... | collective-permute-start | bytes 1572872 | tf_op jit(solution)/shard_map/ppermute | solution.py:48
  3.5 2.1 %collective-permute-start.2 = (bf16[64,4096]{1,0:T(8,128)(2,1)}, bf16[64,4096]{1,0:T(8,128)(2,1)S(1)}, u32[]{:S(2)}, u32[]{:S(2)}) collective-permute-start(bf16[64,4096]{1,0:T(8,128)(2,1)} %refs_0_), channel_id=1, source_target_pairs={{0,96},{8,40},{16,112},{24,56},{32,0},{40,72},{48,16},{56,88},{64,... | collective-permute-start | bytes 1572872 | tf_op jit(solution)/shard_map/ppermute | solution.py:48
  5.6 3.1 %shard_map.37 = bf16[16,256,256]{2,1,0:T(8,128)(2,1)} custom-call(bf16[1,256,4096]{2,1,0:T(8,128)(2,1)} %weights.1), custom_call_target="tpu_custom_call" | custom-call | tf_op jit(solution)/shard_map/pallas_call | solution.py:92
  8.8 4.6 %all-to-all-start = ((bf16[16,256,256]{2,1,0:T(8,128)(2,1)}), bf16[16,256,256]{2,1,0:T(8,128)(2,1)}, u32[]{:S(2)}, u32[]{:S(2)}) async-start(bf16[16,256,256]{2,1,0:T(8,128)(2,1)} %shard_map.37), calls=%async_computation | async-start | bytes 4194304 | tf_op jit(solution)/shard_map/all_to_all | solution.py:332
  13.7 3.3 %collective-permute-done.1.refs_4_ = bf16[64,4096]{1,0:T(8,128)(2,1)S(1)} collective-permute-done((bf16[64,4096]{1,0:T(8,128)(2,1)}, bf16[64,4096]{1,0:T(8,128)(2,1)S(1)}, u32[]{:S(2)}, u32[]{:S(2)}) %collective-permute-start.1) | collective-permute-done | bytes 524320 | tf_op jit(solution)/shard_map/ppermute | solution.py:48
  17.1 9.7 %collective-permute-done.2.refs_6_ = bf16[64,4096]{1,0:T(8,128)(2,1)S(1)} collective-permute-done((bf16[64,4096]{1,0:T(8,128)(2,1)}, bf16[64,4096]{1,0:T(8,128)(2,1)S(1)}, u32[]{:S(2)}, u32[]{:S(2)}) %collective-permute-start.2) | collective-permute-done | bytes 524320 | tf_op jit(solution)/shard_map/ppermute | solution.py:48
  27.6 19.2 %collective-permute-done.3.refs_8_ = bf16[64,4096]{1,0:T(8,128)(2,1)} collective-permute-done((bf16[64,4096]{1,0:T(8,128)(2,1)S(1)}, bf16[64,4096]{1,0:T(8,128)(2,1)}, u32[]{:S(2)}, u32[]{:S(2)}) %collective-permute-start.3) | collective-permute-done | bytes 524320 | tf_op jit(solution)/shard_map/ppermute | solution.py:48
  47.1 5.3 %collective-permute-done.10.refs_10_ = bf16[64,4096]{1,0:T(8,128)(2,1)S(1)} collective-permute-done((bf16[64,4096]{1,0:T(8,128)(2,1)S(1)}, bf16[64,4096]{1,0:T(8,128)(2,1)S(1)}, u32[]{:S(2)}, u32[]{:S(2)}) %collective-permute-start.10) | collective-permute-done | bytes 524320 | tf_op jit(solution)/shard_map/ppermute | solution.py:48
  57.1 7.4 %shard_map.38 = (bf16[1024,256]{1,0:T(8,128)(2,1)S(1)}, bf16[4096,256]{1,0:T(8,128)(2,1)}) custom-call(s32[2,14]{1,0:T(2,128)S(1)} %bitcast.37, bf16[64,4096]{1,0:T(8,128)(2,1)S(1)} %copy-done.2, bf16[64,4096]{1,0:T(8,128)(2,1)S(1)} %collective-permute-done.5.refs_1_, bf16[64,4096]{1,0:T(8,128)(2,1)} %copy-done.3, ...), custom_call_target="tpu_custom_call" | custom-call | flops 1879048192 | bytes 9437184 | tf_op jit(solution)/shard_map/pallas_call | solution.py:127
  66.5 1.6 %copy-done.1 = bf16[4096,256]{1,0:T(8,128)(2,1)S(1)} copy-done((bf16[4096,256]{1,0:T(8,128)(2,1)S(1)}, bf16[4096,256]{1,0:T(8,128)(2,1)}, u32[]{:S(2)}) %copy-start.1) | copy-done | bytes 2097176
  70.3 3.0 %collective-permute-start.21 = (bf16[1024,256]{1,0:T(8,128)(2,1)S(1)}, bf16[1024,256]{1,0:T(8,128)(2,1)S(1)}, u32[]{:S(2)}, u32[]{:S(2)}) collective-permute-start(bf16[1024,256]{1,0:T(8,128)(2,1)S(1)} %shard_map.39.refs_0_), channel_id=1, source_target_pairs={{0,96},{8,40},{16,112},{24,56},{32,0},{40,72},{48,16},{56,88},{64,... | collective-permute-start | bytes 1572872 | tf_op jit(solution)/shard_map/ppermute | solution.py:48
  73.6 4.6 %copy-done = bf16[1536,4096]{1,0:T(8,128)(2,1)S(1)} copy-done((bf16[1536,4096]{1,0:T(8,128)(2,1)S(1)}, bf16[1536,4096]{1,0:T(8,128)(2,1)}, u32[]{:S(2)}) %copy-start) | copy-done | bytes 12582936
  78.1 3.9 %shard_map.40 = (f32[1024,1536]{1,0:T(8,128)S(1)}, bf16[1536,3584]{1,0:T(8,128)(2,1)S(1)}) custom-call(s32[16]{0:T(128)S(1)} %multiply_add_fusion.blocks, bf16[1024,256]{1,0:T(8,128)(2,1)S(1)} %shard_map.39.refs_0_, bf16[1024,256]{1,0:T(8,128)(2,1)S(1)} %collective-permute-done.17.refs_1_, bf16[1536,4096]{1,0:T(8,128)(2,1)S(1)} %copy-done), custom_call_target="tpu_custom_call" | custom-call | flops 1610612736 | bytes 2621440 | tf_op jit(solution)/shard_map/pallas_call | solution.py:201
  82.0 1.5 collective-permute-done.15.refs_0_
  83.5 1.7 %collective-permute-done.16.refs_2_ = bf16[1024,256]{1,0:T(8,128)(2,1)S(1)} collective-permute-done((bf16[1024,256]{1,0:T(8,128)(2,1)S(1)}, bf16[1024,256]{1,0:T(8,128)(2,1)S(1)}, u32[]{:S(2)}, u32[]{:S(2)}) %collective-permute-start.16) | collective-permute-done | bytes 524320 | tf_op jit(solution)/shard_map/ppermute | solution.py:48
  87.1 1.5 collective-permute-start.28
  88.6 5.4 %shard_map.41.refs_7_ = f32[1024,1536]{1,0:T(8,128)S(1)} custom-call(bf16[1024,256]{1,0:T(8,128)(2,1)S(1)} %collective-permute-done.15.refs_0_, bf16[1024,256]{1,0:T(8,128)(2,1)S(1)} %collective-permute-done.19.refs_1_, bf16[1024,256]{1,0:T(8,128)(2,1)S(1)} %collective-permute-done.16.refs_2_, ...), custom_call_target="tpu_custom_call", output_to_operand_aliasing={{}: (7, {})} | custom-call | flops 4831838208 | bytes 7864320 | tf_op jit(solution)/shard_map/pallas_call | solution.py:229
  94.0 2.3 %collective-permute-done.18.refs_0_ = bf16[1024,256]{1,0:T(8,128)(2,1)S(1)} collective-permute-done((bf16[1024,256]{1,0:T(8,128)(2,1)S(1)}, bf16[1024,256]{1,0:T(8,128)(2,1)S(1)}, u32[]{:S(2)}, u32[]{:S(2)}) %collective-permute-start.18) | collective-permute-done | bytes 524320 | tf_op jit(solution)/shard_map/ppermute | solution.py:48
  96.7 5.2 %collective-permute-done.26.refs_2_ = bf16[1024,256]{1,0:T(8,128)(2,1)S(1)} collective-permute-done((bf16[1024,256]{1,0:T(8,128)(2,1)S(1)}, bf16[1024,256]{1,0:T(8,128)(2,1)S(1)}, u32[]{:S(2)}, u32[]{:S(2)}) %collective-permute-start.26) | collective-permute-done | bytes 524320 | tf_op jit(solution)/shard_map/ppermute | solution.py:48
  102.4 5.1 %collective-permute-done.23.refs_0_ = bf16[1024,256]{1,0:T(8,128)(2,1)S(1)} collective-permute-done((bf16[1024,256]{1,0:T(8,128)(2,1)S(1)}, bf16[1024,256]{1,0:T(8,128)(2,1)S(1)}, u32[]{:S(2)}, u32[]{:S(2)}) %collective-permute-start.23) | collective-permute-done | bytes 524320 | tf_op jit(solution)/shard_map/ppermute | solution.py:48
  107.6 2.8 %shard_map.42.refs_3_ = f32[512,1536]{1,0:T(8,128)S(1)} custom-call(bf16[1024,256]{1,0:T(8,128)(2,1)S(1)} %collective-permute-done.18.refs_0_, bf16[1024,256]{1,0:T(8,128)(2,1)S(1)} %collective-permute-done.25.refs_1_, bf16[1024,256]{1,0:T(8,128)(2,1)S(1)} %collective-permute-done.26.refs_2_, bf16[1024,256]{1,0:T(8,128)(2,1)S(1)} %collective-permute-done.27.refs_3_, ...), custom_call_target="tpu_custom_call" | custom-call | flops 2415919104 | bytes 6291456 | tf_op jit(solution)/shard_map/pallas_call | solution.py:257
  111.4 3.1 %collective-permute-start.30 = (bf16[256,1536]{1,0:T(8,128)(2,1)S(1)}, bf16[256,1536]{1,0:T(8,128)(2,1)S(1)}, u32[]{:S(2)}, u32[]{:S(2)}) collective-permute-start(bf16[256,1536]{1,0:T(8,128)(2,1)S(1)} %get-tuple-element.51), channel_id=1, source_target_pairs={{0,4},{1,5},{2,6},{3,7},{4,0},{5,1},{6,2},{7,3},{8,12},{9,13},{10,... | collective-permute-start | bytes 2359304 | tf_op jit(solution)/shard_map/ppermute | solution.py:48
  114.5 2.8 %shard_map.44.refs_3_ = f32[512,1536]{1,0:T(8,128)S(1)} custom-call(bf16[1024,256]{1,0:T(8,128)(2,1)S(1)} %collective-permute-done.18.refs_0_, bf16[1024,256]{1,0:T(8,128)(2,1)S(1)} %collective-permute-done.25.refs_1_, bf16[1024,256]{1,0:T(8,128)(2,1)S(1)} %collective-permute-done.26.refs_2_, bf16[1024,256]{1,0:T(8,128)(2,1)S(1)} %collective-permute-done.27.refs_3_, ...), custom_call_target="tpu_custom_call" | custom-call | flops 2415919104 | bytes 6291456 | tf_op jit(solution)/shard_map/pallas_call | solution.py:257
  118.4 1.6 %collective-permute-start.31 = (bf16[128,1536]{1,0:T(8,128)(2,1)S(1)}, bf16[128,1536]{1,0:T(8,128)(2,1)S(1)}, u32[]{:S(2)}, u32[]{:S(2)}) collective-permute-start(bf16[128,1536]{1,0:T(8,128)(2,1)S(1)} %get-tuple-element.54), channel_id=1, source_target_pairs={{0,1},{1,2},{2,3},{3,0},{4,5},{5,6},{6,7},{7,4},{8,9},{9,10},{10,1... | collective-permute-start | bytes 1179656 | tf_op jit(solution)/shard_map/ppermute | solution.py:48
  120.0 1.7 %collective-permute-start.32 = (bf16[128,1536]{1,0:T(8,128)(2,1)S(1)}, bf16[128,1536]{1,0:T(8,128)(2,1)S(1)}, u32[]{:S(2)}, u32[]{:S(2)}) collective-permute-start(bf16[128,1536]{1,0:T(8,128)(2,1)S(1)} %get-tuple-element.55), channel_id=1, source_target_pairs={{0,3},{1,0},{2,1},{3,2},{4,7},{5,4},{6,5},{7,6},{8,11},{9,8},{10,9... | collective-permute-start | bytes 1179656 | tf_op jit(solution)/shard_map/ppermute | solution.py:48
  121.7 2.0 %collective-permute-start.37 = (bf16[64,1536]{1,0:T(8,128)(2,1)S(1)}, bf16[64,1536]{1,0:T(8,128)(2,1)S(1)}, u32[]{:S(2)}, u32[]{:S(2)}) collective-permute-start(bf16[64,1536]{1,0:T(8,128)(2,1)S(1)} %get-tuple-element.61), channel_id=1, source_target_pairs={{0,2},{1,3},{2,0},{3,1},{4,6},{5,7},{6,4},{7,5},{8,10},{9,11},{10,... | collective-permute-start | bytes 589832 | tf_op jit(solution)/shard_map/ppermute | solution.py:48
  125.2 5.8 %collective-permute-done.31 = bf16[128,1536]{1,0:T(8,128)(2,1)S(1)} collective-permute-done((bf16[128,1536]{1,0:T(8,128)(2,1)S(1)}, bf16[128,1536]{1,0:T(8,128)(2,1)S(1)}, u32[]{:S(2)}, u32[]{:S(2)}) %collective-permute-start.31) | collective-permute-done | bytes 393248 | tf_op jit(solution)/shard_map/ppermute | solution.py:48
  131.0 7.8 %collective-permute-done.32 = bf16[128,1536]{1,0:T(8,128)(2,1)S(1)} collective-permute-done((bf16[128,1536]{1,0:T(8,128)(2,1)S(1)}, bf16[128,1536]{1,0:T(8,128)(2,1)S(1)}, u32[]{:S(2)}, u32[]{:S(2)}) %collective-permute-start.32) | collective-permute-done | bytes 393248 | tf_op jit(solution)/shard_map/ppermute | solution.py:48
  139.4 3.7 %collective-permute-start.34 = (bf16[64,1536]{1,0:T(8,128)(2,1)S(1)}, bf16[64,1536]{1,0:T(8,128)(2,1)S(1)}, u32[]{:S(2)}, u32[]{:S(2)}) collective-permute-start(bf16[64,1536]{1,0:T(8,128)(2,1)S(1)} %get-tuple-element.70), channel_id=1, source_target_pairs={{0,3},{1,0},{2,1},{3,2},{4,7},{5,4},{6,5},{7,6},{8,11},{9,8},{10,9... | collective-permute-start | bytes 589832 | tf_op jit(solution)/shard_map/ppermute | solution.py:48
  144.5 1.7 %collective-permute-done.36 = bf16[64,1536]{1,0:T(8,128)(2,1)S(1)} collective-permute-done((bf16[64,1536]{1,0:T(8,128)(2,1)S(1)}, bf16[64,1536]{1,0:T(8,128)(2,1)S(1)}, u32[]{:S(2)}, u32[]{:S(2)}) %collective-permute-start.36) | collective-permute-done | bytes 196640 | tf_op jit(solution)/shard_map/ppermute | solution.py:48
  147.4 2.9 %collective-permute-done.35 = bf16[64,1536]{1,0:T(8,128)(2,1)S(1)} collective-permute-done((bf16[64,1536]{1,0:T(8,128)(2,1)S(1)}, bf16[64,1536]{1,0:T(8,128)(2,1)S(1)}, u32[]{:S(2)}, u32[]{:S(2)}) %collective-permute-start.35) | collective-permute-done | bytes 196640 | tf_op jit(solution)/shard_map/ppermute | solution.py:48
  (87 shorter events, 21.2 us)
Async XLA Ops:
  0.0 13.7 %collective-permute-start = (bf16[64,4096]{1,0:T(8,128)(2,1)}, bf16[64,4096]{1,0:T(8,128)(2,1)S(1)}, u32[]{:S(2)}, u32[]{:S(2)}) collective-permute-start(bf16[64,4096]{1,0:T(8,128)(2,1)} %refs_0_), channel_id=1, source_target_pairs={{0,16},{8,24},{16,0},{24,8},{32,48},{40,56},{48,32},{56,40},{64,80... | collective-permute-start | bytes 1572872 | tf_op jit(solution)/shard_map/ppermute | solution.py:48
  1.6 15.5 %collective-permute-start.1 = (bf16[64,4096]{1,0:T(8,128)(2,1)}, bf16[64,4096]{1,0:T(8,128)(2,1)S(1)}, u32[]{:S(2)}, u32[]{:S(2)}) collective-permute-start(bf16[64,4096]{1,0:T(8,128)(2,1)} %refs_0_), channel_id=1, source_target_pairs={{0,32},{8,104},{16,48},{24,120},{32,64},{40,8},{48,80},{56,24},{64... | collective-permute-start | bytes 1572872 | tf_op jit(solution)/shard_map/ppermute | solution.py:48
  3.5 23.2 %collective-permute-start.2 = (bf16[64,4096]{1,0:T(8,128)(2,1)}, bf16[64,4096]{1,0:T(8,128)(2,1)S(1)}, u32[]{:S(2)}, u32[]{:S(2)}) collective-permute-start(bf16[64,4096]{1,0:T(8,128)(2,1)} %refs_0_), channel_id=1, source_target_pairs={{0,96},{8,40},{16,112},{24,56},{32,0},{40,72},{48,16},{56,88},{64,... | collective-permute-start | bytes 1572872 | tf_op jit(solution)/shard_map/ppermute | solution.py:48
  8.8 48.3 %all-to-all-start = ((bf16[16,256,256]{2,1,0:T(8,128)(2,1)}), bf16[16,256,256]{2,1,0:T(8,128)(2,1)}, u32[]{:S(2)}, u32[]{:S(2)}) async-start(bf16[16,256,256]{2,1,0:T(8,128)(2,1)} %shard_map.37), calls=%async_computation | async-start | bytes 4194304 | tf_op jit(solution)/shard_map/all_to_all | solution.py:332
  26.7 20.1 %collective-permute-start.3 = (bf16[64,4096]{1,0:T(8,128)(2,1)S(1)}, bf16[64,4096]{1,0:T(8,128)(2,1)}, u32[]{:S(2)}, u32[]{:S(2)}) collective-permute-start(bf16[64,4096]{1,0:T(8,128)(2,1)S(1)} %collective-permute-done.refs_2_), channel_id=1, source_target_pairs={{0,32},{8,104},{16,48},{24,120},{32,64},{40,8},{48,80},{56,24},{64... | collective-permute-start | bytes 1572872 | tf_op jit(solution)/shard_map/ppermute | solution.py:48
  26.7 25.6 %collective-permute-start.10 = (bf16[64,4096]{1,0:T(8,128)(2,1)S(1)}, bf16[64,4096]{1,0:T(8,128)(2,1)S(1)}, u32[]{:S(2)}, u32[]{:S(2)}) collective-permute-start(bf16[64,4096]{1,0:T(8,128)(2,1)S(1)} %collective-permute-done.1.refs_4_), channel_id=1, source_target_pairs={{0,32},{8,104},{16,48},{24,120},{32,64},{40,8},{48,80},{56,24},{64... | collective-permute-start | bytes 1572872 | tf_op jit(solution)/shard_map/ppermute | solution.py:48
  26.7 25.6 %collective-permute-start.12 = (bf16[64,4096]{1,0:T(8,128)(2,1)S(1)}, bf16[64,4096]{1,0:T(8,128)(2,1)}, u32[]{:S(2)}, u32[]{:S(2)}) collective-permute-start(bf16[64,4096]{1,0:T(8,128)(2,1)S(1)} %collective-permute-done.2.refs_6_), channel_id=1, source_target_pairs={{0,16},{8,24},{16,0},{24,8},{32,48},{40,56},{48,32},{56,40},{64,80... | collective-permute-start | bytes 1572872 | tf_op jit(solution)/shard_map/ppermute | solution.py:48
  27.1 26.1 %collective-permute-start.6 = (bf16[64,4096]{1,0:T(8,128)(2,1)S(1)}, bf16[64,4096]{1,0:T(8,128)(2,1)}, u32[]{:S(2)}, u32[]{:S(2)}) collective-permute-start(bf16[64,4096]{1,0:T(8,128)(2,1)S(1)} %collective-permute-done.refs_2_), channel_id=1, source_target_pairs={{0,8},{8,0},{16,24},{24,16},{32,40},{40,32},{48,56},{56,48},{64,72... | collective-permute-start | bytes 1572872 | tf_op jit(solution)/shard_map/ppermute | solution.py:48
  27.1 26.1 %collective-permute-start.7 = (bf16[64,4096]{1,0:T(8,128)(2,1)S(1)}, bf16[64,4096]{1,0:T(8,128)(2,1)}, u32[]{:S(2)}, u32[]{:S(2)}) collective-permute-start(bf16[64,4096]{1,0:T(8,128)(2,1)S(1)} %collective-permute-done.1.refs_4_), channel_id=1, source_target_pairs={{0,8},{8,0},{16,24},{24,16},{32,40},{40,32},{48,56},{56,48},{64,72... | collective-permute-start | bytes 1572872 | tf_op jit(solution)/shard_map/ppermute | solution.py:48
  46.8 7.7 %collective-permute-start.8 = (bf16[64,4096]{1,0:T(8,128)(2,1)S(1)}, bf16[64,4096]{1,0:T(8,128)(2,1)}, u32[]{:S(2)}, u32[]{:S(2)}) collective-permute-start(bf16[64,4096]{1,0:T(8,128)(2,1)S(1)} %collective-permute-done.2.refs_6_), channel_id=1, source_target_pairs={{0,8},{8,0},{16,24},{24,16},{32,40},{40,32},{48,56},{56,48},{64,72... | collective-permute-start | bytes 1572872 | tf_op jit(solution)/shard_map/ppermute | solution.py:48
  53.1 11.4 %collective-permute-start.4 = (bf16[64,4096]{1,0:T(8,128)(2,1)}, bf16[64,4096]{1,0:T(8,128)(2,1)S(1)}, u32[]{:S(2)}, u32[]{:S(2)}) collective-permute-start(bf16[64,4096]{1,0:T(8,128)(2,1)} %collective-permute-done.3.refs_8_), channel_id=1, source_target_pairs={{0,32},{8,104},{16,48},{24,120},{32,64},{40,8},{48,80},{56,24},{64... | collective-permute-start | bytes 1572872 | tf_op jit(solution)/shard_map/ppermute | solution.py:48
  69.1 4.4 %collective-permute-start.17 = (bf16[1024,256]{1,0:T(8,128)(2,1)S(1)}, bf16[1024,256]{1,0:T(8,128)(2,1)S(1)}, u32[]{:S(2)}, u32[]{:S(2)}) collective-permute-start(bf16[1024,256]{1,0:T(8,128)(2,1)S(1)} %shard_map.39.refs_0_), channel_id=1, source_target_pairs={{0,8},{8,0},{16,24},{24,16},{32,40},{40,32},{48,56},{56,48},{64,72... | collective-permute-start | bytes 1572872 | tf_op jit(solution)/shard_map/ppermute | solution.py:48
  69.5 14.0 %collective-permute-start.15 = (bf16[1024,256]{1,0:T(8,128)(2,1)S(1)}, bf16[1024,256]{1,0:T(8,128)(2,1)S(1)}, u32[]{:S(2)}, u32[]{:S(2)}) collective-permute-start(bf16[1024,256]{1,0:T(8,128)(2,1)S(1)} %shard_map.39.refs_0_), channel_id=1, source_target_pairs={{0,16},{8,24},{16,0},{24,8},{32,48},{40,56},{48,32},{56,40},{64,80... | collective-permute-start | bytes 1572872 | tf_op jit(solution)/shard_map/ppermute | solution.py:48
  70.1 15.1 %collective-permute-start.16 = (bf16[1024,256]{1,0:T(8,128)(2,1)S(1)}, bf16[1024,256]{1,0:T(8,128)(2,1)S(1)}, u32[]{:S(2)}, u32[]{:S(2)}) collective-permute-start(bf16[1024,256]{1,0:T(8,128)(2,1)S(1)} %shard_map.39.refs_0_), channel_id=1, source_target_pairs={{0,32},{8,104},{16,48},{24,120},{32,64},{40,8},{48,80},{56,24},{64... | collective-permute-start | bytes 1572872 | tf_op jit(solution)/shard_map/ppermute | solution.py:48
  70.3 15.4 %collective-permute-start.21 = (bf16[1024,256]{1,0:T(8,128)(2,1)S(1)}, bf16[1024,256]{1,0:T(8,128)(2,1)S(1)}, u32[]{:S(2)}, u32[]{:S(2)}) collective-permute-start(bf16[1024,256]{1,0:T(8,128)(2,1)S(1)} %shard_map.39.refs_0_), channel_id=1, source_target_pairs={{0,96},{8,40},{16,112},{24,56},{32,0},{40,72},{48,16},{56,88},{64,... | collective-permute-start | bytes 1572872 | tf_op jit(solution)/shard_map/ppermute | solution.py:48
  85.2 3.4 %collective-permute-start.20 = (bf16[1024,256]{1,0:T(8,128)(2,1)S(1)}, bf16[1024,256]{1,0:T(8,128)(2,1)S(1)}, u32[]{:S(2)}, u32[]{:S(2)}) collective-permute-start(bf16[1024,256]{1,0:T(8,128)(2,1)S(1)} %collective-permute-done.16.refs_2_), channel_id=1, source_target_pairs={{0,8},{8,0},{16,24},{24,16},{32,40},{40,32},{48,56},{56,48},{64,72... | collective-permute-start | bytes 1572872 | tf_op jit(solution)/shard_map/ppermute | solution.py:48
  85.9 10.4 %collective-permute-start.18 = (bf16[1024,256]{1,0:T(8,128)(2,1)S(1)}, bf16[1024,256]{1,0:T(8,128)(2,1)S(1)}, u32[]{:S(2)}, u32[]{:S(2)}) collective-permute-start(bf16[1024,256]{1,0:T(8,128)(2,1)S(1)} %collective-permute-done.15.refs_0_), channel_id=1, source_target_pairs={{0,32},{8,104},{16,48},{24,120},{32,64},{40,8},{48,80},{56,24},{64... | collective-permute-start | bytes 1572872 | tf_op jit(solution)/shard_map/ppermute | solution.py:48
  85.9 16.0 %collective-permute-start.26 = (bf16[1024,256]{1,0:T(8,128)(2,1)S(1)}, bf16[1024,256]{1,0:T(8,128)(2,1)S(1)}, u32[]{:S(2)}, u32[]{:S(2)}) collective-permute-start(bf16[1024,256]{1,0:T(8,128)(2,1)S(1)} %collective-permute-done.16.refs_2_), channel_id=1, source_target_pairs={{0,32},{8,104},{16,48},{24,120},{32,64},{40,8},{48,80},{56,24},{64... | collective-permute-start | bytes 1572872 | tf_op jit(solution)/shard_map/ppermute | solution.py:48
  87.1 14.8 %collective-permute-start.28 = (bf16[1024,256]{1,0:T(8,128)(2,1)S(1)}, bf16[1024,256]{1,0:T(8,128)(2,1)S(1)}, u32[]{:S(2)}, u32[]{:S(2)}) collective-permute-start(bf16[1024,256]{1,0:T(8,128)(2,1)S(1)} %collective-permute-done.21.refs_4_), channel_id=1, source_target_pairs={{0,16},{8,24},{16,0},{24,8},{32,48},{40,56},{48,32},{56,40},{64,80... | collective-permute-start | bytes 1572872 | tf_op jit(solution)/shard_map/ppermute | solution.py:48
  96.3 11.2 %collective-permute-start.23 = (bf16[1024,256]{1,0:T(8,128)(2,1)S(1)}, bf16[1024,256]{1,0:T(8,128)(2,1)S(1)}, u32[]{:S(2)}, u32[]{:S(2)}) collective-permute-start(bf16[1024,256]{1,0:T(8,128)(2,1)S(1)} %collective-permute-done.18.refs_0_), channel_id=1, source_target_pairs={{0,32},{8,104},{16,48},{24,120},{32,64},{40,8},{48,80},{56,24},{64... | collective-permute-start | bytes 1572872 | tf_op jit(solution)/shard_map/ppermute | solution.py:48
  96.3 11.2 %collective-permute-start.25 = (bf16[1024,256]{1,0:T(8,128)(2,1)S(1)}, bf16[1024,256]{1,0:T(8,128)(2,1)S(1)}, u32[]{:S(2)}, u32[]{:S(2)}) collective-permute-start(bf16[1024,256]{1,0:T(8,128)(2,1)S(1)} %collective-permute-done.18.refs_0_), channel_id=1, source_target_pairs={{0,8},{8,0},{16,24},{24,16},{32,40},{40,32},{48,56},{56,48},{64,72... | collective-permute-start | bytes 1572872 | tf_op jit(solution)/shard_map/ppermute | solution.py:48
  101.9 5.6 %collective-permute-start.27 = (bf16[1024,256]{1,0:T(8,128)(2,1)S(1)}, bf16[1024,256]{1,0:T(8,128)(2,1)S(1)}, u32[]{:S(2)}, u32[]{:S(2)}) collective-permute-start(bf16[1024,256]{1,0:T(8,128)(2,1)S(1)} %collective-permute-done.26.refs_2_), channel_id=1, source_target_pairs={{0,8},{8,0},{16,24},{24,16},{32,40},{40,32},{48,56},{56,48},{64,72... | collective-permute-start | bytes 1572872 | tf_op jit(solution)/shard_map/ppermute | solution.py:48
  101.9 5.6 %collective-permute-start.29 = (bf16[1024,256]{1,0:T(8,128)(2,1)S(1)}, bf16[1024,256]{1,0:T(8,128)(2,1)S(1)}, u32[]{:S(2)}, u32[]{:S(2)}) collective-permute-start(bf16[1024,256]{1,0:T(8,128)(2,1)S(1)} %collective-permute-done.28.refs_4_), channel_id=1, source_target_pairs={{0,8},{8,0},{16,24},{24,16},{32,40},{40,32},{48,56},{56,48},{64,72... | collective-permute-start | bytes 1572872 | tf_op jit(solution)/shard_map/ppermute | solution.py:48
  111.4 27.3 %collective-permute-start.30 = (bf16[256,1536]{1,0:T(8,128)(2,1)S(1)}, bf16[256,1536]{1,0:T(8,128)(2,1)S(1)}, u32[]{:S(2)}, u32[]{:S(2)}) collective-permute-start(bf16[256,1536]{1,0:T(8,128)(2,1)S(1)} %get-tuple-element.51), channel_id=1, source_target_pairs={{0,4},{1,5},{2,6},{3,7},{4,0},{5,1},{6,2},{7,3},{8,12},{9,13},{10,... | collective-permute-start | bytes 2359304 | tf_op jit(solution)/shard_map/ppermute | solution.py:48
  118.4 12.6 %collective-permute-start.31 = (bf16[128,1536]{1,0:T(8,128)(2,1)S(1)}, bf16[128,1536]{1,0:T(8,128)(2,1)S(1)}, u32[]{:S(2)}, u32[]{:S(2)}) collective-permute-start(bf16[128,1536]{1,0:T(8,128)(2,1)S(1)} %get-tuple-element.54), channel_id=1, source_target_pairs={{0,1},{1,2},{2,3},{3,0},{4,5},{5,6},{6,7},{7,4},{8,9},{9,10},{10,1... | collective-permute-start | bytes 1179656 | tf_op jit(solution)/shard_map/ppermute | solution.py:48
  120.0 18.7 %collective-permute-start.32 = (bf16[128,1536]{1,0:T(8,128)(2,1)S(1)}, bf16[128,1536]{1,0:T(8,128)(2,1)S(1)}, u32[]{:S(2)}, u32[]{:S(2)}) collective-permute-start(bf16[128,1536]{1,0:T(8,128)(2,1)S(1)} %get-tuple-element.55), channel_id=1, source_target_pairs={{0,3},{1,0},{2,1},{3,2},{4,7},{5,4},{6,5},{7,6},{8,11},{9,8},{10,9... | collective-permute-start | bytes 1179656 | tf_op jit(solution)/shard_map/ppermute | solution.py:48
  121.7 21.4 %collective-permute-start.37 = (bf16[64,1536]{1,0:T(8,128)(2,1)S(1)}, bf16[64,1536]{1,0:T(8,128)(2,1)S(1)}, u32[]{:S(2)}, u32[]{:S(2)}) collective-permute-start(bf16[64,1536]{1,0:T(8,128)(2,1)S(1)} %get-tuple-element.61), channel_id=1, source_target_pairs={{0,2},{1,3},{2,0},{3,1},{4,6},{5,7},{6,4},{7,5},{8,10},{9,11},{10,... | collective-permute-start | bytes 589832 | tf_op jit(solution)/shard_map/ppermute | solution.py:48
  123.7 20.8 %collective-permute-start.38 = (bf16[64,1536]{1,0:T(8,128)(2,1)S(1)}, bf16[64,1536]{1,0:T(8,128)(2,1)S(1)}, u32[]{:S(2)}, u32[]{:S(2)}) collective-permute-start(bf16[64,1536]{1,0:T(8,128)(2,1)S(1)} %get-tuple-element.62), channel_id=1, source_target_pairs={{0,6},{1,7},{2,4},{3,5},{4,2},{5,3},{6,0},{7,1},{8,14},{9,15},{10,... | collective-permute-start | bytes 589832 | tf_op jit(solution)/shard_map/ppermute | solution.py:48
  138.9 7.3 %collective-permute-start.36 = (bf16[64,1536]{1,0:T(8,128)(2,1)S(1)}, bf16[64,1536]{1,0:T(8,128)(2,1)S(1)}, u32[]{:S(2)}, u32[]{:S(2)}) collective-permute-start(bf16[64,1536]{1,0:T(8,128)(2,1)S(1)} %slice.53), channel_id=1, source_target_pairs={{0,4},{1,5},{2,6},{3,7},{4,0},{5,1},{6,2},{7,3},{8,12},{9,13},{10,... | collective-permute-start | bytes 589832 | tf_op jit(solution)/shard_map/ppermute | solution.py:48
  139.3 8.1 %collective-permute-start.33 = (bf16[64,1536]{1,0:T(8,128)(2,1)S(1)}, bf16[64,1536]{1,0:T(8,128)(2,1)S(1)}, u32[]{:S(2)}, u32[]{:S(2)}) collective-permute-start(bf16[64,1536]{1,0:T(8,128)(2,1)S(1)} %get-tuple-element.68), channel_id=1, source_target_pairs={{0,1},{1,2},{2,3},{3,0},{4,5},{5,6},{6,7},{7,4},{8,9},{9,10},{10,1... | collective-permute-start | bytes 589832 | tf_op jit(solution)/shard_map/ppermute | solution.py:48
  139.4 8.0 %collective-permute-start.34 = (bf16[64,1536]{1,0:T(8,128)(2,1)S(1)}, bf16[64,1536]{1,0:T(8,128)(2,1)S(1)}, u32[]{:S(2)}, u32[]{:S(2)}) collective-permute-start(bf16[64,1536]{1,0:T(8,128)(2,1)S(1)} %get-tuple-element.70), channel_id=1, source_target_pairs={{0,3},{1,0},{2,1},{3,2},{4,7},{5,4},{6,5},{7,6},{8,11},{9,8},{10,9... | collective-permute-start | bytes 589832 | tf_op jit(solution)/shard_map/ppermute | solution.py:48
  143.1 7.2 %collective-permute-start.35 = (bf16[64,1536]{1,0:T(8,128)(2,1)S(1)}, bf16[64,1536]{1,0:T(8,128)(2,1)S(1)}, u32[]{:S(2)}, u32[]{:S(2)}) collective-permute-start(bf16[64,1536]{1,0:T(8,128)(2,1)S(1)} %get-tuple-element.69), channel_id=1, source_target_pairs={{0,2},{1,3},{2,0},{3,1},{4,6},{5,7},{6,4},{7,5},{8,10},{9,11},{10,... | collective-permute-start | bytes 589832 | tf_op jit(solution)/shard_map/ppermute | solution.py:48
  (15 other events, 185.2 us)

commit v6 on v5

--- a/solution.py
+++ b/solution.py
@@ -344,15 +344,15 @@
     scores = score_next(0, with_core(one[1:]), columns, scores)
     two[0], scores = lax.optimization_barrier((two[0], scores))
     three = third_stage(*two)
-    scores, *_ = lax.optimization_barrier((scores, three[0]))
+    held, *_ = lax.optimization_barrier((scores, three[0]))
     after, start = (half - NC) * wide, (early - NC) * wide
     middle, pieces = with_core(two), with_core(three)
     tall = conditioned.shape[0] // CHUNKS
-    first = score_chunk(after, middle, columns, scores, 0)
+    first = score_chunk(after, middle, columns, held, 0)
     first = score_last(start, pieces, columns, first, 0, [tall // NH] * NH)
-    scores, *_ = lax.optimization_barrier((scores, first[0]))
     part, less = tall // NY, tall // GROUP
     second = score_chunk(after, middle, columns, scores, 1)
+    second, *_ = lax.optimization_barrier((second, first[0]))
     own, ahead, far, across, back = score_last(start, pieces, columns, second, 1, [part, part, less, less, part])
     go = functools.partial(move, axis="group")
     near = [own, go(ahead, group_perm(0, 1)), go(back, group_perm(0, -1))]

time: 152 us -> 152 us (level)
  no operation moved by 1% of the time
where the time goes in v6:
time: 152 us; the launch traced here: 151 us
  waiting for transfers between devices  77.7 us (51%)
  starting transfers between devices  36.3 us (24%)
  Pallas kernels  28.4 us (19%)
  local copies, waits for them, and re-layouts  7.02 us (5%)
  other arithmetic  1.53 us (1%)
    ppermute x39, waiting for transfers between devices, move(): return lax.ppermute(piece, axis, perm)  77.7 us
    ppermute x39, starting transfers between devices, move(): return lax.ppermute(piece, axis, perm)  31.7 us
    pallas_call x1, Pallas kernels, condition(): pl.pallas_call(functools.partial(condition_kernel, n), out_shape=[jax.Sha...  7.37 us
    unnamed x14, local copies, waits for them, and re-layouts  6.47 us
    pallas_call x2, Pallas kernels, score_chunk(): pl.pallas_call(functools.partial(score_chunk_kernel, n, start, chunk), ou...  5.63 us
    pallas_call x1, Pallas kernels, score_next(): pl.pallas_call(functools.partial(score_next_kernel, n, start), out_shape=...  5.4 us
    all_to_all x1, starting transfers between devices, local(): lax.all_to_all(column_blocks(precond, CHIPS * NC), 'corpus', 0, 0, tiled=...  4.59 us
    pallas_call x1, Pallas kernels, score_first(): pl.pallas_call(functools.partial(score_first_kernel, n), out_shape=[jax.S...  3.9 us
  transfers between devices with their start and end apart: 40, of which 20 were waited for; matrix products, arithmetic and copies ran while one was open for 1% of the time, Pallas kernels for 17%

profile of v6, /device:TPU:0, one launch (start us, length us, event | category | flops | bytes accessed | tf_op | source)
XLA Modules:
  0.0 151.3 jit_solution(2058818311938834700)
XLA Ops:
  0.0 1.6 %collective-permute-start = (bf16[64,4096]{1,0:T(8,128)(2,1)}, bf16[64,4096]{1,0:T(8,128)(2,1)S(1)}, u32[]{:S(2)}, u32[]{:S(2)}) collective-permute-start(bf16[64,4096]{1,0:T(8,128)(2,1)} %refs_0_), channel_id=1, source_target_pairs={{0,16},{8,24},{16,0},{24,8},{32,48},{40,56},{48,32},{56,40},{64,80... | collective-permute-start | bytes 1572872 | tf_op jit(solution)/shard_map/ppermute | solution.py:48
  1.6 1.9 %collective-permute-start.1 = (bf16[64,4096]{1,0:T(8,128)(2,1)}, bf16[64,4096]{1,0:T(8,128)(2,1)S(1)}, u32[]{:S(2)}, u32[]{:S(2)}) collective-permute-start(bf16[64,4096]{1,0:T(8,128)(2,1)} %refs_0_), channel_id=1, source_target_pairs={{0,32},{8,104},{16,48},{24,120},{32,64},{40,8},{48,80},{56,24},{64... | collective-permute-start | bytes 1572872 | tf_op jit(solution)/shard_map/ppermute | solution.py:48
  3.5 2.1 %collective-permute-start.2 = (bf16[64,4096]{1,0:T(8,128)(2,1)}, bf16[64,4096]{1,0:T(8,128)(2,1)S(1)}, u32[]{:S(2)}, u32[]{:S(2)}) collective-permute-start(bf16[64,4096]{1,0:T(8,128)(2,1)} %refs_0_), channel_id=1, source_target_pairs={{0,96},{8,40},{16,112},{24,56},{32,0},{40,72},{48,16},{56,88},{64,... | collective-permute-start | bytes 1572872 | tf_op jit(solution)/shard_map/ppermute | solution.py:48
  5.6 3.1 %shard_map.37 = bf16[16,256,256]{2,1,0:T(8,128)(2,1)} custom-call(bf16[1,256,4096]{2,1,0:T(8,128)(2,1)} %weights.1), custom_call_target="tpu_custom_call" | custom-call | tf_op jit(solution)/shard_map/pallas_call | solution.py:92
  8.8 4.6 %all-to-all-start = ((bf16[16,256,256]{2,1,0:T(8,128)(2,1)}), bf16[16,256,256]{2,1,0:T(8,128)(2,1)}, u32[]{:S(2)}, u32[]{:S(2)}) async-start(bf16[16,256,256]{2,1,0:T(8,128)(2,1)} %shard_map.37), calls=%async_computation | async-start | bytes 4194304 | tf_op jit(solution)/shard_map/all_to_all | solution.py:332
  13.7 3.3 %collective-permute-done.1.refs_4_ = bf16[64,4096]{1,0:T(8,128)(2,1)S(1)} collective-permute-done((bf16[64,4096]{1,0:T(8,128)(2,1)}, bf16[64,4096]{1,0:T(8,128)(2,1)S(1)}, u32[]{:S(2)}, u32[]{:S(2)}) %collective-permute-start.1) | collective-permute-done | bytes 524320 | tf_op jit(solution)/shard_map/ppermute | solution.py:48
  17.1 9.7 %collective-permute-done.2.refs_6_ = bf16[64,4096]{1,0:T(8,128)(2,1)S(1)} collective-permute-done((bf16[64,4096]{1,0:T(8,128)(2,1)}, bf16[64,4096]{1,0:T(8,128)(2,1)S(1)}, u32[]{:S(2)}, u32[]{:S(2)}) %collective-permute-start.2) | collective-permute-done | bytes 524320 | tf_op jit(solution)/shard_map/ppermute | solution.py:48
  27.6 19.2 %collective-permute-done.3.refs_8_ = bf16[64,4096]{1,0:T(8,128)(2,1)} collective-permute-done((bf16[64,4096]{1,0:T(8,128)(2,1)S(1)}, bf16[64,4096]{1,0:T(8,128)(2,1)}, u32[]{:S(2)}, u32[]{:S(2)}) %collective-permute-start.3) | collective-permute-done | bytes 524320 | tf_op jit(solution)/shard_map/ppermute | solution.py:48
  47.1 5.3 %collective-permute-done.10.refs_10_ = bf16[64,4096]{1,0:T(8,128)(2,1)S(1)} collective-permute-done((bf16[64,4096]{1,0:T(8,128)(2,1)S(1)}, bf16[64,4096]{1,0:T(8,128)(2,1)S(1)}, u32[]{:S(2)}, u32[]{:S(2)}) %collective-permute-start.10) | collective-permute-done | bytes 524320 | tf_op jit(solution)/shard_map/ppermute | solution.py:48
  57.1 7.4 %shard_map.38 = (bf16[1024,256]{1,0:T(8,128)(2,1)S(1)}, bf16[4096,256]{1,0:T(8,128)(2,1)}) custom-call(s32[2,14]{1,0:T(2,128)S(1)} %bitcast.37, bf16[64,4096]{1,0:T(8,128)(2,1)S(1)} %copy-done.2, bf16[64,4096]{1,0:T(8,128)(2,1)S(1)} %collective-permute-done.5.refs_1_, bf16[64,4096]{1,0:T(8,128)(2,1)} %copy-done.3, ...), custom_call_target="tpu_custom_call" | custom-call | flops 1879048192 | bytes 9437184 | tf_op jit(solution)/shard_map/pallas_call | solution.py:127
  66.5 1.6 %copy-done.1 = bf16[4096,256]{1,0:T(8,128)(2,1)S(1)} copy-done((bf16[4096,256]{1,0:T(8,128)(2,1)S(1)}, bf16[4096,256]{1,0:T(8,128)(2,1)}, u32[]{:S(2)}) %copy-start.1) | copy-done | bytes 2097176
  70.3 3.0 %collective-permute-start.21 = (bf16[1024,256]{1,0:T(8,128)(2,1)S(1)}, bf16[1024,256]{1,0:T(8,128)(2,1)S(1)}, u32[]{:S(2)}, u32[]{:S(2)}) collective-permute-start(bf16[1024,256]{1,0:T(8,128)(2,1)S(1)} %shard_map.39.refs_0_), channel_id=1, source_target_pairs={{0,96},{8,40},{16,112},{24,56},{32,0},{40,72},{48,16},{56,88},{64,... | collective-permute-start | bytes 1572872 | tf_op jit(solution)/shard_map/ppermute | solution.py:48
  73.6 4.6 %copy-done = bf16[1536,4096]{1,0:T(8,128)(2,1)S(1)} copy-done((bf16[1536,4096]{1,0:T(8,128)(2,1)S(1)}, bf16[1536,4096]{1,0:T(8,128)(2,1)}, u32[]{:S(2)}) %copy-start) | copy-done | bytes 12582936
  78.1 3.9 %shard_map.40 = (f32[1024,1536]{1,0:T(8,128)S(1)}, bf16[1536,3584]{1,0:T(8,128)(2,1)S(1)}) custom-call(s32[16]{0:T(128)S(1)} %multiply_add_fusion.blocks, bf16[1024,256]{1,0:T(8,128)(2,1)S(1)} %shard_map.39.refs_0_, bf16[1024,256]{1,0:T(8,128)(2,1)S(1)} %collective-permute-done.17.refs_1_, bf16[1536,4096]{1,0:T(8,128)(2,1)S(1)} %copy-done), custom_call_target="tpu_custom_call" | custom-call | flops 1610612736 | bytes 2621440 | tf_op jit(solution)/shard_map/pallas_call | solution.py:201
  82.0 1.5 collective-permute-done.15.refs_0_
  83.5 1.7 %collective-permute-done.16.refs_2_ = bf16[1024,256]{1,0:T(8,128)(2,1)S(1)} collective-permute-done((bf16[1024,256]{1,0:T(8,128)(2,1)S(1)}, bf16[1024,256]{1,0:T(8,128)(2,1)S(1)}, u32[]{:S(2)}, u32[]{:S(2)}) %collective-permute-start.16) | collective-permute-done | bytes 524320 | tf_op jit(solution)/shard_map/ppermute | solution.py:48
  87.1 1.5 collective-permute-start.28
  88.6 5.4 %shard_map.41.refs_7_ = f32[1024,1536]{1,0:T(8,128)S(1)} custom-call(bf16[1024,256]{1,0:T(8,128)(2,1)S(1)} %collective-permute-done.15.refs_0_, bf16[1024,256]{1,0:T(8,128)(2,1)S(1)} %collective-permute-done.19.refs_1_, bf16[1024,256]{1,0:T(8,128)(2,1)S(1)} %collective-permute-done.16.refs_2_, ...), custom_call_target="tpu_custom_call", output_to_operand_aliasing={{}: (7, {})} | custom-call | flops 4831838208 | bytes 7864320 | tf_op jit(solution)/shard_map/pallas_call | solution.py:229
  94.0 2.3 %collective-permute-done.18.refs_0_ = bf16[1024,256]{1,0:T(8,128)(2,1)S(1)} collective-permute-done((bf16[1024,256]{1,0:T(8,128)(2,1)S(1)}, bf16[1024,256]{1,0:T(8,128)(2,1)S(1)}, u32[]{:S(2)}, u32[]{:S(2)}) %collective-permute-start.18) | collective-permute-done | bytes 524320 | tf_op jit(solution)/shard_map/ppermute | solution.py:48
  96.7 5.2 %collective-permute-done.26.refs_2_ = bf16[1024,256]{1,0:T(8,128)(2,1)S(1)} collective-permute-done((bf16[1024,256]{1,0:T(8,128)(2,1)S(1)}, bf16[1024,256]{1,0:T(8,128)(2,1)S(1)}, u32[]{:S(2)}, u32[]{:S(2)}) %collective-permute-start.26) | collective-permute-done | bytes 524320 | tf_op jit(solution)/shard_map/ppermute | solution.py:48
  102.4 5.1 %collective-permute-done.23.refs_0_ = bf16[1024,256]{1,0:T(8,128)(2,1)S(1)} collective-permute-done((bf16[1024,256]{1,0:T(8,128)(2,1)S(1)}, bf16[1024,256]{1,0:T(8,128)(2,1)S(1)}, u32[]{:S(2)}, u32[]{:S(2)}) %collective-permute-start.23) | collective-permute-done | bytes 524320 | tf_op jit(solution)/shard_map/ppermute | solution.py:48
  107.6 2.8 %shard_map.42.refs_3_ = f32[512,1536]{1,0:T(8,128)S(1)} custom-call(bf16[1024,256]{1,0:T(8,128)(2,1)S(1)} %collective-permute-done.18.refs_0_, bf16[1024,256]{1,0:T(8,128)(2,1)S(1)} %collective-permute-done.25.refs_1_, bf16[1024,256]{1,0:T(8,128)(2,1)S(1)} %collective-permute-done.26.refs_2_, bf16[1024,256]{1,0:T(8,128)(2,1)S(1)} %collective-permute-done.27.refs_3_, ...), custom_call_target="tpu_custom_call" | custom-call | flops 2415919104 | bytes 6291456 | tf_op jit(solution)/shard_map/pallas_call | solution.py:257
  111.4 3.1 %collective-permute-start.30 = (bf16[256,1536]{1,0:T(8,128)(2,1)S(1)}, bf16[256,1536]{1,0:T(8,128)(2,1)S(1)}, u32[]{:S(2)}, u32[]{:S(2)}) collective-permute-start(bf16[256,1536]{1,0:T(8,128)(2,1)S(1)} %get-tuple-element.51), channel_id=1, source_target_pairs={{0,4},{1,5},{2,6},{3,7},{4,0},{5,1},{6,2},{7,3},{8,12},{9,13},{10,... | collective-permute-start | bytes 2359304 | tf_op jit(solution)/shard_map/ppermute | solution.py:48
  114.5 2.8 %shard_map.44.refs_3_ = f32[512,1536]{1,0:T(8,128)S(1)} custom-call(bf16[1024,256]{1,0:T(8,128)(2,1)S(1)} %collective-permute-done.18.refs_0_, bf16[1024,256]{1,0:T(8,128)(2,1)S(1)} %collective-permute-done.25.refs_1_, bf16[1024,256]{1,0:T(8,128)(2,1)S(1)} %collective-permute-done.26.refs_2_, bf16[1024,256]{1,0:T(8,128)(2,1)S(1)} %collective-permute-done.27.refs_3_, ...), custom_call_target="tpu_custom_call" | custom-call | flops 2415919104 | bytes 6291456 | tf_op jit(solution)/shard_map/pallas_call | solution.py:257
  118.4 1.6 %collective-permute-start.31 = (bf16[128,1536]{1,0:T(8,128)(2,1)S(1)}, bf16[128,1536]{1,0:T(8,128)(2,1)S(1)}, u32[]{:S(2)}, u32[]{:S(2)}) collective-permute-start(bf16[128,1536]{1,0:T(8,128)(2,1)S(1)} %get-tuple-element.54), channel_id=1, source_target_pairs={{0,1},{1,2},{2,3},{3,0},{4,5},{5,6},{6,7},{7,4},{8,9},{9,10},{10,1... | collective-permute-start | bytes 1179656 | tf_op jit(solution)/shard_map/ppermute | solution.py:48
  120.0 1.7 %collective-permute-start.32 = (bf16[128,1536]{1,0:T(8,128)(2,1)S(1)}, bf16[128,1536]{1,0:T(8,128)(2,1)S(1)}, u32[]{:S(2)}, u32[]{:S(2)}) collective-permute-start(bf16[128,1536]{1,0:T(8,128)(2,1)S(1)} %get-tuple-element.55), channel_id=1, source_target_pairs={{0,3},{1,0},{2,1},{3,2},{4,7},{5,4},{6,5},{7,6},{8,11},{9,8},{10,9... | collective-permute-start | bytes 1179656 | tf_op jit(solution)/shard_map/ppermute | solution.py:48
  121.7 2.0 %collective-permute-start.37 = (bf16[64,1536]{1,0:T(8,128)(2,1)S(1)}, bf16[64,1536]{1,0:T(8,128)(2,1)S(1)}, u32[]{:S(2)}, u32[]{:S(2)}) collective-permute-start(bf16[64,1536]{1,0:T(8,128)(2,1)S(1)} %get-tuple-element.61), channel_id=1, source_target_pairs={{0,2},{1,3},{2,0},{3,1},{4,6},{5,7},{6,4},{7,5},{8,10},{9,11},{10,... | collective-permute-start | bytes 589832 | tf_op jit(solution)/shard_map/ppermute | solution.py:48
  125.2 5.8 %collective-permute-done.31 = bf16[128,1536]{1,0:T(8,128)(2,1)S(1)} collective-permute-done((bf16[128,1536]{1,0:T(8,128)(2,1)S(1)}, bf16[128,1536]{1,0:T(8,128)(2,1)S(1)}, u32[]{:S(2)}, u32[]{:S(2)}) %collective-permute-start.31) | collective-permute-done | bytes 393248 | tf_op jit(solution)/shard_map/ppermute | solution.py:48
  131.0 7.8 %collective-permute-done.32 = bf16[128,1536]{1,0:T(8,128)(2,1)S(1)} collective-permute-done((bf16[128,1536]{1,0:T(8,128)(2,1)S(1)}, bf16[128,1536]{1,0:T(8,128)(2,1)S(1)}, u32[]{:S(2)}, u32[]{:S(2)}) %collective-permute-start.32) | collective-permute-done | bytes 393248 | tf_op jit(solution)/shard_map/ppermute | solution.py:48
  139.4 3.7 %collective-permute-start.34 = (bf16[64,1536]{1,0:T(8,128)(2,1)S(1)}, bf16[64,1536]{1,0:T(8,128)(2,1)S(1)}, u32[]{:S(2)}, u32[]{:S(2)}) collective-permute-start(bf16[64,1536]{1,0:T(8,128)(2,1)S(1)} %get-tuple-element.70), channel_id=1, source_target_pairs={{0,3},{1,0},{2,1},{3,2},{4,7},{5,4},{6,5},{7,6},{8,11},{9,8},{10,9... | collective-permute-start | bytes 589832 | tf_op jit(solution)/shard_map/ppermute | solution.py:48
  144.5 1.7 %collective-permute-done.36 = bf16[64,1536]{1,0:T(8,128)(2,1)S(1)} collective-permute-done((bf16[64,1536]{1,0:T(8,128)(2,1)S(1)}, bf16[64,1536]{1,0:T(8,128)(2,1)S(1)}, u32[]{:S(2)}, u32[]{:S(2)}) %collective-permute-start.36) | collective-permute-done | bytes 196640 | tf_op jit(solution)/shard_map/ppermute | solution.py:48
  147.4 2.9 %collective-permute-done.35 = bf16[64,1536]{1,0:T(8,128)(2,1)S(1)} collective-permute-done((bf16[64,1536]{1,0:T(8,128)(2,1)S(1)}, bf16[64,1536]{1,0:T(8,128)(2,1)S(1)}, u32[]{:S(2)}, u32[]{:S(2)}) %collective-permute-start.35) | collective-permute-done | bytes 196640 | tf_op jit(solution)/shard_map/ppermute | solution.py:48
  (87 shorter events, 21.2 us)
Async XLA Ops:
  0.0 13.7 %collective-permute-start = (bf16[64,4096]{1,0:T(8,128)(2,1)}, bf16[64,4096]{1,0:T(8,128)(2,1)S(1)}, u32[]{:S(2)}, u32[]{:S(2)}) collective-permute-start(bf16[64,4096]{1,0:T(8,128)(2,1)} %refs_0_), channel_id=1, source_target_pairs={{0,16},{8,24},{16,0},{24,8},{32,48},{40,56},{48,32},{56,40},{64,80... | collective-permute-start | bytes 1572872 | tf_op jit(solution)/shard_map/ppermute | solution.py:48
  1.6 15.5 %collective-permute-start.1 = (bf16[64,4096]{1,0:T(8,128)(2,1)}, bf16[64,4096]{1,0:T(8,128)(2,1)S(1)}, u32[]{:S(2)}, u32[]{:S(2)}) collective-permute-start(bf16[64,4096]{1,0:T(8,128)(2,1)} %refs_0_), channel_id=1, source_target_pairs={{0,32},{8,104},{16,48},{24,120},{32,64},{40,8},{48,80},{56,24},{64... | collective-permute-start | bytes 1572872 | tf_op jit(solution)/shard_map/ppermute | solution.py:48
  3.5 23.2 %collective-permute-start.2 = (bf16[64,4096]{1,0:T(8,128)(2,1)}, bf16[64,4096]{1,0:T(8,128)(2,1)S(1)}, u32[]{:S(2)}, u32[]{:S(2)}) collective-permute-start(bf16[64,4096]{1,0:T(8,128)(2,1)} %refs_0_), channel_id=1, source_target_pairs={{0,96},{8,40},{16,112},{24,56},{32,0},{40,72},{48,16},{56,88},{64,... | collective-permute-start | bytes 1572872 | tf_op jit(solution)/shard_map/ppermute | solution.py:48
  8.8 48.3 %all-to-all-start = ((bf16[16,256,256]{2,1,0:T(8,128)(2,1)}), bf16[16,256,256]{2,1,0:T(8,128)(2,1)}, u32[]{:S(2)}, u32[]{:S(2)}) async-start(bf16[16,256,256]{2,1,0:T(8,128)(2,1)} %shard_map.37), calls=%async_computation | async-start | bytes 4194304 | tf_op jit(solution)/shard_map/all_to_all | solution.py:332
  26.7 20.1 %collective-permute-start.3 = (bf16[64,4096]{1,0:T(8,128)(2,1)S(1)}, bf16[64,4096]{1,0:T(8,128)(2,1)}, u32[]{:S(2)}, u32[]{:S(2)}) collective-permute-start(bf16[64,4096]{1,0:T(8,128)(2,1)S(1)} %collective-permute-done.refs_2_), channel_id=1, source_target_pairs={{0,32},{8,104},{16,48},{24,120},{32,64},{40,8},{48,80},{56,24},{64... | collective-permute-start | bytes 1572872 | tf_op jit(solution)/shard_map/ppermute | solution.py:48
  26.7 25.6 %collective-permute-start.10 = (bf16[64,4096]{1,0:T(8,128)(2,1)S(1)}, bf16[64,4096]{1,0:T(8,128)(2,1)S(1)}, u32[]{:S(2)}, u32[]{:S(2)}) collective-permute-start(bf16[64,4096]{1,0:T(8,128)(2,1)S(1)} %collective-permute-done.1.refs_4_), channel_id=1, source_target_pairs={{0,32},{8,104},{16,48},{24,120},{32,64},{40,8},{48,80},{56,24},{64... | collective-permute-start | bytes 1572872 | tf_op jit(solution)/shard_map/ppermute | solution.py:48
  26.7 25.6 %collective-permute-start.12 = (bf16[64,4096]{1,0:T(8,128)(2,1)S(1)}, bf16[64,4096]{1,0:T(8,128)(2,1)}, u32[]{:S(2)}, u32[]{:S(2)}) collective-permute-start(bf16[64,4096]{1,0:T(8,128)(2,1)S(1)} %collective-permute-done.2.refs_6_), channel_id=1, source_target_pairs={{0,16},{8,24},{16,0},{24,8},{32,48},{40,56},{48,32},{56,40},{64,80... | collective-permute-start | bytes 1572872 | tf_op jit(solution)/shard_map/ppermute | solution.py:48
  27.1 26.1 %collective-permute-start.6 = (bf16[64,4096]{1,0:T(8,128)(2,1)S(1)}, bf16[64,4096]{1,0:T(8,128)(2,1)}, u32[]{:S(2)}, u32[]{:S(2)}) collective-permute-start(bf16[64,4096]{1,0:T(8,128)(2,1)S(1)} %collective-permute-done.refs_2_), channel_id=1, source_target_pairs={{0,8},{8,0},{16,24},{24,16},{32,40},{40,32},{48,56},{56,48},{64,72... | collective-permute-start | bytes 1572872 | tf_op jit(solution)/shard_map/ppermute | solution.py:48
  27.1 26.1 %collective-permute-start.7 = (bf16[64,4096]{1,0:T(8,128)(2,1)S(1)}, bf16[64,4096]{1,0:T(8,128)(2,1)}, u32[]{:S(2)}, u32[]{:S(2)}) collective-permute-start(bf16[64,4096]{1,0:T(8,128)(2,1)S(1)} %collective-permute-done.1.refs_4_), channel_id=1, source_target_pairs={{0,8},{8,0},{16,24},{24,16},{32,40},{40,32},{48,56},{56,48},{64,72... | collective-permute-start | bytes 1572872 | tf_op jit(solution)/shard_map/ppermute | solution.py:48
  46.8 7.7 %collective-permute-start.8 = (bf16[64,4096]{1,0:T(8,128)(2,1)S(1)}, bf16[64,4096]{1,0:T(8,128)(2,1)}, u32[]{:S(2)}, u32[]{:S(2)}) collective-permute-start(bf16[64,4096]{1,0:T(8,128)(2,1)S(1)} %collective-permute-done.2.refs_6_), channel_id=1, source_target_pairs={{0,8},{8,0},{16,24},{24,16},{32,40},{40,32},{48,56},{56,48},{64,72... | collective-permute-start | bytes 1572872 | tf_op jit(solution)/shard_map/ppermute | solution.py:48
  53.1 11.4 %collective-permute-start.4 = (bf16[64,4096]{1,0:T(8,128)(2,1)}, bf16[64,4096]{1,0:T(8,128)(2,1)S(1)}, u32[]{:S(2)}, u32[]{:S(2)}) collective-permute-start(bf16[64,4096]{1,0:T(8,128)(2,1)} %collective-permute-done.3.refs_8_), channel_id=1, source_target_pairs={{0,32},{8,104},{16,48},{24,120},{32,64},{40,8},{48,80},{56,24},{64... | collective-permute-start | bytes 1572872 | tf_op jit(solution)/shard_map/ppermute | solution.py:48
  69.1 4.4 %collective-permute-start.17 = (bf16[1024,256]{1,0:T(8,128)(2,1)S(1)}, bf16[1024,256]{1,0:T(8,128)(2,1)S(1)}, u32[]{:S(2)}, u32[]{:S(2)}) collective-permute-start(bf16[1024,256]{1,0:T(8,128)(2,1)S(1)} %shard_map.39.refs_0_), channel_id=1, source_target_pairs={{0,8},{8,0},{16,24},{24,16},{32,40},{40,32},{48,56},{56,48},{64,72... | collective-permute-start | bytes 1572872 | tf_op jit(solution)/shard_map/ppermute | solution.py:48
  69.5 14.0 %collective-permute-start.15 = (bf16[1024,256]{1,0:T(8,128)(2,1)S(1)}, bf16[1024,256]{1,0:T(8,128)(2,1)S(1)}, u32[]{:S(2)}, u32[]{:S(2)}) collective-permute-start(bf16[1024,256]{1,0:T(8,128)(2,1)S(1)} %shard_map.39.refs_0_), channel_id=1, source_target_pairs={{0,16},{8,24},{16,0},{24,8},{32,48},{40,56},{48,32},{56,40},{64,80... | collective-permute-start | bytes 1572872 | tf_op jit(solution)/shard_map/ppermute | solution.py:48
  70.1 15.1 %collective-permute-start.16 = (bf16[1024,256]{1,0:T(8,128)(2,1)S(1)}, bf16[1024,256]{1,0:T(8,128)(2,1)S(1)}, u32[]{:S(2)}, u32[]{:S(2)}) collective-permute-start(bf16[1024,256]{1,0:T(8,128)(2,1)S(1)} %shard_map.39.refs_0_), channel_id=1, source_target_pairs={{0,32},{8,104},{16,48},{24,120},{32,64},{40,8},{48,80},{56,24},{64... | collective-permute-start | bytes 1572872 | tf_op jit(solution)/shard_map/ppermute | solution.py:48
  70.3 15.4 %collective-permute-start.21 = (bf16[1024,256]{1,0:T(8,128)(2,1)S(1)}, bf16[1024,256]{1,0:T(8,128)(2,1)S(1)}, u32[]{:S(2)}, u32[]{:S(2)}) collective-permute-start(bf16[1024,256]{1,0:T(8,128)(2,1)S(1)} %shard_map.39.refs_0_), channel_id=1, source_target_pairs={{0,96},{8,40},{16,112},{24,56},{32,0},{40,72},{48,16},{56,88},{64,... | collective-permute-start | bytes 1572872 | tf_op jit(solution)/shard_map/ppermute | solution.py:48
  85.2 3.4 %collective-permute-start.20 = (bf16[1024,256]{1,0:T(8,128)(2,1)S(1)}, bf16[1024,256]{1,0:T(8,128)(2,1)S(1)}, u32[]{:S(2)}, u32[]{:S(2)}) collective-permute-start(bf16[1024,256]{1,0:T(8,128)(2,1)S(1)} %collective-permute-done.16.refs_2_), channel_id=1, source_target_pairs={{0,8},{8,0},{16,24},{24,16},{32,40},{40,32},{48,56},{56,48},{64,72... | collective-permute-start | bytes 1572872 | tf_op jit(solution)/shard_map/ppermute | solution.py:48
  85.9 10.4 %collective-permute-start.18 = (bf16[1024,256]{1,0:T(8,128)(2,1)S(1)}, bf16[1024,256]{1,0:T(8,128)(2,1)S(1)}, u32[]{:S(2)}, u32[]{:S(2)}) collective-permute-start(bf16[1024,256]{1,0:T(8,128)(2,1)S(1)} %collective-permute-done.15.refs_0_), channel_id=1, source_target_pairs={{0,32},{8,104},{16,48},{24,120},{32,64},{40,8},{48,80},{56,24},{64... | collective-permute-start | bytes 1572872 | tf_op jit(solution)/shard_map/ppermute | solution.py:48
  85.9 16.0 %collective-permute-start.26 = (bf16[1024,256]{1,0:T(8,128)(2,1)S(1)}, bf16[1024,256]{1,0:T(8,128)(2,1)S(1)}, u32[]{:S(2)}, u32[]{:S(2)}) collective-permute-start(bf16[1024,256]{1,0:T(8,128)(2,1)S(1)} %collective-permute-done.16.refs_2_), channel_id=1, source_target_pairs={{0,32},{8,104},{16,48},{24,120},{32,64},{40,8},{48,80},{56,24},{64... | collective-permute-start | bytes 1572872 | tf_op jit(solution)/shard_map/ppermute | solution.py:48
  87.1 14.8 %collective-permute-start.28 = (bf16[1024,256]{1,0:T(8,128)(2,1)S(1)}, bf16[1024,256]{1,0:T(8,128)(2,1)S(1)}, u32[]{:S(2)}, u32[]{:S(2)}) collective-permute-start(bf16[1024,256]{1,0:T(8,128)(2,1)S(1)} %collective-permute-done.21.refs_4_), channel_id=1, source_target_pairs={{0,16},{8,24},{16,0},{24,8},{32,48},{40,56},{48,32},{56,40},{64,80... | collective-permute-start | bytes 1572872 | tf_op jit(solution)/shard_map/ppermute | solution.py:48
  96.3 11.2 %collective-permute-start.23 = (bf16[1024,256]{1,0:T(8,128)(2,1)S(1)}, bf16[1024,256]{1,0:T(8,128)(2,1)S(1)}, u32[]{:S(2)}, u32[]{:S(2)}) collective-permute-start(bf16[1024,256]{1,0:T(8,128)(2,1)S(1)} %collective-permute-done.18.refs_0_), channel_id=1, source_target_pairs={{0,32},{8,104},{16,48},{24,120},{32,64},{40,8},{48,80},{56,24},{64... | collective-permute-start | bytes 1572872 | tf_op jit(solution)/shard_map/ppermute | solution.py:48
  96.3 11.2 %collective-permute-start.25 = (bf16[1024,256]{1,0:T(8,128)(2,1)S(1)}, bf16[1024,256]{1,0:T(8,128)(2,1)S(1)}, u32[]{:S(2)}, u32[]{:S(2)}) collective-permute-start(bf16[1024,256]{1,0:T(8,128)(2,1)S(1)} %collective-permute-done.18.refs_0_), channel_id=1, source_target_pairs={{0,8},{8,0},{16,24},{24,16},{32,40},{40,32},{48,56},{56,48},{64,72... | collective-permute-start | bytes 1572872 | tf_op jit(solution)/shard_map/ppermute | solution.py:48
  101.9 5.6 %collective-permute-start.27 = (bf16[1024,256]{1,0:T(8,128)(2,1)S(1)}, bf16[1024,256]{1,0:T(8,128)(2,1)S(1)}, u32[]{:S(2)}, u32[]{:S(2)}) collective-permute-start(bf16[1024,256]{1,0:T(8,128)(2,1)S(1)} %collective-permute-done.26.refs_2_), channel_id=1, source_target_pairs={{0,8},{8,0},{16,24},{24,16},{32,40},{40,32},{48,56},{56,48},{64,72... | collective-permute-start | bytes 1572872 | tf_op jit(solution)/shard_map/ppermute | solution.py:48
  101.9 5.6 %collective-permute-start.29 = (bf16[1024,256]{1,0:T(8,128)(2,1)S(1)}, bf16[1024,256]{1,0:T(8,128)(2,1)S(1)}, u32[]{:S(2)}, u32[]{:S(2)}) collective-permute-start(bf16[1024,256]{1,0:T(8,128)(2,1)S(1)} %collective-permute-done.28.refs_4_), channel_id=1, source_target_pairs={{0,8},{8,0},{16,24},{24,16},{32,40},{40,32},{48,56},{56,48},{64,72... | collective-permute-start | bytes 1572872 | tf_op jit(solution)/shard_map/ppermute | solution.py:48
  111.4 27.3 %collective-permute-start.30 = (bf16[256,1536]{1,0:T(8,128)(2,1)S(1)}, bf16[256,1536]{1,0:T(8,128)(2,1)S(1)}, u32[]{:S(2)}, u32[]{:S(2)}) collective-permute-start(bf16[256,1536]{1,0:T(8,128)(2,1)S(1)} %get-tuple-element.51), channel_id=1, source_target_pairs={{0,4},{1,5},{2,6},{3,7},{4,0},{5,1},{6,2},{7,3},{8,12},{9,13},{10,... | collective-permute-start | bytes 2359304 | tf_op jit(solution)/shard_map/ppermute | solution.py:48
  118.4 12.6 %collective-permute-start.31 = (bf16[128,1536]{1,0:T(8,128)(2,1)S(1)}, bf16[128,1536]{1,0:T(8,128)(2,1)S(1)}, u32[]{:S(2)}, u32[]{:S(2)}) collective-permute-start(bf16[128,1536]{1,0:T(8,128)(2,1)S(1)} %get-tuple-element.54), channel_id=1, source_target_pairs={{0,1},{1,2},{2,3},{3,0},{4,5},{5,6},{6,7},{7,4},{8,9},{9,10},{10,1... | collective-permute-start | bytes 1179656 | tf_op jit(solution)/shard_map/ppermute | solution.py:48
  120.0 18.7 %collective-permute-start.32 = (bf16[128,1536]{1,0:T(8,128)(2,1)S(1)}, bf16[128,1536]{1,0:T(8,128)(2,1)S(1)}, u32[]{:S(2)}, u32[]{:S(2)}) collective-permute-start(bf16[128,1536]{1,0:T(8,128)(2,1)S(1)} %get-tuple-element.55), channel_id=1, source_target_pairs={{0,3},{1,0},{2,1},{3,2},{4,7},{5,4},{6,5},{7,6},{8,11},{9,8},{10,9... | collective-permute-start | bytes 1179656 | tf_op jit(solution)/shard_map/ppermute | solution.py:48
  121.7 21.4 %collective-permute-start.37 = (bf16[64,1536]{1,0:T(8,128)(2,1)S(1)}, bf16[64,1536]{1,0:T(8,128)(2,1)S(1)}, u32[]{:S(2)}, u32[]{:S(2)}) collective-permute-start(bf16[64,1536]{1,0:T(8,128)(2,1)S(1)} %get-tuple-element.61), channel_id=1, source_target_pairs={{0,2},{1,3},{2,0},{3,1},{4,6},{5,7},{6,4},{7,5},{8,10},{9,11},{10,... | collective-permute-start | bytes 589832 | tf_op jit(solution)/shard_map/ppermute | solution.py:48
  123.7 20.8 %collective-permute-start.38 = (bf16[64,1536]{1,0:T(8,128)(2,1)S(1)}, bf16[64,1536]{1,0:T(8,128)(2,1)S(1)}, u32[]{:S(2)}, u32[]{:S(2)}) collective-permute-start(bf16[64,1536]{1,0:T(8,128)(2,1)S(1)} %get-tuple-element.62), channel_id=1, source_target_pairs={{0,6},{1,7},{2,4},{3,5},{4,2},{5,3},{6,0},{7,1},{8,14},{9,15},{10,... | collective-permute-start | bytes 589832 | tf_op jit(solution)/shard_map/ppermute | solution.py:48
  138.9 7.3 %collective-permute-start.36 = (bf16[64,1536]{1,0:T(8,128)(2,1)S(1)}, bf16[64,1536]{1,0:T(8,128)(2,1)S(1)}, u32[]{:S(2)}, u32[]{:S(2)}) collective-permute-start(bf16[64,1536]{1,0:T(8,128)(2,1)S(1)} %slice.53), channel_id=1, source_target_pairs={{0,4},{1,5},{2,6},{3,7},{4,0},{5,1},{6,2},{7,3},{8,12},{9,13},{10,... | collective-permute-start | bytes 589832 | tf_op jit(solution)/shard_map/ppermute | solution.py:48
  139.3 8.1 %collective-permute-start.33 = (bf16[64,1536]{1,0:T(8,128)(2,1)S(1)}, bf16[64,1536]{1,0:T(8,128)(2,1)S(1)}, u32[]{:S(2)}, u32[]{:S(2)}) collective-permute-start(bf16[64,1536]{1,0:T(8,128)(2,1)S(1)} %get-tuple-element.68), channel_id=1, source_target_pairs={{0,1},{1,2},{2,3},{3,0},{4,5},{5,6},{6,7},{7,4},{8,9},{9,10},{10,1... | collective-permute-start | bytes 589832 | tf_op jit(solution)/shard_map/ppermute | solution.py:48
  139.4 8.0 %collective-permute-start.34 = (bf16[64,1536]{1,0:T(8,128)(2,1)S(1)}, bf16[64,1536]{1,0:T(8,128)(2,1)S(1)}, u32[]{:S(2)}, u32[]{:S(2)}) collective-permute-start(bf16[64,1536]{1,0:T(8,128)(2,1)S(1)} %get-tuple-element.70), channel_id=1, source_target_pairs={{0,3},{1,0},{2,1},{3,2},{4,7},{5,4},{6,5},{7,6},{8,11},{9,8},{10,9... | collective-permute-start | bytes 589832 | tf_op jit(solution)/shard_map/ppermute | solution.py:48
  143.1 7.2 %collective-permute-start.35 = (bf16[64,1536]{1,0:T(8,128)(2,1)S(1)}, bf16[64,1536]{1,0:T(8,128)(2,1)S(1)}, u32[]{:S(2)}, u32[]{:S(2)}) collective-permute-start(bf16[64,1536]{1,0:T(8,128)(2,1)S(1)} %get-tuple-element.69), channel_id=1, source_target_pairs={{0,2},{1,3},{2,0},{3,1},{4,6},{5,7},{6,4},{7,5},{8,10},{9,11},{10,... | collective-permute-start | bytes 589832 | tf_op jit(solution)/shard_map/ppermute | solution.py:48
  (15 other events, 185.2 us)
